TPU v7x, 32 devices: a whole 2x2x4 slice. The times are simulated.
32 devices in a mesh: groups: 2 (over y), rows: 4 (over z), feat: 2 (over x), sub: 2 (over core).
Axes of the slice: x: 2, y: 2, z: 4, core: 2. Of those that a mesh axis runs over, the one named last changes fastest.
Arguments:
- embeddings: float32 [8192, 768], P(('groups', 'rows', 'feat', 'sub')), parts along dimension 0, may hold values from -64 to 64
- assign: int32 [8192], P(('groups', 'rows', 'feat', 'sub')), parts along dimension 0, may hold values from 0 to 1023, as said below
- order: int32 [8192], P(('groups', 'rows', 'feat', 'sub')), parts along dimension 0, may hold values from 0 to 4095, each once
Outputs:
- dup_score: float32 [8192], P(('groups', 'rows', 'feat', 'sub')), parts along dimension 0
- cent_score: float32 [8192], P(('groups', 'rows', 'feat', 'sub')), parts along dimension 0
- centroids: float32 [2048, 768], P(('groups', 'rows', 'feat')), parts along dimension 0
There are 2 independent parts, one for each index of `groups`. A program takes and returns all parts, laid end to end along the dimension named above; each array names one. Nothing has to cross between parts.
Inputs may be any that keep to these rules, and one draw needn't show every extreme that they name: `assign`: cluster k belongs to owner k // 128. Among the 256 rows of one device (aligned blocks), at most 64 rows belong to one owner's clusters; in every block some owner has exactly 64, and one owner has exactly 64 in every block.
All inputs are finite; a program needn't handle non-finite values.
Results may differ from a plain program's by a relative error of at most 0.00061.
Values may be sent and summed in bfloat16 or wider, within the bound.
No kernel may reach another device: no remote copies, remote signals or barrier semaphores. Data moves between devices by JAX's collectives and lax.ppermute only.
A program may use at most 64 MiB of HBM per device.

v0:
```python
import jax
import jax.numpy as jnp
from jax import lax
from jax.sharding import PartitionSpec as P

K = 1024


EPSILON = 1e-06


def swapped(shard, axis, distance):
    return lax.ppermute(shard, axis, [(i, i ^ 1 << distance) for i in range(lax.axis_size(axis))])


def unit_rows(values):
    return values * lax.rsqrt(jnp.sum(values * values, axis=1, keepdims=True) + EPSILON)


def best_against(q_vec, q_clu, q_ord, k_vec, k_clu, k_ord):
    scores = lax.dot_general(
        q_vec, k_vec, (((1,), (1,)), ((), ())), preferred_element_type=jnp.float32
    )
    allowed = (q_clu[:, None] == k_clu[None, :]) & (k_ord[None, :] < q_ord[:, None])
    return jnp.max(jnp.where(allowed, scores, -1.0), axis=1)


def cluster_sums(vectors, clusters, first_cluster, per_owner):
    local = clusters - first_cluster
    member = (jnp.arange(per_owner, dtype=jnp.int32)[:, None] == local[None, :]).astype(jnp.float32)
    return jnp.dot(
        member, vectors, precision=lax.Precision.HIGHEST, preferred_element_type=jnp.float32
    )


def body(embeddings, assign, order):
    owners = lax.axis_size("rows") * lax.axis_size("feat")
    rows_dev = embeddings.shape[0]
    width = embeddings.shape[1]
    capacity = 2 * rows_dev // owners
    per_owner = K // owners
    slots = owners * capacity
    here = lax.axis_index(("rows", "feat"))
    unit = unit_rows(embeddings)
    target = assign // per_owner
    hits = (target[:, None] == jnp.arange(owners, dtype=jnp.int32)[None, :]).astype(jnp.int32)
    before = jnp.cumsum(hits, axis=0) - hits
    slot = target * capacity + jnp.sum(before * hits, axis=1)
    send_clu = jnp.full((slots,), -1, jnp.int32).at[slot].set(assign)
    send_ord = jnp.zeros((slots,), jnp.int32).at[slot].set(order)
    send_wide = jnp.zeros((slots, width), jnp.float32).at[slot].set(unit)
    wide_vec, got_clu, got_ord = (
        lax.all_to_all(
            send_wide.reshape(owners, capacity, width),
            ("rows", "feat"),
            split_axis=0,
            concat_axis=0,
            tiled=True,
        ),
        lax.all_to_all(
            send_clu.reshape(owners, capacity),
            ("rows", "feat"),
            split_axis=0,
            concat_axis=0,
            tiled=True,
        ),
        lax.all_to_all(
            send_ord.reshape(owners, capacity),
            ("rows", "feat"),
            split_axis=0,
            concat_axis=0,
            tiled=True,
        ),
    )
    wide_vec = wide_vec.reshape(slots, width)
    got_clu = got_clu.reshape(slots)
    got_ord = got_ord.reshape(slots)
    other_wide, other_clu, other_ord = swapped((wide_vec, got_clu, got_ord), "sub", 0)
    first_cluster = here * per_owner
    own_sums = cluster_sums(wide_vec, got_clu, first_cluster, per_owner)
    pair_sums = cluster_sums(other_wide, other_clu, first_cluster, per_owner)
    own_cent = unit_rows(own_sums + pair_sums)
    got_vec = wide_vec.astype(jnp.bfloat16)
    other_vec = other_wide.astype(jnp.bfloat16)
    block = min(512, slots)
    nblock = slots // block

    def per_block(pieces):
        q_vec, q_clu, q_ord = pieces
        first = best_against(q_vec, q_clu, q_ord, got_vec, got_clu, got_ord)
        second = best_against(q_vec, q_clu, q_ord, other_vec, other_clu, other_ord)
        return jnp.maximum(first, second)

    best = lax.map(
        per_block,
        (
            got_vec.reshape(nblock, block, width),
            got_clu.reshape(nblock, block),
            got_ord.reshape(nblock, block),
        ),
    ).reshape(slots)
    local = jnp.clip(got_clu - here * per_owner, 0, per_owner - 1)
    fits = jnp.dot(
        got_vec.astype(jnp.float32),
        own_cent.T,
        precision=lax.Precision.HIGHEST,
        preferred_element_type=jnp.float32,
    )
    pick = local[:, None] == jnp.arange(per_owner, dtype=jnp.int32)[None, :]
    near = jnp.sum(jnp.where(pick, fits, 0.0), axis=1)
    back_best, back_near = (
        lax.all_to_all(
            best.reshape(owners, capacity),
            ("rows", "feat"),
            split_axis=0,
            concat_axis=0,
            tiled=True,
        ),
        lax.all_to_all(
            near.reshape(owners, capacity),
            ("rows", "feat"),
            split_axis=0,
            concat_axis=0,
            tiled=True,
        ),
    )
    return (back_best.reshape(slots)[slot], back_near.reshape(slots)[slot], own_cent)


def solution(mesh):
    return jax.shard_map(
        body,
        mesh=mesh,
        in_specs=(
            P(("groups", "rows", "feat", "sub"), None),
            P(("groups", "rows", "feat", "sub")),
            P(("groups", "rows", "feat", "sub")),
        ),
        out_specs=(
            P(("groups", "rows", "feat", "sub")),
            P(("groups", "rows", "feat", "sub")),
            P(("groups", "rows", "feat"), None),
        ),
        check_vma=False,
    )
```

profile of v0, /device:TPU:0, one launch (start us, length us, event | category | flops | bytes accessed | tf_op | source)
XLA Modules:
  0.0 103.5 jit_solution(11496720424707080008)
XLA Ops:
  0.6 0.7 fusion.27
  1.3 0.7 and_select_fusion
  2.0 0.6 reduce-window.6
  2.6 0.2 slice_reduce_fusion
  2.9 0.1 fusion.16
  2.9 0.7 compare_select_fusion
  3.6 0.0 copy-start.1
  3.6 1.3 %multiply_reduce_fusion = f32[256]{0:T(256)S(1)} fusion(f32[256,768]{1,0:T(8,128)} %param.3), kind=kLoop, calls=%fused_computation.15 | loop fusion | flops 392960 | bytes 787456 | tf_op jit(solution)/shard_map/reduce_sum | solution.py:17
  4.9 2.5 %scatter_custom_fusion.2 = f32[512,768]{1,0:T(8,128)S(1)} fusion(s32[256]{0:T(256)S(1)} %compare_select_fusion, f32[256,768]{1,0:T(8,128)} %param.3, f32[]{:T(128)} %constant.56.clone.1, f32[256]{0:T(256)S(1)} %add_rsqrt_fusion), kind=kCustom, calls=%fused_computation.13 | custom fusion | flops 196608 | bytes 2360324 | tf_op jit(solution)/shard_map/scatter | solution.py:51
  7.4 44.1 %all_to_all.38 = f32[8,64,768]{2,1,0:T(8,128)S(1)} all-to-all(f32[8,64,768]{2,1,0:T(8,128)S(1)} %bitcast.22), channel_id=1, replica_groups=mesh['groups'=2,'rows'=4,'feat'=2,'sub'=2] {'rows','feat'}, dimensions={0} | all-to-all | bytes 3145728 | tf_op jit(solution)/shard_map/all_to_all | solution.py:53
  51.5 0.0 collective-permute-start.2
  51.5 1.6 %scatter_custom_fusion.1 = s32[512]{0:T(512)S(1)} fusion(s32[256]{0:T(256)S(1)} %compare_select_fusion, s32[256]{0:T(256)} %param.5, s32[]{:T(128)} %constant.34.clone.1), kind=kCustom, calls=%fused_computation.45 | custom fusion | bytes 2560 | tf_op jit(solution)/shard_map/scatter | solution.py:50
  53.1 0.7 all_to_all.27
  53.7 3.6 %all-to-all-start.1 = ((s32[8,1,64]{2,1,0:T(1,128)}), s32[8,1,64]{2,1,0:T(1,128)S(1)}, u32[]{:S(2)}, u32[]{:S(2)}) async-start(s32[8,1,64]{2,1,0:T(1,128)} %all_to_all.27), calls=%async_computation.1 | async-start | bytes 8192 | tf_op jit(solution)/shard_map/all_to_all | solution.py:67
  57.3 0.0 copy-done.1
  57.3 1.6 %scatter_custom_fusion = s32[512]{0:T(512)S(1)} fusion(s32[256]{0:T(256)S(1)} %compare_select_fusion, s32[256]{0:T(256)} %param.4, s32[]{:T(128)} %constant.27.clone.1), kind=kCustom, calls=%fused_computation.47 | custom fusion | bytes 2560 | tf_op jit(solution)/shard_map/scatter | solution.py:49
  58.9 0.7 all_to_all.25
  59.6 4.1 %all-to-all-done.1 = s32[8,1,64]{2,1,0:T(1,128)S(1)} async-done(((s32[8,1,64]{2,1,0:T(1,128)}), s32[8,1,64]{2,1,0:T(1,128)S(1)}, u32[]{:S(2)}, u32[]{:S(2)}) %all-to-all-start.1) | async-done | bytes 2080 | tf_op jit(solution)/shard_map/all_to_all | solution.py:67
  63.7 3.3 %all-to-all-start = ((s32[8,1,64]{2,1,0:T(1,128)}), s32[8,1,64]{2,1,0:T(1,128)S(1)}, u32[]{:S(2)}, u32[]{:S(2)}) async-start(s32[8,1,64]{2,1,0:T(1,128)} %all_to_all.25), calls=%async_computation | async-start | bytes 8192 | tf_op jit(solution)/shard_map/all_to_all | solution.py:60
  67.1 0.5 broadcast.83
  67.6 0.7 reduce.14
  68.2 0.1 lt.46
  68.3 5.1 %all-to-all-done = s32[8,1,64]{2,1,0:T(1,128)S(1)} async-done(((s32[8,1,64]{2,1,0:T(1,128)}), s32[8,1,64]{2,1,0:T(1,128)S(1)}, u32[]{:S(2)}, u32[]{:S(2)}) %all-to-all-start) | async-done | bytes 2080 | tf_op jit(solution)/shard_map/all_to_all | solution.py:60
  73.5 0.7 reduce.15
  74.1 0.1 eq.106
  74.2 0.0 collective-permute-start.1
  74.2 0.5 collective-permute-start
  74.7 0.8 collective-permute-done
  75.5 0.1 convert_element_type.24
  75.6 0.7 fusion.12
  76.4 0.6 fusion
  77.0 0.0 collective-permute-done.1
  77.0 0.0 collective-permute-done.2
  77.0 0.7 select_reduce_fusion
  77.7 0.7 max.20
  78.4 3.3 %all-to-all-start.3 = ((f32[8,1,64]{2,1,0:T(1,128)}), f32[8,1,64]{2,1,0:T(1,128)S(1)}, u32[]{:S(2)}, u32[]{:S(2)}) async-start(f32[8,1,64]{2,1,0:T(1,128)} %max.20), calls=%async_computation.3 | async-start | bytes 8192 | tf_op jit(solution)/shard_map/all_to_all | solution.py:112
  81.7 0.8 multiply_reduce_fusion.1
  82.5 0.0 copy-start.2
  82.6 0.1 broadcast_multiply_fusion
  82.7 0.0 copy-start
  82.7 0.9 fusion.1
  83.6 0.7 all_to_all.31
  84.3 3.9 %all-to-all-done.3 = f32[8,1,64]{2,1,0:T(1,128)S(1)} async-done(((f32[8,1,64]{2,1,0:T(1,128)}), f32[8,1,64]{2,1,0:T(1,128)S(1)}, u32[]{:S(2)}, u32[]{:S(2)}) %all-to-all-start.3) | async-done | bytes 2080 | tf_op jit(solution)/shard_map/all_to_all | solution.py:112
  88.1 3.2 %all-to-all-start.4 = ((f32[8,1,64]{2,1,0:T(1,128)}), f32[8,1,64]{2,1,0:T(1,128)S(1)}, u32[]{:S(2)}, u32[]{:S(2)}) async-start(f32[8,1,64]{2,1,0:T(1,128)} %all_to_all.31), calls=%async_computation.4 | async-start | bytes 8192 | tf_op jit(solution)/shard_map/all_to_all | solution.py:119
  91.4 0.0 copy-done.2
  91.4 0.5 broadcast.85
  91.9 0.7 reduce.16
  92.6 0.1 reshape.123
  92.7 5.1 %all-to-all-done.4 = f32[8,1,64]{2,1,0:T(1,128)S(1)} async-done(((f32[8,1,64]{2,1,0:T(1,128)}), f32[8,1,64]{2,1,0:T(1,128)S(1)}, u32[]{:S(2)}, u32[]{:S(2)}) %all-to-all-start.4) | async-done | bytes 2080 | tf_op jit(solution)/shard_map/all_to_all | solution.py:119
  97.8 0.7 reduce.17
  98.4 0.1 reshape.124
  98.5 2.5 %gather_fusion = f32[256]{0:T(256)} fusion(f32[512]{0:T(512)S(1)} %reshape.123, s32[1024]{0:T(1024)S(1)} %pad_clamp_fusion), kind=kCustom, calls=%fused_computation | custom fusion | bytes 3072 | tf_op jit(solution)/shard_map/gather | solution.py:127
  101.0 2.5 %gather_fusion.1 = f32[256]{0:T(256)} fusion(f32[512]{0:T(512)S(1)} %reshape.124, s32[1024]{0:T(1024)S(1)} %pad_clamp_fusion), kind=kCustom, calls=%fused_computation.1 | custom fusion | bytes 3072 | tf_op jit(solution)/shard_map/gather | solution.py:127
  103.5 0.0 copy-done
  (9 shorter events, 0.1 us)
Async XLA Ops:
  3.6 53.7 %copy-start.1 = (s32[256]{0:T(256)}, s32[256]{0:T(256)S(1)}, u32[]{:S(2)}) copy-start(s32[256]{0:T(256)S(1)} %compare_select_fusion) | copy-start | bytes 3076
  51.5 25.5 %collective-permute-start.2 = (f32[512,768]{1,0:T(8,128)S(1)}, f32[512,768]{1,0:T(8,128)S(1)}, u32[]{:S(2)}, u32[]{:S(2)}) collective-permute-start(f32[512,768]{1,0:T(8,128)S(1)} %bitcast.18), channel_id=1, source_target_pairs={{0,1},{1,0},{2,3},{3,2},{4,5},{5,4},{6,7},{7,6},{8,9},{9,8},{10,11... | collective-permute-start | bytes 4718600 | tf_op jit(solution)/shard_map/ppermute | solution.py:13
  53.7 10.0 %all-to-all-start.1 = ((s32[8,1,64]{2,1,0:T(1,128)}), s32[8,1,64]{2,1,0:T(1,128)S(1)}, u32[]{:S(2)}, u32[]{:S(2)}) async-start(s32[8,1,64]{2,1,0:T(1,128)} %all_to_all.27), calls=%async_computation.1 | async-start | bytes 8192 | tf_op jit(solution)/shard_map/all_to_all | solution.py:67
  63.7 9.7 %all-to-all-start = ((s32[8,1,64]{2,1,0:T(1,128)}), s32[8,1,64]{2,1,0:T(1,128)S(1)}, u32[]{:S(2)}, u32[]{:S(2)}) async-start(s32[8,1,64]{2,1,0:T(1,128)} %all_to_all.25), calls=%async_computation | async-start | bytes 8192 | tf_op jit(solution)/shard_map/all_to_all | solution.py:60
  74.2 2.8 %collective-permute-start.1 = (s32[512]{0:T(512)S(1)}, s32[512]{0:T(512)S(1)}, u32[]{:S(2)}, u32[]{:S(2)}) collective-permute-start(s32[512]{0:T(512)S(1)} %lt.46), channel_id=1, source_target_pairs={{0,1},{1,0},{2,3},{3,2},{4,5},{5,4},{6,7},{7,6},{8,9},{9,8},{10,11... | collective-permute-start | bytes 6152 | tf_op jit(solution)/shard_map/ppermute | solution.py:13
  74.2 1.3 %collective-permute-start = (s32[512]{0:T(512)S(1)}, s32[512]{0:T(512)S(1)}, u32[]{:S(2)}, u32[]{:S(2)}) collective-permute-start(s32[512]{0:T(512)S(1)} %eq.106), channel_id=1, source_target_pairs={{0,1},{1,0},{2,3},{3,2},{4,5},{5,4},{6,7},{7,6},{8,9},{9,8},{10,11... | collective-permute-start | bytes 6152 | tf_op jit(solution)/shard_map/ppermute | solution.py:13
  78.4 9.7 %all-to-all-start.3 = ((f32[8,1,64]{2,1,0:T(1,128)}), f32[8,1,64]{2,1,0:T(1,128)S(1)}, u32[]{:S(2)}, u32[]{:S(2)}) async-start(f32[8,1,64]{2,1,0:T(1,128)} %max.20), calls=%async_computation.3 | async-start | bytes 8192 | tf_op jit(solution)/shard_map/all_to_all | solution.py:112
  82.5 8.8 %copy-start.2 = (s32[256]{0:T(256)S(1)}, s32[256]{0:T(256)}, u32[]{:S(2)}) copy-start(s32[256]{0:T(256)} %copy-done.1) | copy-start | bytes 3076
  82.7 20.9 %copy-start = (f32[128,768]{1,0:T(8,128)}, f32[128,768]{1,0:T(8,128)S(1)}, u32[]{:S(2)}) copy-start(f32[128,768]{1,0:T(8,128)S(1)} %broadcast_multiply_fusion) | copy-start | bytes 1179652
  88.1 9.7 %all-to-all-start.4 = ((f32[8,1,64]{2,1,0:T(1,128)}), f32[8,1,64]{2,1,0:T(1,128)S(1)}, u32[]{:S(2)}, u32[]{:S(2)}) async-start(f32[8,1,64]{2,1,0:T(1,128)} %all_to_all.31), calls=%async_computation.4 | async-start | bytes 8192 | tf_op jit(solution)/shard_map/all_to_all | solution.py:119
where the time goes:
time: 104 us
  blocking collectives  44.1 us (42%)
  waiting for transfers between devices  19.1 us (18%)
  starting transfers between devices  14 us (13%)
  local copies, waits for them, and re-layouts  12.4 us (12%)
  other arithmetic  9.41 us (9%)
  matrix products  3.76 us (4%)
    all_to_all x1, blocking collectives, body(): lax.all_to_all(send_wide.reshape(owners, capacity, width), ('rows', 'feat...  44.1 us
    all_to_all x1, waiting for transfers between devices, body(): lax.all_to_all(send_clu.reshape(owners, capacity), ('rows', 'feat'), spli...  5.14 us
    all_to_all x1, waiting for transfers between devices, body(): lax.all_to_all(near.reshape(owners, capacity), ('rows', 'feat'), split_ax...  5.12 us
    all_to_all x1, waiting for transfers between devices, body(): lax.all_to_all(send_ord.reshape(owners, capacity), ('rows', 'feat'), spli...  4.15 us
    all_to_all x1, waiting for transfers between devices, body(): lax.all_to_all(best.reshape(owners, capacity), ('rows', 'feat'), split_ax...  3.87 us
    all_to_all x1, starting transfers between devices, body(): lax.all_to_all(send_ord.reshape(owners, capacity), ('rows', 'feat'), spli...  3.59 us
    all_to_all x1, starting transfers between devices, body(): lax.all_to_all(send_clu.reshape(owners, capacity), ('rows', 'feat'), spli...  3.33 us
    all_to_all x1, starting transfers between devices, body(): lax.all_to_all(best.reshape(owners, capacity), ('rows', 'feat'), split_ax...  3.33 us
  transfers between devices with their start and end apart: 7, of which 5 were waited for; matrix products, arithmetic and copies ran while one was open for 9% of the time, Pallas kernels for 0%

commit v1 on v0

--- a/solution.py
+++ b/solution.py
@@ -1,12 +1,20 @@
+import functools
+
 import jax
 import jax.numpy as jnp
 from jax import lax
+from jax.experimental import pallas as pl
+from jax.experimental.pallas import tpu as pltpu
 from jax.sharding import PartitionSpec as P
 
 K = 1024
 
 
 EPSILON = 1e-06
+LANES = 128
+META = 16
+FULL = 32768.0
+STEPS = (32, 16, 8, 4, 2, 1)
 
 
 def swapped(shard, axis, distance):
@@ -33,7 +41,7 @@
     )
 
 
-def body(embeddings, assign, order):
+def exchange_all(embeddings, assign, order):
     owners = lax.axis_size("rows") * lax.axis_size("feat")
     rows_dev = embeddings.shape[0]
     width = embeddings.shape[1]
@@ -49,32 +57,12 @@
     send_clu = jnp.full((slots,), -1, jnp.int32).at[slot].set(assign)
     send_ord = jnp.zeros((slots,), jnp.int32).at[slot].set(order)
     send_wide = jnp.zeros((slots, width), jnp.float32).at[slot].set(unit)
-    wide_vec, got_clu, got_ord = (
-        lax.all_to_all(
-            send_wide.reshape(owners, capacity, width),
-            ("rows", "feat"),
-            split_axis=0,
-            concat_axis=0,
-            tiled=True,
-        ),
-        lax.all_to_all(
-            send_clu.reshape(owners, capacity),
-            ("rows", "feat"),
-            split_axis=0,
-            concat_axis=0,
-            tiled=True,
-        ),
-        lax.all_to_all(
-            send_ord.reshape(owners, capacity),
-            ("rows", "feat"),
-            split_axis=0,
-            concat_axis=0,
-            tiled=True,
-        ),
-    )
-    wide_vec = wide_vec.reshape(slots, width)
-    got_clu = got_clu.reshape(slots)
-    got_ord = got_ord.reshape(slots)
+    spread = functools.partial(
+        lax.all_to_all, axis_name=("rows", "feat"), split_axis=0, concat_axis=0, tiled=True
+    )
+    wide_vec = spread(send_wide.reshape(owners, capacity, width)).reshape(slots, width)
+    got_clu = spread(send_clu.reshape(owners, capacity)).reshape(slots)
+    got_ord = spread(send_ord.reshape(owners, capacity)).reshape(slots)
     other_wide, other_clu, other_ord = swapped((wide_vec, got_clu, got_ord), "sub", 0)
     first_cluster = here * per_owner
     own_sums = cluster_sums(wide_vec, got_clu, first_cluster, per_owner)
@@ -108,23 +96,216 @@
     )
     pick = local[:, None] == jnp.arange(per_owner, dtype=jnp.int32)[None, :]
     near = jnp.sum(jnp.where(pick, fits, 0.0), axis=1)
-    back_best, back_near = (
-        lax.all_to_all(
-            best.reshape(owners, capacity),
-            ("rows", "feat"),
-            split_axis=0,
-            concat_axis=0,
-            tiled=True,
-        ),
-        lax.all_to_all(
-            near.reshape(owners, capacity),
-            ("rows", "feat"),
-            split_axis=0,
-            concat_axis=0,
-            tiled=True,
-        ),
-    )
+    back_best = spread(best.reshape(owners, capacity))
+    back_near = spread(near.reshape(owners, capacity))
     return (back_best.reshape(slots)[slot], back_near.reshape(slots)[slot], own_cent)
+
+
+def iota(shape, dim):
+    return lax.broadcasted_iota(jnp.int32, shape, dim)
+
+
+def dot_t(a, b):
+    return lax.dot_general(a, b, (((1,), (1,)), ((), ())), preferred_element_type=jnp.float32)
+
+
+def halves(x):
+    high = x.astype(jnp.bfloat16)
+    return high, (x - high.astype(jnp.float32)).astype(jnp.bfloat16)
+
+
+def pack_kernel(owners, capacity, per_owner, emb_ref, asg_ref, ord_ref, *outs):
+    packs, pos_ref = outs[:owners], outs[owners]
+    rows, width = emb_ref.shape
+    slots = owners * capacity
+    me = lax.axis_index(("rows", "feat"))
+    x = emb_ref[...]
+    unit = x * lax.rsqrt(jnp.sum(x * x, axis=1, keepdims=True) + EPSILON)
+    top = jnp.max(jnp.abs(unit), axis=1, keepdims=True)
+    scale = jnp.ones_like(top)
+    power = jnp.zeros_like(top)
+    for step in STEPS:
+        small = top * (scale * 2.0**step) < 1.0
+        scale = jnp.where(small, scale * 2.0**step, scale)
+        power = jnp.where(small, power + step, power)
+    coded = jnp.clip(jnp.round(unit * (scale * FULL)), -FULL, FULL - 1.0)
+    high, low = halves(coded)
+
+    asg = asg_ref[...]
+    rank = ord_ref[...]
+    target = lax.div(asg, jnp.int32(per_owner))
+    seat = target ^ me
+    hits = iota((owners, rows), 0) == target
+    earlier = (iota((rows, rows), 0) < iota((rows, rows), 1)).astype(jnp.bfloat16)
+    before = jnp.dot(
+        hits.astype(jnp.bfloat16), earlier, preferred_element_type=jnp.float32
+    )
+    pos = jnp.sum(jnp.where(hits, before, 0.0), axis=0, keepdims=True).astype(jnp.int32)
+    pos_ref[...] = pos
+    place = (iota((slots, rows), 0) == seat * capacity + pos).astype(jnp.bfloat16)
+
+    power_row = jnp.transpose(jnp.broadcast_to(power, (rows, LANES)))[:1, :]
+    facts = jnp.concatenate(
+        [
+            (asg - target * per_owner + 1).astype(jnp.float32),
+            (rank & 255).astype(jnp.float32),
+            (rank >> 8).astype(jnp.float32),
+            power_row,
+            jnp.zeros((4, rows), jnp.float32),
+        ],
+        axis=0,
+    ).astype(jnp.bfloat16)
+    facts = dot_t(facts, place)
+    for v in range(owners):
+        mine = place[v * capacity : (v + 1) * capacity, :]
+        block = jnp.dot(mine, high, preferred_element_type=jnp.float32) + jnp.dot(
+            mine, low, preferred_element_type=jnp.float32
+        )
+        block = block.astype(jnp.int32).astype(jnp.int16)
+        for c in range(width // LANES):
+            packs[v][c * capacity : (c + 1) * capacity, :] = block[:, c * LANES : (c + 1) * LANES]
+        notes = facts[:, v * capacity : (v + 1) * capacity]
+        notes = jnp.concatenate([notes, jnp.zeros((8, LANES - capacity), jnp.float32)], axis=1)
+        notes = jnp.concatenate([notes, jnp.zeros((META - 8, LANES), jnp.float32)], axis=0)
+        packs[v][width // LANES * capacity :, :] = notes.astype(jnp.int32).astype(jnp.int16)
+
+
+def score_kernel(owners, capacity, per_owner, width, *refs):
+    count = 2 * owners
+    chunks = refs[:count]
+    cent_ref, back_ref, high_ref, low_ref = refs[count:]
+    tiles = width // LANES
+    slots = owners * capacity
+    me = lax.axis_index(("rows", "feat"))
+    eye = (iota((LANES, LANES), 0) == iota((LANES, LANES), 1)).astype(jnp.float32)
+    clu_rows, code_rows, code_cols = [], [], []
+    for pair in range(owners):
+        notes = [
+            ref[tiles * capacity :, :].astype(jnp.int32).astype(jnp.float32)[:8, :capacity]
+            for ref in chunks[2 * pair : 2 * pair + 2]
+        ]
+        notes = jnp.concatenate(notes, axis=1)
+        clu = notes[0:1, :] - 1.0
+        rank = notes[1:2, :] + 256.0 * notes[2:3, :]
+        power = notes[3:4, :]
+        scale = jnp.full_like(power, 1.0 / FULL)
+        for step in STEPS:
+            there = power >= step
+            scale = jnp.where(there, scale * 2.0**-step, scale)
+            power = jnp.where(there, power - step, power)
+        code = jnp.where(clu >= 0.0, clu * 65536.0 + rank, -1.0)
+        both = jnp.concatenate([code, scale, jnp.zeros((6, LANES), jnp.float32)], axis=0)
+        cols = lax.dot_general(
+            eye,
+            both,
+            (((1,), (1,)), ((), ())),
+            precision=lax.Precision.HIGHEST,
+            preferred_element_type=jnp.float32,
+        )
+        clu_rows.append(clu)
+        code_rows.append(code)
+        code_cols.append(cols[:, 0:1])
+        for half in range(2):
+            ref = chunks[2 * pair + half]
+            first = (2 * pair + half) * capacity
+            factor = cols[half * capacity : (half + 1) * capacity, 1:2]
+            for c in range(tiles):
+                part = ref[c * capacity : (c + 1) * capacity, :]
+                high, low = halves(part.astype(jnp.int32).astype(jnp.float32) * factor)
+                high_ref[first : first + capacity, c * LANES : (c + 1) * LANES] = high
+                low_ref[first : first + capacity, c * LANES : (c + 1) * LANES] = low
+    clu_all = jnp.concatenate(clu_rows, axis=1)
+    member = (iota((per_owner, 2 * slots), 0).astype(jnp.float32) == clu_all).astype(jnp.bfloat16)
+    sums = jnp.dot(member, high_ref[...], preferred_element_type=jnp.float32) + jnp.dot(
+        member, low_ref[...], preferred_element_type=jnp.float32
+    )
+    cent = sums * lax.rsqrt(jnp.sum(sums * sums, axis=1, keepdims=True) + EPSILON)
+    cent_ref[...] = cent
+    cent_high, cent_low = halves(cent)
+    asked = high_ref[:slots, :]
+    fits = dot_t(cent_high, asked) + dot_t(cent_low, asked)
+    near = jnp.sum(jnp.where(member[:, :slots] > 0, fits, 0.0), axis=0, keepdims=True)
+    own_code = jnp.concatenate(code_rows[: owners // 2], axis=1)
+    own_base = jnp.concatenate(clu_rows[: owners // 2], axis=1) * 65536.0
+    best = jnp.full((1, slots), -1.0, jnp.float32)
+    for pair in range(owners):
+        scores = dot_t(high_ref[pair * LANES : (pair + 1) * LANES, :], asked)
+        code = code_cols[pair]
+        allowed = (code >= own_base) & (code < own_code)
+        best = jnp.maximum(
+            best, jnp.max(jnp.where(allowed, scores, -1.0), axis=0, keepdims=True)
+        )
+    for v in range(owners):
+        part = slice(v * capacity, (v + 1) * capacity)
+        back_ref[pl.ds(me ^ v, 1), :] = jnp.concatenate([best[:, part], near[:, part]], axis=1)
+
+
+def pick_kernel(owners, capacity, per_owner, back_ref, asg_ref, pos_ref, best_ref, near_ref):
+    rows = asg_ref.shape[1]
+    target = lax.div(asg_ref[...], jnp.int32(per_owner))
+    pos = pos_ref[...]
+    hits = iota((owners, rows), 0) == target
+    back = back_ref[...]
+    for first, ref in ((0, best_ref), (capacity, near_ref)):
+        place = (iota((LANES, rows), 0) == pos + first).astype(jnp.float32)
+        found = jnp.dot(
+            back, place, precision=lax.Precision.HIGHEST, preferred_element_type=jnp.float32
+        )
+        ref[...] = jnp.sum(jnp.where(hits, found, 0.0), axis=0, keepdims=True)
+
+
+def exchange_pairs(embeddings, assign, order):
+    owners = lax.axis_size("rows") * lax.axis_size("feat")
+    rows, width = embeddings.shape
+    capacity = 2 * rows // owners
+    per_owner = K // owners
+    slots = owners * capacity
+    tall = width // LANES * capacity + META
+    assign = assign.reshape(1, rows)
+    order = order.reshape(1, rows)
+    vmem = pl.BlockSpec(memory_space=pltpu.VMEM)
+    *packs, pos = pl.pallas_call(
+        functools.partial(pack_kernel, owners, capacity, per_owner),
+        out_shape=[jax.ShapeDtypeStruct((tall, LANES), jnp.int16)] * owners
+        + [jax.ShapeDtypeStruct((1, rows), jnp.int32)],
+        in_specs=[vmem] * 3,
+        out_specs=[vmem] * (owners + 1),
+        compiler_params=pltpu.CompilerParams(vmem_limit_bytes=32 << 20),
+        name="pack",
+    )(embeddings, assign, order)
+    got = [packs[0]] + [
+        lax.ppermute(packs[v], ("rows", "feat"), [(i, i ^ v) for i in range(owners)])
+        for v in range(1, owners)
+    ]
+    other = [swapped(chunk, "sub", 0) for chunk in got]
+    cent, back = pl.pallas_call(
+        functools.partial(score_kernel, owners, capacity, per_owner, width),
+        out_shape=[
+            jax.ShapeDtypeStruct((per_owner, width), jnp.float32),
+            jax.ShapeDtypeStruct((owners, LANES), jnp.float32),
+        ],
+        in_specs=[vmem] * (2 * owners),
+        out_specs=[vmem] * 2,
+        scratch_shapes=[pltpu.VMEM((2 * slots, width), jnp.bfloat16)] * 2,
+        compiler_params=pltpu.CompilerParams(vmem_limit_bytes=32 << 20),
+        name="score",
+    )(*got, *other)
+    back = lax.all_to_all(back, ("rows", "feat"), split_axis=0, concat_axis=0, tiled=True)
+    best, near = pl.pallas_call(
+        functools.partial(pick_kernel, owners, capacity, per_owner),
+        out_shape=[jax.ShapeDtypeStruct((1, rows), jnp.float32)] * 2,
+        in_specs=[vmem] * 3,
+        out_specs=[vmem] * 2,
+        name="pick",
+    )(back, assign, pos)
+    return best.reshape(rows), near.reshape(rows), cent
+
+
+def body(embeddings, assign, order):
+    owners = lax.axis_size("rows") * lax.axis_size("feat")
+    rows, width = embeddings.shape
+    few = owners == 8 and 2 * rows // owners * 2 == LANES and width % LANES == 0
+    return (exchange_pairs if few else exchange_all)(embeddings, assign, order)
 
 
 def solution(mesh):

time: 104 us -> 49.1 us (0.47)
  blocking collectives: 44.1 us -> 12.6 us
  local copies, waits for them, and re-layouts: 12.4 us -> 1.82 us
  other arithmetic: 9.41 us -> 0 us
  Pallas kernels: 0 us -> 8.01 us
  waiting for transfers between devices: 19.1 us -> 11.3 us
  matrix products: 3.76 us -> 0 us
    all_to_all x1, blocking collectives: 44.1 us -> 12.6 us  [exchange_pairs(): lax.all_to_all(back, ('rows', 'feat'), split_axis=0, concat_axis=0, tiled...]
    all_to_all x4 -> x0, waiting for transfers between devices: 18.3 us -> none  [the longest x1 5.14 us: body(): lax.all_to_all(send_clu.reshape(owners, capacity), ('rows', 'feat'), spli...]
    all_to_all x4 -> x0, starting transfers between devices: 13.5 us -> none  [the longest x1 3.59 us: body(): lax.all_to_all(send_ord.reshape(owners, capacity), ('rows', 'feat'), spli...]
    ppermute x0 -> x7, starting transfers between devices: none -> 12.6 us  [exchange_pairs(): lax.ppermute(packs[v], ('rows', 'feat'), [(i, i ^ v) for i in range(owner...]
    ppermute x0 -> x7, waiting for transfers between devices: none -> 10.1 us  [exchange_pairs(): lax.ppermute(packs[v], ('rows', 'feat'), [(i, i ^ v) for i in range(owner...]
    pallas_call x0 -> x3, Pallas kernels: none -> 8.01 us  [the longest x1 4.69 us: exchange_pairs(): pl.pallas_call(functools.partial(score_kernel, owners, capacity, per_owne...]
    gather x2 -> x0, local copies, waits for them, and re-layouts: 5.01 us -> none  [the longest x1 2.5 us: body(): back_best.reshape(slots)[slot]]
    dot_general x5 -> x0, matrix products: 3.76 us -> none  [the longest x2 1.54 us: cluster_sums(): jnp.dot(member, vectors, precision=lax.Precision.HIGHEST, preferred_eleme...]
  transfers between devices with their start and end apart: 7 -> 15, of which waited for: 5 -> 6; matrix products, arithmetic and copies ran while one was open for 9% -> 0% of each run, Pallas kernels for 0% -> 0%
where the time goes in v1:
time: 49.1 us; the launch traced here: 48.8 us
  starting transfers between devices  14.4 us (29%)
  blocking collectives  12.6 us (26%)
  waiting for transfers between devices  11.3 us (23%)
  Pallas kernels  8.01 us (16%)
  local copies, waits for them, and re-layouts  1.82 us (4%)
  between operations  0.68 us (1%)
    ppermute x7, starting transfers between devices, exchange_pairs(): lax.ppermute(packs[v], ('rows', 'feat'), [(i, i ^ v) for i in range(owner...  12.6 us
    all_to_all x1, blocking collectives, exchange_pairs(): lax.all_to_all(back, ('rows', 'feat'), split_axis=0, concat_axis=0, tiled...  12.6 us
    ppermute x7, waiting for transfers between devices, exchange_pairs(): lax.ppermute(packs[v], ('rows', 'feat'), [(i, i ^ v) for i in range(owner...  10.1 us
    pallas_call x1, Pallas kernels, exchange_pairs(): pl.pallas_call(functools.partial(score_kernel, owners, capacity, per_owne...  4.69 us
    ppermute x8, starting transfers between devices, swapped(): lax.ppermute(shard, axis, [(i, i ^ 1 << distance) for i in range(lax.axis...  1.84 us
    unnamed x8, local copies, waits for them, and re-layouts  1.82 us
    pallas_call x1, Pallas kernels, exchange_pairs(): pl.pallas_call(functools.partial(pack_kernel, owners, capacity, per_owner...  1.8 us
    pallas_call x1, Pallas kernels, exchange_pairs(): pl.pallas_call(functools.partial(pick_kernel, owners, capacity, per_owner...  1.52 us
  transfers between devices with their start and end apart: 15, of which 6 were waited for; matrix products, arithmetic and copies ran while one was open for 0% of the time, Pallas kernels for 0%

profile of v1, /device:TPU:0, one launch (start us, length us, event | category | flops | bytes accessed | tf_op | source)
XLA Modules:
  0.0 48.8 jit_solution(1954153006694478938)
XLA Ops:
  0.6 0.0 copy-start.2
  0.6 0.0 copy-start.1
  0.7 0.7 %copy-done.2 = s32[256]{0:T(256)S(1)} copy-done((s32[256]{0:T(256)S(1)}, s32[256]{0:T(256)}, u32[]{:S(2)}) %copy-start.2) | copy-done | bytes 1048
  1.3 0.0 copy-done.1
  1.3 0.0 copy-start
  1.3 1.1 %copy-done = f32[256,768]{1,0:T(8,128)S(1)} copy-done((f32[256,768]{1,0:T(8,128)S(1)}, f32[256,768]{1,0:T(8,128)}, u32[]{:S(2)}) %copy-start) | copy-done | bytes 786456
  2.5 1.8 %pack.1 = (s16[400,128]{1,0:T(8,128)(2,1)S(1)}, s16[400,128]{1,0:T(8,128)(2,1)S(1)}, s16[400,128]{1,0:T(8,128)(2,1)S(1)}, s16[400,128]{1,0:T(8,128)(2,1)S(1)}, s...) custom-call(f32[256,768]{1,0:T(8,128)S(1)} %copy-done, ...), custom_call_target="tpu_custom_call" | custom-call | tf_op jit(solution)/shard_map/pack/pallas_call | solution.py:267
  4.3 0.0 copy-start.3
  4.3 3.0 %collective-permute-start = (s16[400,128]{1,0:T(8,128)(2,1)S(1)}, s16[400,128]{1,0:T(8,128)(2,1)S(1)}, u32[]{:S(2)}, u32[]{:S(2)}) collective-permute-start(s16[400,128]{1,0:T(8,128)(2,1)S(1)} %get-tuple-element.17), channel_id=1, source_target_pairs={{0,2},{2,0},{4,6},{6,4},{8,10},{10,8},{12,14},{14,12},{1,3},{3,1},... | collective-permute-start | bytes 307208 | tf_op jit(solution)/shard_map/ppermute | solution.py:277
  7.3 0.0 copy-done.3
  7.3 1.6 %collective-permute-start.1 = (s16[400,128]{1,0:T(8,128)(2,1)S(1)}, s16[400,128]{1,0:T(8,128)(2,1)S(1)}, u32[]{:S(2)}, u32[]{:S(2)}) collective-permute-start(s16[400,128]{1,0:T(8,128)(2,1)S(1)} %get-tuple-element.18), channel_id=1, source_target_pairs={{0,4},{2,6},{4,0},{6,2},{8,12},{10,14},{12,8},{14,10},{1,5},{3,7},... | collective-permute-start | bytes 307208 | tf_op jit(solution)/shard_map/ppermute | solution.py:277
  8.9 0.4 collective-permute-start.2
  9.2 2.7 %collective-permute-start.3 = (s16[400,128]{1,0:T(8,128)(2,1)S(1)}, s16[400,128]{1,0:T(8,128)(2,1)S(1)}, u32[]{:S(2)}, u32[]{:S(2)}) collective-permute-start(s16[400,128]{1,0:T(8,128)(2,1)S(1)} %get-tuple-element.20), channel_id=1, source_target_pairs={{0,8},{2,10},{4,12},{6,14},{8,0},{10,2},{12,4},{14,6},{1,9},{3,11}... | collective-permute-start | bytes 307208 | tf_op jit(solution)/shard_map/ppermute | solution.py:277
  11.9 1.3 %collective-permute-start.4 = (s16[400,128]{1,0:T(8,128)(2,1)S(1)}, s16[400,128]{1,0:T(8,128)(2,1)S(1)}, u32[]{:S(2)}, u32[]{:S(2)}) collective-permute-start(s16[400,128]{1,0:T(8,128)(2,1)S(1)} %get-tuple-element.21), channel_id=1, source_target_pairs={{0,10},{2,8},{4,14},{6,12},{8,2},{10,0},{12,6},{14,4},{1,11},{3,9}... | collective-permute-start | bytes 307208 | tf_op jit(solution)/shard_map/ppermute | solution.py:277
  13.1 0.0 collective-permute-done.refs_1_
  13.1 3.6 %collective-permute-start.5 = (s16[400,128]{1,0:T(8,128)(2,1)S(1)}, s16[400,128]{1,0:T(8,128)(2,1)S(1)}, u32[]{:S(2)}, u32[]{:S(2)}) collective-permute-start(s16[400,128]{1,0:T(8,128)(2,1)S(1)} %get-tuple-element.22), channel_id=1, source_target_pairs={{0,12},{2,14},{4,8},{6,10},{8,4},{10,6},{12,0},{14,2},{1,13},{3,15... | collective-permute-start | bytes 307208 | tf_op jit(solution)/shard_map/ppermute | solution.py:277
  16.7 0.0 collective-permute-done.1.refs_2_
  16.7 0.1 collective-permute-start.6
  16.9 0.0 collective-permute-done.2.refs_3_
  16.9 0.0 collective-permute-start.7
  16.9 0.0 collective-permute-done.3.refs_4_
  16.9 0.5 %collective-permute-start.8 = (s16[400,128]{1,0:T(8,128)(2,1)S(1)}, s16[400,128]{1,0:T(8,128)(2,1)S(1)}, u32[]{:S(2)}, u32[]{:S(2)}) collective-permute-start(s16[400,128]{1,0:T(8,128)(2,1)S(1)} %collective-permute-done.refs_1_), channel_id=1, source_target_pairs={{0,1},{1,0},{2,3},{3,2},{4,5},{5,4},{6,7},{7,6},{8,9},{9,8},{10,11... | collective-permute-start | bytes 307208 | tf_op jit(solution)/shard_map/ppermute | solution.py:21
  17.4 10.1 %collective-permute-done.4.refs_5_ = s16[400,128]{1,0:T(8,128)(2,1)S(1)} collective-permute-done((s16[400,128]{1,0:T(8,128)(2,1)S(1)}, s16[400,128]{1,0:T(8,128)(2,1)S(1)}, u32[]{:S(2)}, u32[]{:S(2)}) %collective-permute-start.4) | collective-permute-done | bytes 102432 | tf_op jit(solution)/shard_map/ppermute | solution.py:277
  27.4 0.0 collective-permute-start.9
  27.4 0.0 collective-permute-done.5.refs_6_
  27.4 0.5 %collective-permute-start.10 = (s16[400,128]{1,0:T(8,128)(2,1)S(1)}, s16[400,128]{1,0:T(8,128)(2,1)S(1)}, u32[]{:S(2)}, u32[]{:S(2)}) collective-permute-start(s16[400,128]{1,0:T(8,128)(2,1)S(1)} %collective-permute-done.2.refs_3_), channel_id=1, source_target_pairs={{0,1},{1,0},{2,3},{3,2},{4,5},{5,4},{6,7},{7,6},{8,9},{9,8},{10,11... | collective-permute-start | bytes 307208 | tf_op jit(solution)/shard_map/ppermute | solution.py:21
  28.0 0.0 collective-permute-done.6.refs_7_
  28.0 0.1 collective-permute-start.11
  28.0 0.0 collective-permute-done.7.refs_8_
  28.0 0.4 collective-permute-start.12
  28.5 0.0 collective-permute-done.8.refs_9_
  28.5 0.1 collective-permute-start.13
  28.6 0.2 collective-permute-done.9.refs_10_
  28.8 0.2 collective-permute-start.14
  29.0 0.0 collective-permute-done.10.refs_11_
  29.0 0.3 collective-permute-done.11.refs_12_
  29.3 0.2 collective-permute-done.12.refs_13_
  29.4 0.4 collective-permute-done.13.refs_14_
  29.8 0.3 collective-permute-done.14.refs_15_
  30.1 4.7 %score.1 = (f32[128,768]{1,0:T(8,128)}, f32[8,128]{1,0:T(8,128)S(1)}) custom-call(s16[400,128]{1,0:T(8,128)(2,1)S(1)} %get-tuple-element.16.refs_0_, s16[400,128]{1,0:T(8,128)(2,1)S(1)} %collective-permute-done.refs_1_, s16[400,128]{1,0:T(8,128)(2,1)S(1)} %collective-permute-done.1.refs_2_, s16[400,128]{1,0:T(8,128)(2,1)S(1)} %collective-permute-done.2.refs_3_, ...), custom_call_target="tpu_custom_call" | custom-call | tf_op jit(solution)/shard_map/score/pallas_call | solution.py:281
  34.7 12.6 %all_to_all.11 = f32[8,1,128]{2,1,0:T(1,128)} all-to-all(f32[8,1,128]{2,1,0:T(1,128)S(1)} %bitcast.10), channel_id=1, replica_groups=mesh['groups'=2,'rows'=4,'feat'=2,'sub'=2] {'rows','feat'}, dimensions={0} | all-to-all | bytes 8192 | tf_op jit(solution)/shard_map/all_to_all | solution.py:293
  47.3 1.5 %pick.1 = (f32[1,256]{1,0:T(1,128)}, f32[1,256]{1,0:T(1,128)}) custom-call(f32[8,128]{1,0:T(8,128)} %bitcast.12, s32[1,256]{1,0:T(1,128)} %bitcast.8, s32[1,256]{1,0:T(1,128)} %copy-done.3), custom_call_target="tpu_custom_call" | custom-call | tf_op jit(solution)/shard_map/pick/pallas_call | solution.py:294
Async XLA Ops:
  0.6 0.7 %copy-start.2 = (s32[256]{0:T(256)S(1)}, s32[256]{0:T(256)}, u32[]{:S(2)}) copy-start(s32[256]{0:T(256)} %param.5) | copy-start | bytes 3076
  0.6 0.7 %copy-start.1 = (s32[256]{0:T(256)S(1)}, s32[256]{0:T(256)}, u32[]{:S(2)}) copy-start(s32[256]{0:T(256)} %param.4) | copy-start | bytes 3076
  1.3 1.1 %copy-start = (f32[256,768]{1,0:T(8,128)S(1)}, f32[256,768]{1,0:T(8,128)}, u32[]{:S(2)}) copy-start(f32[256,768]{1,0:T(8,128)} %emb_ref.1) | copy-start | bytes 2359300
  4.3 3.0 %copy-start.3 = (s32[1,256]{1,0:T(1,128)}, s32[1,256]{1,0:T(1,128)S(1)}, u32[]{:S(2)}) copy-start(s32[1,256]{1,0:T(1,128)S(1)} %get-tuple-element.25.pos_ref) | copy-start | bytes 3076
  4.3 8.9 %collective-permute-start = (s16[400,128]{1,0:T(8,128)(2,1)S(1)}, s16[400,128]{1,0:T(8,128)(2,1)S(1)}, u32[]{:S(2)}, u32[]{:S(2)}) collective-permute-start(s16[400,128]{1,0:T(8,128)(2,1)S(1)} %get-tuple-element.17), channel_id=1, source_target_pairs={{0,2},{2,0},{4,6},{6,4},{8,10},{10,8},{12,14},{14,12},{1,3},{3,1},... | collective-permute-start | bytes 307208 | tf_op jit(solution)/shard_map/ppermute | solution.py:277
  7.3 9.5 %collective-permute-start.1 = (s16[400,128]{1,0:T(8,128)(2,1)S(1)}, s16[400,128]{1,0:T(8,128)(2,1)S(1)}, u32[]{:S(2)}, u32[]{:S(2)}) collective-permute-start(s16[400,128]{1,0:T(8,128)(2,1)S(1)} %get-tuple-element.18), channel_id=1, source_target_pairs={{0,4},{2,6},{4,0},{6,2},{8,12},{10,14},{12,8},{14,10},{1,5},{3,7},... | collective-permute-start | bytes 307208 | tf_op jit(solution)/shard_map/ppermute | solution.py:277
  8.9 8.0 %collective-permute-start.2 = (s16[400,128]{1,0:T(8,128)(2,1)S(1)}, s16[400,128]{1,0:T(8,128)(2,1)S(1)}, u32[]{:S(2)}, u32[]{:S(2)}) collective-permute-start(s16[400,128]{1,0:T(8,128)(2,1)S(1)} %get-tuple-element.19), channel_id=1, source_target_pairs={{0,6},{2,4},{4,2},{6,0},{8,14},{10,12},{12,10},{14,8},{1,7},{3,5},... | collective-permute-start | bytes 307208 | tf_op jit(solution)/shard_map/ppermute | solution.py:277
  9.2 7.7 %collective-permute-start.3 = (s16[400,128]{1,0:T(8,128)(2,1)S(1)}, s16[400,128]{1,0:T(8,128)(2,1)S(1)}, u32[]{:S(2)}, u32[]{:S(2)}) collective-permute-start(s16[400,128]{1,0:T(8,128)(2,1)S(1)} %get-tuple-element.20), channel_id=1, source_target_pairs={{0,8},{2,10},{4,12},{6,14},{8,0},{10,2},{12,4},{14,6},{1,9},{3,11}... | collective-permute-start | bytes 307208 | tf_op jit(solution)/shard_map/ppermute | solution.py:277
  11.9 15.6 %collective-permute-start.4 = (s16[400,128]{1,0:T(8,128)(2,1)S(1)}, s16[400,128]{1,0:T(8,128)(2,1)S(1)}, u32[]{:S(2)}, u32[]{:S(2)}) collective-permute-start(s16[400,128]{1,0:T(8,128)(2,1)S(1)} %get-tuple-element.21), channel_id=1, source_target_pairs={{0,10},{2,8},{4,14},{6,12},{8,2},{10,0},{12,6},{14,4},{1,11},{3,9}... | collective-permute-start | bytes 307208 | tf_op jit(solution)/shard_map/ppermute | solution.py:277
  13.1 14.3 %collective-permute-start.5 = (s16[400,128]{1,0:T(8,128)(2,1)S(1)}, s16[400,128]{1,0:T(8,128)(2,1)S(1)}, u32[]{:S(2)}, u32[]{:S(2)}) collective-permute-start(s16[400,128]{1,0:T(8,128)(2,1)S(1)} %get-tuple-element.22), channel_id=1, source_target_pairs={{0,12},{2,14},{4,8},{6,10},{8,4},{10,6},{12,0},{14,2},{1,13},{3,15... | collective-permute-start | bytes 307208 | tf_op jit(solution)/shard_map/ppermute | solution.py:277
  16.7 11.2 %collective-permute-start.6 = (s16[400,128]{1,0:T(8,128)(2,1)S(1)}, s16[400,128]{1,0:T(8,128)(2,1)S(1)}, u32[]{:S(2)}, u32[]{:S(2)}) collective-permute-start(s16[400,128]{1,0:T(8,128)(2,1)S(1)} %get-tuple-element.23), channel_id=1, source_target_pairs={{0,14},{2,12},{4,10},{6,8},{8,6},{10,4},{12,2},{14,0},{1,15},{3,13... | collective-permute-start | bytes 307208 | tf_op jit(solution)/shard_map/ppermute | solution.py:277
  16.9 11.2 %collective-permute-start.7 = (s16[400,128]{1,0:T(8,128)(2,1)S(1)}, s16[400,128]{1,0:T(8,128)(2,1)S(1)}, u32[]{:S(2)}, u32[]{:S(2)}) collective-permute-start(s16[400,128]{1,0:T(8,128)(2,1)S(1)} %get-tuple-element.16.refs_0_), channel_id=1, source_target_pairs={{0,1},{1,0},{2,3},{3,2},{4,5},{5,4},{6,7},{7,6},{8,9},{9,8},{10,11... | collective-permute-start | bytes 307208 | tf_op jit(solution)/shard_map/ppermute | solution.py:21
  16.9 11.6 %collective-permute-start.8 = (s16[400,128]{1,0:T(8,128)(2,1)S(1)}, s16[400,128]{1,0:T(8,128)(2,1)S(1)}, u32[]{:S(2)}, u32[]{:S(2)}) collective-permute-start(s16[400,128]{1,0:T(8,128)(2,1)S(1)} %collective-permute-done.refs_1_), channel_id=1, source_target_pairs={{0,1},{1,0},{2,3},{3,2},{4,5},{5,4},{6,7},{7,6},{8,9},{9,8},{10,11... | collective-permute-start | bytes 307208 | tf_op jit(solution)/shard_map/ppermute | solution.py:21
  27.4 1.3 %collective-permute-start.9 = (s16[400,128]{1,0:T(8,128)(2,1)S(1)}, s16[400,128]{1,0:T(8,128)(2,1)S(1)}, u32[]{:S(2)}, u32[]{:S(2)}) collective-permute-start(s16[400,128]{1,0:T(8,128)(2,1)S(1)} %collective-permute-done.1.refs_2_), channel_id=1, source_target_pairs={{0,1},{1,0},{2,3},{3,2},{4,5},{5,4},{6,7},{7,6},{8,9},{9,8},{10,11... | collective-permute-start | bytes 307208 | tf_op jit(solution)/shard_map/ppermute | solution.py:21
  27.4 1.5 %collective-permute-start.10 = (s16[400,128]{1,0:T(8,128)(2,1)S(1)}, s16[400,128]{1,0:T(8,128)(2,1)S(1)}, u32[]{:S(2)}, u32[]{:S(2)}) collective-permute-start(s16[400,128]{1,0:T(8,128)(2,1)S(1)} %collective-permute-done.2.refs_3_), channel_id=1, source_target_pairs={{0,1},{1,0},{2,3},{3,2},{4,5},{5,4},{6,7},{7,6},{8,9},{9,8},{10,11... | collective-permute-start | bytes 307208 | tf_op jit(solution)/shard_map/ppermute | solution.py:21
  28.0 1.3 %collective-permute-start.11 = (s16[400,128]{1,0:T(8,128)(2,1)S(1)}, s16[400,128]{1,0:T(8,128)(2,1)S(1)}, u32[]{:S(2)}, u32[]{:S(2)}) collective-permute-start(s16[400,128]{1,0:T(8,128)(2,1)S(1)} %collective-permute-done.3.refs_4_), channel_id=1, source_target_pairs={{0,1},{1,0},{2,3},{3,2},{4,5},{5,4},{6,7},{7,6},{8,9},{9,8},{10,11... | collective-permute-start | bytes 307208 | tf_op jit(solution)/shard_map/ppermute | solution.py:21
  28.0 1.4 %collective-permute-start.12 = (s16[400,128]{1,0:T(8,128)(2,1)S(1)}, s16[400,128]{1,0:T(8,128)(2,1)S(1)}, u32[]{:S(2)}, u32[]{:S(2)}) collective-permute-start(s16[400,128]{1,0:T(8,128)(2,1)S(1)} %collective-permute-done.4.refs_5_), channel_id=1, source_target_pairs={{0,1},{1,0},{2,3},{3,2},{4,5},{5,4},{6,7},{7,6},{8,9},{9,8},{10,11... | collective-permute-start | bytes 307208 | tf_op jit(solution)/shard_map/ppermute | solution.py:21
  28.5 1.3 %collective-permute-start.13 = (s16[400,128]{1,0:T(8,128)(2,1)S(1)}, s16[400,128]{1,0:T(8,128)(2,1)S(1)}, u32[]{:S(2)}, u32[]{:S(2)}) collective-permute-start(s16[400,128]{1,0:T(8,128)(2,1)S(1)} %collective-permute-done.5.refs_6_), channel_id=1, source_target_pairs={{0,1},{1,0},{2,3},{3,2},{4,5},{5,4},{6,7},{7,6},{8,9},{9,8},{10,11... | collective-permute-start | bytes 307208 | tf_op jit(solution)/shard_map/ppermute | solution.py:21
  28.8 1.3 %collective-permute-start.14 = (s16[400,128]{1,0:T(8,128)(2,1)S(1)}, s16[400,128]{1,0:T(8,128)(2,1)S(1)}, u32[]{:S(2)}, u32[]{:S(2)}) collective-permute-start(s16[400,128]{1,0:T(8,128)(2,1)S(1)} %collective-permute-done.6.refs_7_), channel_id=1, source_target_pairs={{0,1},{1,0},{2,3},{3,2},{4,5},{5,4},{6,7},{7,6},{8,9},{9,8},{10,11... | collective-permute-start | bytes 307208 | tf_op jit(solution)/shard_map/ppermute | solution.py:21

commit v2 on v1

v2 whole, which is shorter than its diff:
```python
import functools

import jax
import jax.numpy as jnp
from jax import lax
from jax.experimental import pallas as pl
from jax.experimental.pallas import tpu as pltpu
from jax.sharding import PartitionSpec as P

K = 1024


EPSILON = 1e-06
LANES = 128
META = 16
FULL = 32768.0
STEPS = (32, 16, 8, 4, 2, 1)
CODE = 65536.0
NONE = -1e30
FIRST = (4, 1, 5, 2, 6, 3, 7, 0)


def swapped(shard, axis, distance):
    return lax.ppermute(shard, axis, [(i, i ^ 1 << distance) for i in range(lax.axis_size(axis))])


def unit_rows(values):
    return values * lax.rsqrt(jnp.sum(values * values, axis=1, keepdims=True) + EPSILON)


def best_against(q_vec, q_clu, q_ord, k_vec, k_clu, k_ord):
    scores = lax.dot_general(
        q_vec, k_vec, (((1,), (1,)), ((), ())), preferred_element_type=jnp.float32
    )
    allowed = (q_clu[:, None] == k_clu[None, :]) & (k_ord[None, :] < q_ord[:, None])
    return jnp.max(jnp.where(allowed, scores, -1.0), axis=1)


def cluster_sums(vectors, clusters, first_cluster, per_owner):
    local = clusters - first_cluster
    member = (jnp.arange(per_owner, dtype=jnp.int32)[:, None] == local[None, :]).astype(jnp.float32)
    return jnp.dot(
        member, vectors, precision=lax.Precision.HIGHEST, preferred_element_type=jnp.float32
    )


def exchange_all(embeddings, assign, order):
    owners = lax.axis_size("rows") * lax.axis_size("feat")
    rows_dev = embeddings.shape[0]
    width = embeddings.shape[1]
    capacity = 2 * rows_dev // owners
    per_owner = K // owners
    slots = owners * capacity
    here = lax.axis_index(("rows", "feat"))
    unit = unit_rows(embeddings)
    target = assign // per_owner
    hits = (target[:, None] == jnp.arange(owners, dtype=jnp.int32)[None, :]).astype(jnp.int32)
    before = jnp.cumsum(hits, axis=0) - hits
    slot = target * capacity + jnp.sum(before * hits, axis=1)
    send_clu = jnp.full((slots,), -1, jnp.int32).at[slot].set(assign)
    send_ord = jnp.zeros((slots,), jnp.int32).at[slot].set(order)
    send_wide = jnp.zeros((slots, width), jnp.float32).at[slot].set(unit)
    spread = functools.partial(
        lax.all_to_all, axis_name=("rows", "feat"), split_axis=0, concat_axis=0, tiled=True
    )
    wide_vec = spread(send_wide.reshape(owners, capacity, width)).reshape(slots, width)
    got_clu = spread(send_clu.reshape(owners, capacity)).reshape(slots)
    got_ord = spread(send_ord.reshape(owners, capacity)).reshape(slots)
    other_wide, other_clu, other_ord = swapped((wide_vec, got_clu, got_ord), "sub", 0)
    first_cluster = here * per_owner
    own_sums = cluster_sums(wide_vec, got_clu, first_cluster, per_owner)
    pair_sums = cluster_sums(other_wide, other_clu, first_cluster, per_owner)
    own_cent = unit_rows(own_sums + pair_sums)
    got_vec = wide_vec.astype(jnp.bfloat16)
    other_vec = other_wide.astype(jnp.bfloat16)
    block = min(512, slots)
    nblock = slots // block

    def per_block(pieces):
        q_vec, q_clu, q_ord = pieces
        first = best_against(q_vec, q_clu, q_ord, got_vec, got_clu, got_ord)
        second = best_against(q_vec, q_clu, q_ord, other_vec, other_clu, other_ord)
        return jnp.maximum(first, second)

    best = lax.map(
        per_block,
        (
            got_vec.reshape(nblock, block, width),
            got_clu.reshape(nblock, block),
            got_ord.reshape(nblock, block),
        ),
    ).reshape(slots)
    local = jnp.clip(got_clu - here * per_owner, 0, per_owner - 1)
    fits = jnp.dot(
        got_vec.astype(jnp.float32),
        own_cent.T,
        precision=lax.Precision.HIGHEST,
        preferred_element_type=jnp.float32,
    )
    pick = local[:, None] == jnp.arange(per_owner, dtype=jnp.int32)[None, :]
    near = jnp.sum(jnp.where(pick, fits, 0.0), axis=1)
    back_best = spread(best.reshape(owners, capacity))
    back_near = spread(near.reshape(owners, capacity))
    return (back_best.reshape(slots)[slot], back_near.reshape(slots)[slot], own_cent)


def iota(shape, dim):
    return lax.broadcasted_iota(jnp.int32, shape, dim)


def dot(a, b):
    return jnp.dot(a, b, preferred_element_type=jnp.float32)


def dot_t(a, b):
    return lax.dot_general(a, b, (((1,), (1,)), ((), ())), preferred_element_type=jnp.float32)


def halves(x):
    high = x.astype(jnp.bfloat16)
    return high, (x - high.astype(jnp.float32)).astype(jnp.bfloat16)


def pack_kernel(owners, capacity, per_owner, emb_ref, asg_ref, ord_ref, *refs):
    packs, slot_hbm = refs[:owners], refs[owners]
    slot_ref, slot_sem = refs[owners + 1 :]
    rows, width = emb_ref.shape
    slots = owners * capacity
    tiles = width // LANES
    me = lax.axis_index(("rows", "feat"))
    asg = asg_ref[...]
    rank = ord_ref[...]
    target = lax.div(asg, jnp.int32(per_owner))
    hits = iota((owners, rows), 0) == target
    earlier = (iota((rows, rows), 0) < iota((rows, rows), 1)).astype(jnp.bfloat16)
    before = dot(hits.astype(jnp.bfloat16), earlier)
    pos = jnp.sum(jnp.where(hits, before, 0.0), axis=0, keepdims=True).astype(jnp.int32)
    slot = (target ^ me) * capacity + pos
    slot_ref[...] = slot
    slot_copy = pltpu.make_async_copy(slot_ref, slot_hbm, slot_sem)
    slot_copy.start()
    place = (iota((slots, rows), 0) == slot).astype(jnp.bfloat16)

    x = emb_ref[...]
    unit = x * lax.rsqrt(jnp.sum(x * x, axis=1, keepdims=True) + EPSILON)
    top = jnp.max(jnp.abs(unit), axis=1, keepdims=True)
    scale = jnp.ones_like(top)
    power = jnp.zeros_like(top)
    for step in STEPS:
        small = top * (scale * 2.0**step) < 1.0
        scale = jnp.where(small, scale * 2.0**step, scale)
        power = jnp.where(small, power + step, power)
    coded = jnp.minimum(jnp.round(unit * (scale * FULL)), FULL - 1.0)
    high, low = halves(coded)
    power_row = jnp.transpose(jnp.broadcast_to(power, (rows, LANES)))[:1, :]
    facts = jnp.concatenate(
        [
            (asg - target * per_owner + 1).astype(jnp.float32),
            (rank & 255).astype(jnp.float32),
            (rank >> 8).astype(jnp.float32),
            power_row,
            jnp.zeros((4, rows), jnp.float32),
        ],
        axis=0,
    ).astype(jnp.bfloat16)
    facts = dot_t(facts, place)
    packed = (dot(place, high) + dot(place, low)).astype(jnp.int32).astype(jnp.int16)
    for v in range(owners):
        mine = slice(v * capacity, (v + 1) * capacity)
        for c in range(tiles):
            packs[v][c * capacity : (c + 1) * capacity, :] = packed[
                mine, c * LANES : (c + 1) * LANES
            ]
        notes = jnp.concatenate(
            [facts[:, mine], jnp.zeros((8, LANES - capacity), jnp.float32)], axis=1
        )
        notes = jnp.concatenate([notes, jnp.zeros((META - 8, LANES), jnp.float32)], axis=0)
        packs[v][tiles * capacity :, :] = notes.astype(jnp.int32).astype(jnp.int16)
    slot_copy.wait()


def digest(chunks, capacity, width, high_ref, low_ref):
    tiles = width // LANES
    clus, codes, scales = [], [], []
    for pair in range(len(chunks) // 2):
        notes = [
            ref[tiles * capacity :, :].astype(jnp.int32).astype(jnp.float32)[:8, :capacity]
            for ref in chunks[2 * pair : 2 * pair + 2]
        ]
        notes = jnp.concatenate(notes, axis=1)
        clu = notes[0:1, :] - 1.0
        rank = notes[1:2, :] + 256.0 * notes[2:3, :]
        power = notes[3:4, :]
        scale = jnp.full_like(power, 1.0 / FULL)
        for step in STEPS:
            there = power >= step
            scale = jnp.where(there, scale * 2.0**-step, scale)
            power = jnp.where(there, power - step, power)
        clus.append(clu)
        codes.append(jnp.where(clu >= 0.0, clu * CODE + rank, -1.0))
        scales.append(scale)
    blocks = len(clus)
    cols = jnp.transpose(
        jnp.concatenate(
            codes + scales + [jnp.zeros((LANES - 2 * blocks, LANES), jnp.float32)], axis=0
        )
    )[:, : 2 * blocks]
    for i, ref in enumerate(chunks):
        here = slice(i * capacity, (i + 1) * capacity)
        for c in range(tiles):
            tile = ref[c * capacity : (c + 1) * capacity, :]
            high, low = halves(tile.astype(jnp.int32).astype(jnp.float32))
            high_ref[here, c * LANES : (c + 1) * LANES] = high
            low_ref[here, c * LANES : (c + 1) * LANES] = low
    rows = [jnp.concatenate(x, axis=1) for x in (clus, codes, scales)]
    return jnp.concatenate(rows + [jnp.zeros((5, rows[0].shape[1]), jnp.float32)], axis=0), cols


def part_sums(facts, per_owner, high_ref, low_ref):
    own = iota((per_owner, facts.shape[1]), 0).astype(jnp.float32) == facts[0:1, :]
    member = jnp.where(own, facts[2:3, :], 0.0).astype(jnp.bfloat16)
    return dot(member, high_ref[...]) + dot(member, low_ref[...])


def best_of(scores, cols, facts):
    base = facts[0:1, :] * CODE
    code = facts[1:2, :]
    blocks = cols.shape[1] // 2
    best = jnp.full((1, scores.shape[1]), NONE, jnp.float32)
    for i in range(blocks):
        key = cols[:, i : i + 1]
        found = scores[i * LANES : (i + 1) * LANES, :] * cols[:, blocks + i : blocks + i + 1]
        found = jnp.where((key >= base) & (key < code), found, NONE)
        best = jnp.maximum(best, jnp.max(found, axis=0, keepdims=True))
    return best


def early_kernel(owners, capacity, per_owner, width, *refs):
    chunks = refs[: owners // 2]
    high_ref, facts_ref, cols_ref, sums_ref, best_ref, low_ref = refs[owners // 2 :]
    facts, cols = digest(chunks, capacity, width, high_ref, low_ref)
    facts_ref[...] = facts
    cols_ref[...] = cols
    sums_ref[...] = part_sums(facts, per_owner, high_ref, low_ref)
    best_ref[...] = best_of(dot_t(high_ref[...], high_ref[...]), cols, facts)


def late_kernel(owners, capacity, per_owner, width, *refs):
    half = owners // 2
    chunks = refs[:half]
    old_ref, old_facts_ref, old_cols_ref, old_sums_ref, old_best_ref = refs[half : half + 5]
    high_ref, facts_ref, sums_ref, best_ref, low_ref = refs[half + 5 :]
    count = half * capacity
    new_ref = high_ref.at[count:, :]
    facts, cols = digest(chunks, capacity, width, new_ref, low_ref)
    high_ref[:count, :] = old_ref[...]
    old_facts = old_facts_ref[...]
    facts_ref[:, :count] = old_facts
    facts_ref[:, count:] = facts
    sums_ref[...] = old_sums_ref[...] + part_sums(facts, per_owner, new_ref, low_ref)
    scores = dot_t(high_ref[...], new_ref[...])
    best_ref[:, count:] = jnp.maximum(
        best_of(scores[:count, :], old_cols_ref[...], facts), best_of(scores[count:, :], cols, facts)
    )
    best_ref[:, :count] = jnp.maximum(
        old_best_ref[...], best_of(dot_t(new_ref[...], old_ref[...]), cols, old_facts)
    )


def last_kernel(owners, capacity, per_owner, width, *refs):
    chunks = refs[:owners]
    asked_ref, asked_facts_ref, old_sums_ref, old_best_ref = refs[owners : owners + 4]
    cent_ref, back_ref, high_ref, low_ref = refs[owners + 4 :]
    me = lax.axis_index(("rows", "feat"))
    facts, cols = digest(chunks, capacity, width, high_ref, low_ref)
    sums = old_sums_ref[...] + part_sums(facts, per_owner, high_ref, low_ref)
    cent = sums * lax.rsqrt(jnp.sum(sums * sums, axis=1, keepdims=True) + EPSILON)
    cent_ref[...] = cent
    asked = asked_ref[...]
    asked_facts = asked_facts_ref[...]
    scale = asked_facts[2:3, :]
    best = best_of(dot_t(high_ref[...], asked), cols, asked_facts)
    best = jnp.maximum(jnp.maximum(best, old_best_ref[...]) * scale, -1.0)
    fits = dot_t(jnp.concatenate(halves(cent), axis=0), asked)
    fits = fits[:per_owner, :] + fits[per_owner:, :]
    own = iota(fits.shape, 0).astype(jnp.float32) == asked_facts[0:1, :]
    near = jnp.sum(jnp.where(own, fits, 0.0), axis=0, keepdims=True) * scale
    for i, v in enumerate(FIRST):
        part = slice(i * capacity, (i + 1) * capacity)
        back_ref[pl.ds(me ^ v, 1), :] = jnp.concatenate([best[:, part], near[:, part]], axis=1)


def pick_kernel(owners, capacity, per_owner, back_ref, asg_ref, slot_ref, best_ref, near_ref):
    rows = asg_ref.shape[1]
    back = back_ref[...]
    for first in range(0, rows, LANES):
        here = slice(first, first + LANES)
        hits = iota((owners, LANES), 0) == lax.div(asg_ref[:, here], jnp.int32(per_owner))
        pos = jnp.broadcast_to(lax.rem(slot_ref[:, here], jnp.int32(capacity)), (owners, LANES))
        for start, ref in ((0, best_ref), (capacity, near_ref)):
            found = jnp.take_along_axis(back, pos + start, axis=1, mode="promise_in_bounds")
            ref[:, here] = jnp.sum(jnp.where(hits, found, 0.0), axis=0, keepdims=True)


def exchange_pairs(embeddings, assign, order):
    owners = lax.axis_size("rows") * lax.axis_size("feat")
    rows, width = embeddings.shape
    half = owners // 2
    capacity = 2 * rows // owners
    per_owner = K // owners
    slots = owners * capacity
    tall = width // LANES * capacity + META
    assign = assign.reshape(1, rows)
    order = order.reshape(1, rows)
    vmem = pl.BlockSpec(memory_space=pltpu.VMEM)
    hbm = pl.BlockSpec(memory_space=pltpu.HBM)
    params = pltpu.CompilerParams(vmem_limit_bytes=32 << 20)

    def full(*shape, dtype=jnp.float32):
        return jax.ShapeDtypeStruct(shape, dtype)

    *packs, slot = pl.pallas_call(
        functools.partial(pack_kernel, owners, capacity, per_owner),
        out_shape=[full(tall, LANES, dtype=jnp.int16)] * owners + [full(1, rows, dtype=jnp.int32)],
        in_specs=[vmem] * 3,
        out_specs=[vmem] * owners + [hbm],
        scratch_shapes=[pltpu.VMEM((1, rows), jnp.int32), pltpu.SemaphoreType.DMA],
        compiler_params=params,
        name="pack",
    )(embeddings, assign, order)
    got = [packs[0]] + [None] * (owners - 1)
    for v in range(1, owners):
        got[v] = lax.ppermute(packs[v], ("rows", "feat"), [(i, i ^ v) for i in range(owners)])
    other = [swapped(chunk, "sub", 0) for chunk in got]
    near = pl.pallas_call(
        functools.partial(early_kernel, owners, capacity, per_owner, width),
        out_shape=[
            full(slots // 2, width, dtype=jnp.bfloat16),
            full(8, slots // 2),
            full(LANES, slots // LANES),
            full(per_owner, width),
            full(1, slots // 2),
        ],
        in_specs=[vmem] * half,
        out_specs=[vmem] * 5,
        scratch_shapes=[pltpu.VMEM((slots // 2, width), jnp.bfloat16)],
        compiler_params=params,
        name="score_early",
    )(*[got[v] for v in FIRST[:half]])
    asked = pl.pallas_call(
        functools.partial(late_kernel, owners, capacity, per_owner, width),
        out_shape=[
            full(slots, width, dtype=jnp.bfloat16),
            full(8, slots),
            full(per_owner, width),
            full(1, slots),
        ],
        in_specs=[vmem] * (half + 5),
        out_specs=[vmem] * 4,
        scratch_shapes=[pltpu.VMEM((slots // 2, width), jnp.bfloat16)],
        compiler_params=params,
        name="score_late",
    )(*[got[v] for v in FIRST[half:]], *near)
    cent, back = pl.pallas_call(
        functools.partial(last_kernel, owners, capacity, per_owner, width),
        out_shape=[full(per_owner, width), full(owners, LANES)],
        in_specs=[vmem] * (owners + 4),
        out_specs=[vmem] * 2,
        scratch_shapes=[pltpu.VMEM((slots, width), jnp.bfloat16)] * 2,
        compiler_params=params,
        name="score_last",
    )(*[other[v] for v in FIRST], *asked)
    back = lax.all_to_all(back, ("rows", "feat"), split_axis=0, concat_axis=0, tiled=True)
    best, near = pl.pallas_call(
        functools.partial(pick_kernel, owners, capacity, per_owner),
        out_shape=[full(1, rows)] * 2,
        in_specs=[vmem] * 3,
        out_specs=[vmem] * 2,
        name="pick",
    )(back, assign, slot)
    return best.reshape(rows), near.reshape(rows), cent


def body(embeddings, assign, order):
    owners = lax.axis_size("rows") * lax.axis_size("feat")
    rows, width = embeddings.shape
    few = owners == 8 and 2 * rows // owners * 2 == LANES and width % LANES == 0
    return (exchange_pairs if few else exchange_all)(embeddings, assign, order)


def solution(mesh):
    return jax.shard_map(
        body,
        mesh=mesh,
        in_specs=(
            P(("groups", "rows", "feat", "sub"), None),
            P(("groups", "rows", "feat", "sub")),
            P(("groups", "rows", "feat", "sub")),
        ),
        out_specs=(
            P(("groups", "rows", "feat", "sub")),
            P(("groups", "rows", "feat", "sub")),
            P(("groups", "rows", "feat"), None),
        ),
        check_vma=False,
    )
```

time: 49.1 us -> 43.9 us (0.89)
  waiting for transfers between devices: 11.3 us -> 8.04 us
  Pallas kernels: 8.01 us -> 6.28 us
  blocking collectives: 12.6 us -> 11.3 us
  starting transfers between devices: 14.4 us -> 15.5 us
    ppermute x7, waiting for transfers between devices: 10.1 us -> 8.01 us  [exchange_pairs(): lax.ppermute(packs[v], ('rows', 'feat'), [(i, i ^ v) for i in range(owner...]
    ppermute x7, starting transfers between devices: 12.6 us -> 13.9 us  [exchange_pairs(): lax.ppermute(packs[v], ('rows', 'feat'), [(i, i ^ v) for i in range(owner...]
    ppermute x8, waiting for transfers between devices: 1.27 us -> 0.02 us  [swapped(): lax.ppermute(shard, axis, [(i, i ^ 1 << distance) for i in range(lax.axis...]
    all_to_all x1, blocking collectives: 12.6 us -> 11.3 us  [exchange_pairs(): lax.all_to_all(back, ('rows', 'feat'), split_axis=0, concat_axis=0, tiled...]
    pallas_call x1 -> x3, Pallas kernels: 4.69 us -> 3.71 us  [the longest x1 2.25 us: exchange_pairs(): pl.pallas_call(functools.partial(last_kernel, owners, capacity, per_owner...]
    pallas_call x1, Pallas kernels: 1.8 us -> 1.22 us  [exchange_pairs(): pl.pallas_call(functools.partial(pack_kernel, owners, capacity, per_owner...]
  transfers between devices with their start and end apart: 15 -> 15, of which waited for: 6 -> 3; matrix products, arithmetic and copies ran while one was open for 0% -> 0% of each run, Pallas kernels for 0% -> 3%
where the time goes in v2:
time: 43.9 us; the launch traced here: 43.7 us
  starting transfers between devices  15.5 us (35%)
  blocking collectives  11.3 us (26%)
  waiting for transfers between devices  8.04 us (18%)
  Pallas kernels  6.28 us (14%)
  local copies, waits for them, and re-layouts  1.82 us (4%)
  between operations  0.73 us (2%)
    ppermute x7, starting transfers between devices, exchange_pairs(): lax.ppermute(packs[v], ('rows', 'feat'), [(i, i ^ v) for i in range(owner...  13.9 us
    all_to_all x1, blocking collectives, exchange_pairs(): lax.all_to_all(back, ('rows', 'feat'), split_axis=0, concat_axis=0, tiled...  11.3 us
    ppermute x7, waiting for transfers between devices, exchange_pairs(): lax.ppermute(packs[v], ('rows', 'feat'), [(i, i ^ v) for i in range(owner...  8.01 us
    pallas_call x1, Pallas kernels, exchange_pairs(): pl.pallas_call(functools.partial(last_kernel, owners, capacity, per_owner...  2.25 us
    unnamed x8, local copies, waits for them, and re-layouts  1.82 us
    ppermute x8, starting transfers between devices, swapped(): lax.ppermute(shard, axis, [(i, i ^ 1 << distance) for i in range(lax.axis...  1.6 us
    pallas_call x1, Pallas kernels, exchange_pairs(): pl.pallas_call(functools.partial(pick_kernel, owners, capacity, per_owner...  1.34 us
    pallas_call x1, Pallas kernels, exchange_pairs(): pl.pallas_call(functools.partial(pack_kernel, owners, capacity, per_owner...  1.22 us
  transfers between devices with their start and end apart: 15, of which 3 were waited for; matrix products, arithmetic and copies ran while one was open for 0% of the time, Pallas kernels for 3%

profile of v2, /device:TPU:0, one launch (start us, length us, event | category | flops | bytes accessed | tf_op | source)
XLA Modules:
  0.0 43.7 jit_solution(5154559328251930986)
XLA Ops:
  0.6 0.0 copy-start.2
  0.6 0.0 copy-start.1
  0.7 0.7 %copy-done.2 = s32[256]{0:T(256)S(1)} copy-done((s32[256]{0:T(256)S(1)}, s32[256]{0:T(256)}, u32[]{:S(2)}) %copy-start.2) | copy-done | bytes 1048
  1.3 0.0 copy-done.1
  1.3 0.0 copy-start
  1.3 1.1 %copy-done = f32[256,768]{1,0:T(8,128)S(1)} copy-done((f32[256,768]{1,0:T(8,128)S(1)}, f32[256,768]{1,0:T(8,128)}, u32[]{:S(2)}) %copy-start) | copy-done | bytes 786456
  2.5 1.2 %pack.1 = (s16[400,128]{1,0:T(8,128)(2,1)S(1)}, s16[400,128]{1,0:T(8,128)(2,1)S(1)}, s16[400,128]{1,0:T(8,128)(2,1)S(1)}, s16[400,128]{1,0:T(8,128)(2,1)S(1)}, s...) custom-call(f32[256,768]{1,0:T(8,128)S(1)} %copy-done, ...), custom_call_target="tpu_custom_call" | custom-call | tf_op jit(solution)/shard_map/pack/pallas_call | solution.py:322
  3.7 0.0 copy-start.3
  3.7 4.1 %collective-permute-start = (s16[400,128]{1,0:T(8,128)(2,1)S(1)}, s16[400,128]{1,0:T(8,128)(2,1)S(1)}, u32[]{:S(2)}, u32[]{:S(2)}) collective-permute-start(s16[400,128]{1,0:T(8,128)(2,1)S(1)} %get-tuple-element.25), channel_id=1, source_target_pairs={{0,8},{2,10},{4,12},{6,14},{8,0},{10,2},{12,4},{14,6},{1,9},{3,11}... | collective-permute-start | bytes 307208 | tf_op jit(solution)/shard_map/ppermute | solution.py:333
  7.8 0.0 copy-done.3
  7.8 1.5 %collective-permute-start.2 = (s16[400,128]{1,0:T(8,128)(2,1)S(1)}, s16[400,128]{1,0:T(8,128)(2,1)S(1)}, u32[]{:S(2)}, u32[]{:S(2)}) collective-permute-start(s16[400,128]{1,0:T(8,128)(2,1)S(1)} %get-tuple-element.26), channel_id=1, source_target_pairs={{0,2},{2,0},{4,6},{6,4},{8,10},{10,8},{12,14},{14,12},{1,3},{3,1},... | collective-permute-start | bytes 307208 | tf_op jit(solution)/shard_map/ppermute | solution.py:333
  9.3 0.4 collective-permute-start.4
  9.7 1.6 %collective-permute-start.6 = (s16[400,128]{1,0:T(8,128)(2,1)S(1)}, s16[400,128]{1,0:T(8,128)(2,1)S(1)}, u32[]{:S(2)}, u32[]{:S(2)}) collective-permute-start(s16[400,128]{1,0:T(8,128)(2,1)S(1)} %get-tuple-element.28), channel_id=1, source_target_pairs={{0,4},{2,6},{4,0},{6,2},{8,12},{10,14},{12,8},{14,10},{1,5},{3,7},... | collective-permute-start | bytes 307208 | tf_op jit(solution)/shard_map/ppermute | solution.py:333
  11.3 1.4 %collective-permute-start.10 = (s16[400,128]{1,0:T(8,128)(2,1)S(1)}, s16[400,128]{1,0:T(8,128)(2,1)S(1)}, u32[]{:S(2)}, u32[]{:S(2)}) collective-permute-start(s16[400,128]{1,0:T(8,128)(2,1)S(1)} %get-tuple-element.30), channel_id=1, source_target_pairs={{0,6},{2,4},{4,2},{6,0},{8,14},{10,12},{12,10},{14,8},{1,7},{3,5},... | collective-permute-start | bytes 307208 | tf_op jit(solution)/shard_map/ppermute | solution.py:333
  12.7 2.3 %collective-permute-done.refs_0_ = s16[400,128]{1,0:T(8,128)(2,1)S(1)} collective-permute-done((s16[400,128]{1,0:T(8,128)(2,1)S(1)}, s16[400,128]{1,0:T(8,128)(2,1)S(1)}, u32[]{:S(2)}, u32[]{:S(2)}) %collective-permute-start) | collective-permute-done | bytes 102432 | tf_op jit(solution)/shard_map/ppermute | solution.py:333
  15.0 4.8 %collective-permute-start.12 = (s16[400,128]{1,0:T(8,128)(2,1)S(1)}, s16[400,128]{1,0:T(8,128)(2,1)S(1)}, u32[]{:S(2)}, u32[]{:S(2)}) collective-permute-start(s16[400,128]{1,0:T(8,128)(2,1)S(1)} %get-tuple-element.31), channel_id=1, source_target_pairs={{0,14},{2,12},{4,10},{6,8},{8,6},{10,4},{12,2},{14,0},{1,15},{3,13... | collective-permute-start | bytes 307208 | tf_op jit(solution)/shard_map/ppermute | solution.py:333
  19.7 0.0 collective-permute-done.2.refs_1_
  19.7 0.1 collective-permute-start.8
  19.9 0.0 collective-permute-done.4.refs_2_
  19.9 0.0 collective-permute-start.14
  19.9 0.0 collective-permute-done.6.refs_3_
  19.9 0.5 %collective-permute-start.1 = (s16[400,128]{1,0:T(8,128)(2,1)S(1)}, s16[400,128]{1,0:T(8,128)(2,1)S(1)}, u32[]{:S(2)}, u32[]{:S(2)}) collective-permute-start(s16[400,128]{1,0:T(8,128)(2,1)S(1)} %collective-permute-done.refs_0_), channel_id=1, source_target_pairs={{0,1},{1,0},{2,3},{3,2},{4,5},{5,4},{6,7},{7,6},{8,9},{9,8},{10,11... | collective-permute-start | bytes 307208 | tf_op jit(solution)/shard_map/ppermute | solution.py:24
  20.4 0.0 collective-permute-done.10.refs_1_
  20.4 0.1 collective-permute-start.11
  20.5 2.6 %collective-permute-done.12.refs_2_ = s16[400,128]{1,0:T(8,128)(2,1)S(1)} collective-permute-done((s16[400,128]{1,0:T(8,128)(2,1)S(1)}, s16[400,128]{1,0:T(8,128)(2,1)S(1)}, u32[]{:S(2)}, u32[]{:S(2)}) %collective-permute-start.12) | collective-permute-done | bytes 102432 | tf_op jit(solution)/shard_map/ppermute | solution.py:333
  23.0 0.0 collective-permute-start.13
  23.0 3.2 %collective-permute-done.8.refs_0_ = s16[400,128]{1,0:T(8,128)(2,1)S(1)} collective-permute-done((s16[400,128]{1,0:T(8,128)(2,1)S(1)}, s16[400,128]{1,0:T(8,128)(2,1)S(1)}, u32[]{:S(2)}, u32[]{:S(2)}) %collective-permute-start.8) | collective-permute-done | bytes 102432 | tf_op jit(solution)/shard_map/ppermute | solution.py:333
  26.2 0.0 collective-permute-start.3
  26.2 0.0 collective-permute-done.14.refs_7_
  26.2 0.5 %collective-permute-start.5 = (s16[400,128]{1,0:T(8,128)(2,1)S(1)}, s16[400,128]{1,0:T(8,128)(2,1)S(1)}, u32[]{:S(2)}, u32[]{:S(2)}) collective-permute-start(s16[400,128]{1,0:T(8,128)(2,1)S(1)} %collective-permute-done.4.refs_2_), channel_id=1, source_target_pairs={{0,1},{1,0},{2,3},{3,2},{4,5},{5,4},{6,7},{7,6},{8,9},{9,8},{10,11... | collective-permute-start | bytes 307208 | tf_op jit(solution)/shard_map/ppermute | solution.py:24
  26.7 0.0 collective-permute-done.1.refs_0_
  26.7 0.1 collective-permute-start.7
  26.8 0.0 collective-permute-done.11.refs_5_
  26.8 0.4 %collective-permute-start.9 = (s16[400,128]{1,0:T(8,128)(2,1)S(1)}, s16[400,128]{1,0:T(8,128)(2,1)S(1)}, u32[]{:S(2)}, u32[]{:S(2)}) collective-permute-start(s16[400,128]{1,0:T(8,128)(2,1)S(1)} %collective-permute-done.8.refs_0_), channel_id=1, source_target_pairs={{0,1},{1,0},{2,3},{3,2},{4,5},{5,4},{6,7},{7,6},{8,9},{9,8},{10,11... | collective-permute-start | bytes 307208 | tf_op jit(solution)/shard_map/ppermute | solution.py:24
  27.2 0.6 %score_early.1 = (bf16[256,768]{1,0:T(8,128)(2,1)S(1)}, f32[8,256]{1,0:T(8,128)S(1)}, f32[128,4]{1,0:T(8,128)S(1)}, f32[128,768]{1,0:T(8,128)S(1)}, f32[1,256]{1,0:T(1,128)S(1)}) custom-call(s16[400,128]{1,0:T(8,128)(2,1)S(1)} %collective-permute-done.refs_0_, s16[400,128]{1,0:T(8,128)(2,1)S(1)} %collective-permute-done.2.refs_1_, ...), custom_call_target="tpu_custom_call" | custom-call | tf_op jit(solution)/shard_map/score_early/pallas_call | solution.py:335
  27.8 0.9 %score_late.1 = (bf16[512,768]{1,0:T(8,128)(2,1)S(1)}, f32[8,512]{1,0:T(8,128)S(1)}, f32[128,768]{1,0:T(8,128)S(1)}, f32[1,512]{1,0:T(1,128)S(1)}) custom-call(s16[400,128]{1,0:T(8,128)(2,1)S(1)} %collective-permute-done.8.refs_0_, s16[400,128]{1,0:T(8,128)(2,1)S(1)} %collective-permute-done.10.refs_1_, s16[400,128]{1,0:T(8,128)(2,1)S(1)} %collective-permute-done.12.refs_2_, ...), custom_call_target="tpu_custom_call" | custom-call | tf_op jit(solution)/shard_map/score_late/pallas_call | solution.py:350
  28.7 0.0 collective-permute-done.13.refs_6_
  28.7 0.0 collective-permute-done.3.refs_1_
  28.7 0.0 collective-permute-done.5.refs_2_
  28.7 0.0 collective-permute-done.7.refs_3_
  28.8 0.0 collective-permute-done.9.refs_4_
  28.8 2.2 %score_last.1 = (f32[128,768]{1,0:T(8,128)}, f32[8,128]{1,0:T(8,128)S(1)}) custom-call(s16[400,128]{1,0:T(8,128)(2,1)S(1)} %collective-permute-done.1.refs_0_, s16[400,128]{1,0:T(8,128)(2,1)S(1)} %collective-permute-done.3.refs_1_, s16[400,128]{1,0:T(8,128)(2,1)S(1)} %collective-permute-done.5.refs_2_, s16[400,128]{1,0:T(8,128)(2,1)S(1)} %collective-permute-done.7.refs_3_, ...), custom_call_target="tpu_custom_call" | custom-call | tf_op jit(solution)/shard_map/score_last/pallas_call | solution.py:364
  31.0 11.3 %all_to_all.11 = f32[8,1,128]{2,1,0:T(1,128)} all-to-all(f32[8,1,128]{2,1,0:T(1,128)S(1)} %bitcast.10), channel_id=1, replica_groups=mesh['groups'=2,'rows'=4,'feat'=2,'sub'=2] {'rows','feat'}, dimensions={0} | all-to-all | bytes 8192 | tf_op jit(solution)/shard_map/all_to_all | solution.py:373
  42.3 1.3 %pick.1 = (f32[1,256]{1,0:T(1,128)}, f32[1,256]{1,0:T(1,128)}) custom-call(f32[8,128]{1,0:T(8,128)} %bitcast.12, s32[1,256]{1,0:T(1,128)} %bitcast.8, s32[1,256]{1,0:T(1,128)} %copy-done.3), custom_call_target="tpu_custom_call" | custom-call | tf_op jit(solution)/shard_map/pick/pallas_call | solution.py:374
Async XLA Ops:
  0.6 0.7 %copy-start.2 = (s32[256]{0:T(256)S(1)}, s32[256]{0:T(256)}, u32[]{:S(2)}) copy-start(s32[256]{0:T(256)} %param.5) | copy-start | bytes 3076
  0.6 0.7 %copy-start.1 = (s32[256]{0:T(256)S(1)}, s32[256]{0:T(256)}, u32[]{:S(2)}) copy-start(s32[256]{0:T(256)} %param.4) | copy-start | bytes 3076
  1.3 1.1 %copy-start = (f32[256,768]{1,0:T(8,128)S(1)}, f32[256,768]{1,0:T(8,128)}, u32[]{:S(2)}) copy-start(f32[256,768]{1,0:T(8,128)} %emb_ref.1) | copy-start | bytes 2359300
  3.7 4.1 %copy-start.3 = (s32[1,256]{1,0:T(1,128)}, s32[1,256]{1,0:T(1,128)S(1)}, u32[]{:S(2)}) copy-start(s32[1,256]{1,0:T(1,128)S(1)} %get-tuple-element.43.slot_ref) | copy-start | bytes 3076
  3.7 11.3 %collective-permute-start = (s16[400,128]{1,0:T(8,128)(2,1)S(1)}, s16[400,128]{1,0:T(8,128)(2,1)S(1)}, u32[]{:S(2)}, u32[]{:S(2)}) collective-permute-start(s16[400,128]{1,0:T(8,128)(2,1)S(1)} %get-tuple-element.25), channel_id=1, source_target_pairs={{0,8},{2,10},{4,12},{6,14},{8,0},{10,2},{12,4},{14,6},{1,9},{3,11}... | collective-permute-start | bytes 307208 | tf_op jit(solution)/shard_map/ppermute | solution.py:333
  7.8 11.9 %collective-permute-start.2 = (s16[400,128]{1,0:T(8,128)(2,1)S(1)}, s16[400,128]{1,0:T(8,128)(2,1)S(1)}, u32[]{:S(2)}, u32[]{:S(2)}) collective-permute-start(s16[400,128]{1,0:T(8,128)(2,1)S(1)} %get-tuple-element.26), channel_id=1, source_target_pairs={{0,2},{2,0},{4,6},{6,4},{8,10},{10,8},{12,14},{14,12},{1,3},{3,1},... | collective-permute-start | bytes 307208 | tf_op jit(solution)/shard_map/ppermute | solution.py:333
  9.3 10.6 %collective-permute-start.4 = (s16[400,128]{1,0:T(8,128)(2,1)S(1)}, s16[400,128]{1,0:T(8,128)(2,1)S(1)}, u32[]{:S(2)}, u32[]{:S(2)}) collective-permute-start(s16[400,128]{1,0:T(8,128)(2,1)S(1)} %get-tuple-element.27), channel_id=1, source_target_pairs={{0,10},{2,8},{4,14},{6,12},{8,2},{10,0},{12,6},{14,4},{1,11},{3,9}... | collective-permute-start | bytes 307208 | tf_op jit(solution)/shard_map/ppermute | solution.py:333
  9.7 10.1 %collective-permute-start.6 = (s16[400,128]{1,0:T(8,128)(2,1)S(1)}, s16[400,128]{1,0:T(8,128)(2,1)S(1)}, u32[]{:S(2)}, u32[]{:S(2)}) collective-permute-start(s16[400,128]{1,0:T(8,128)(2,1)S(1)} %get-tuple-element.28), channel_id=1, source_target_pairs={{0,4},{2,6},{4,0},{6,2},{8,12},{10,14},{12,8},{14,10},{1,5},{3,7},... | collective-permute-start | bytes 307208 | tf_op jit(solution)/shard_map/ppermute | solution.py:333
  11.3 9.1 %collective-permute-start.10 = (s16[400,128]{1,0:T(8,128)(2,1)S(1)}, s16[400,128]{1,0:T(8,128)(2,1)S(1)}, u32[]{:S(2)}, u32[]{:S(2)}) collective-permute-start(s16[400,128]{1,0:T(8,128)(2,1)S(1)} %get-tuple-element.30), channel_id=1, source_target_pairs={{0,6},{2,4},{4,2},{6,0},{8,14},{10,12},{12,10},{14,8},{1,7},{3,5},... | collective-permute-start | bytes 307208 | tf_op jit(solution)/shard_map/ppermute | solution.py:333
  15.0 8.1 %collective-permute-start.12 = (s16[400,128]{1,0:T(8,128)(2,1)S(1)}, s16[400,128]{1,0:T(8,128)(2,1)S(1)}, u32[]{:S(2)}, u32[]{:S(2)}) collective-permute-start(s16[400,128]{1,0:T(8,128)(2,1)S(1)} %get-tuple-element.31), channel_id=1, source_target_pairs={{0,14},{2,12},{4,10},{6,8},{8,6},{10,4},{12,2},{14,0},{1,15},{3,13... | collective-permute-start | bytes 307208 | tf_op jit(solution)/shard_map/ppermute | solution.py:333
  19.7 6.5 %collective-permute-start.8 = (s16[400,128]{1,0:T(8,128)(2,1)S(1)}, s16[400,128]{1,0:T(8,128)(2,1)S(1)}, u32[]{:S(2)}, u32[]{:S(2)}) collective-permute-start(s16[400,128]{1,0:T(8,128)(2,1)S(1)} %get-tuple-element.29), channel_id=1, source_target_pairs={{0,12},{2,14},{4,8},{6,10},{8,4},{10,6},{12,0},{14,2},{1,13},{3,15... | collective-permute-start | bytes 307208 | tf_op jit(solution)/shard_map/ppermute | solution.py:333
  19.9 6.3 %collective-permute-start.14 = (s16[400,128]{1,0:T(8,128)(2,1)S(1)}, s16[400,128]{1,0:T(8,128)(2,1)S(1)}, u32[]{:S(2)}, u32[]{:S(2)}) collective-permute-start(s16[400,128]{1,0:T(8,128)(2,1)S(1)} %get-tuple-element.32.refs_3_), channel_id=1, source_target_pairs={{0,1},{1,0},{2,3},{3,2},{4,5},{5,4},{6,7},{7,6},{8,9},{9,8},{10,11... | collective-permute-start | bytes 307208 | tf_op jit(solution)/shard_map/ppermute | solution.py:24
  19.9 6.8 %collective-permute-start.1 = (s16[400,128]{1,0:T(8,128)(2,1)S(1)}, s16[400,128]{1,0:T(8,128)(2,1)S(1)}, u32[]{:S(2)}, u32[]{:S(2)}) collective-permute-start(s16[400,128]{1,0:T(8,128)(2,1)S(1)} %collective-permute-done.refs_0_), channel_id=1, source_target_pairs={{0,1},{1,0},{2,3},{3,2},{4,5},{5,4},{6,7},{7,6},{8,9},{9,8},{10,11... | collective-permute-start | bytes 307208 | tf_op jit(solution)/shard_map/ppermute | solution.py:24
  20.4 6.4 %collective-permute-start.11 = (s16[400,128]{1,0:T(8,128)(2,1)S(1)}, s16[400,128]{1,0:T(8,128)(2,1)S(1)}, u32[]{:S(2)}, u32[]{:S(2)}) collective-permute-start(s16[400,128]{1,0:T(8,128)(2,1)S(1)} %collective-permute-done.10.refs_1_), channel_id=1, source_target_pairs={{0,1},{1,0},{2,3},{3,2},{4,5},{5,4},{6,7},{7,6},{8,9},{9,8},{10,11... | collective-permute-start | bytes 307208 | tf_op jit(solution)/shard_map/ppermute | solution.py:24
  23.0 5.7 %collective-permute-start.13 = (s16[400,128]{1,0:T(8,128)(2,1)S(1)}, s16[400,128]{1,0:T(8,128)(2,1)S(1)}, u32[]{:S(2)}, u32[]{:S(2)}) collective-permute-start(s16[400,128]{1,0:T(8,128)(2,1)S(1)} %collective-permute-done.12.refs_2_), channel_id=1, source_target_pairs={{0,1},{1,0},{2,3},{3,2},{4,5},{5,4},{6,7},{7,6},{8,9},{9,8},{10,11... | collective-permute-start | bytes 307208 | tf_op jit(solution)/shard_map/ppermute | solution.py:24
  26.2 2.5 %collective-permute-start.3 = (s16[400,128]{1,0:T(8,128)(2,1)S(1)}, s16[400,128]{1,0:T(8,128)(2,1)S(1)}, u32[]{:S(2)}, u32[]{:S(2)}) collective-permute-start(s16[400,128]{1,0:T(8,128)(2,1)S(1)} %collective-permute-done.2.refs_1_), channel_id=1, source_target_pairs={{0,1},{1,0},{2,3},{3,2},{4,5},{5,4},{6,7},{7,6},{8,9},{9,8},{10,11... | collective-permute-start | bytes 307208 | tf_op jit(solution)/shard_map/ppermute | solution.py:24
  26.2 2.5 %collective-permute-start.5 = (s16[400,128]{1,0:T(8,128)(2,1)S(1)}, s16[400,128]{1,0:T(8,128)(2,1)S(1)}, u32[]{:S(2)}, u32[]{:S(2)}) collective-permute-start(s16[400,128]{1,0:T(8,128)(2,1)S(1)} %collective-permute-done.4.refs_2_), channel_id=1, source_target_pairs={{0,1},{1,0},{2,3},{3,2},{4,5},{5,4},{6,7},{7,6},{8,9},{9,8},{10,11... | collective-permute-start | bytes 307208 | tf_op jit(solution)/shard_map/ppermute | solution.py:24
  26.7 2.0 %collective-permute-start.7 = (s16[400,128]{1,0:T(8,128)(2,1)S(1)}, s16[400,128]{1,0:T(8,128)(2,1)S(1)}, u32[]{:S(2)}, u32[]{:S(2)}) collective-permute-start(s16[400,128]{1,0:T(8,128)(2,1)S(1)} %collective-permute-done.6.refs_3_), channel_id=1, source_target_pairs={{0,1},{1,0},{2,3},{3,2},{4,5},{5,4},{6,7},{7,6},{8,9},{9,8},{10,11... | collective-permute-start | bytes 307208 | tf_op jit(solution)/shard_map/ppermute | solution.py:24
  26.8 2.0 %collective-permute-start.9 = (s16[400,128]{1,0:T(8,128)(2,1)S(1)}, s16[400,128]{1,0:T(8,128)(2,1)S(1)}, u32[]{:S(2)}, u32[]{:S(2)}) collective-permute-start(s16[400,128]{1,0:T(8,128)(2,1)S(1)} %collective-permute-done.8.refs_0_), channel_id=1, source_target_pairs={{0,1},{1,0},{2,3},{3,2},{4,5},{5,4},{6,7},{7,6},{8,9},{9,8},{10,11... | collective-permute-start | bytes 307208 | tf_op jit(solution)/shard_map/ppermute | solution.py:24

commit v3 on v2

--- a/solution.py
+++ b/solution.py
@@ -121,26 +121,28 @@
     return high, (x - high.astype(jnp.float32)).astype(jnp.bfloat16)
 
 
-def pack_kernel(owners, capacity, per_owner, emb_ref, asg_ref, ord_ref, *refs):
-    packs, slot_hbm = refs[:owners], refs[owners]
-    slot_ref, slot_sem = refs[owners + 1 :]
+def earlier_kernel(earlier_ref):
+    shape = earlier_ref.shape
+    earlier_ref[...] = (iota(shape, 0) < iota(shape, 1)).astype(jnp.bfloat16)
+
+
+def slots_of(owners, capacity, per_owner, asg, earlier):
+    me = lax.axis_index(("rows", "feat"))
+    target = lax.div(asg, jnp.int32(per_owner))
+    hits = iota((owners, asg.shape[1]), 0) == target
+    before = dot(hits.astype(jnp.bfloat16), earlier)
+    pos = jnp.sum(jnp.where(hits, before, 0.0), axis=0, keepdims=True).astype(jnp.int32)
+    return (target ^ me) * capacity + pos
+
+
+def pack_kernel(owners, capacity, per_owner, emb_ref, asg_ref, ord_ref, earlier_ref, *packs):
     rows, width = emb_ref.shape
     slots = owners * capacity
     tiles = width // LANES
-    me = lax.axis_index(("rows", "feat"))
     asg = asg_ref[...]
     rank = ord_ref[...]
-    target = lax.div(asg, jnp.int32(per_owner))
-    hits = iota((owners, rows), 0) == target
-    earlier = (iota((rows, rows), 0) < iota((rows, rows), 1)).astype(jnp.bfloat16)
-    before = dot(hits.astype(jnp.bfloat16), earlier)
-    pos = jnp.sum(jnp.where(hits, before, 0.0), axis=0, keepdims=True).astype(jnp.int32)
-    slot = (target ^ me) * capacity + pos
-    slot_ref[...] = slot
-    slot_copy = pltpu.make_async_copy(slot_ref, slot_hbm, slot_sem)
-    slot_copy.start()
+    slot = slots_of(owners, capacity, per_owner, asg, earlier_ref[...])
     place = (iota((slots, rows), 0) == slot).astype(jnp.bfloat16)
-
     x = emb_ref[...]
     unit = x * lax.rsqrt(jnp.sum(x * x, axis=1, keepdims=True) + EPSILON)
     top = jnp.max(jnp.abs(unit), axis=1, keepdims=True)
@@ -155,7 +157,7 @@
     power_row = jnp.transpose(jnp.broadcast_to(power, (rows, LANES)))[:1, :]
     facts = jnp.concatenate(
         [
-            (asg - target * per_owner + 1).astype(jnp.float32),
+            (lax.rem(asg, jnp.int32(per_owner)) + 1).astype(jnp.float32),
             (rank & 255).astype(jnp.float32),
             (rank >> 8).astype(jnp.float32),
             power_row,
@@ -176,7 +178,6 @@
         )
         notes = jnp.concatenate([notes, jnp.zeros((META - 8, LANES), jnp.float32)], axis=0)
         packs[v][tiles * capacity :, :] = notes.astype(jnp.int32).astype(jnp.int16)
-    slot_copy.wait()
 
 
 def digest(chunks, capacity, width, high_ref, low_ref):
@@ -236,8 +237,9 @@
 
 
 def early_kernel(owners, capacity, per_owner, width, *refs):
-    chunks = refs[: owners // 2]
-    high_ref, facts_ref, cols_ref, sums_ref, best_ref, low_ref = refs[owners // 2 :]
+    asg_ref, earlier_ref, *chunks = refs[: owners // 2 + 2]
+    slot_ref, high_ref, facts_ref, cols_ref, sums_ref, best_ref, low_ref = refs[owners // 2 + 2 :]
+    slot_ref[...] = slots_of(owners, capacity, per_owner, asg_ref[...], earlier_ref[...])
     facts, cols = digest(chunks, capacity, width, high_ref, low_ref)
     facts_ref[...] = facts
     cols_ref[...] = cols
@@ -313,40 +315,49 @@
     assign = assign.reshape(1, rows)
     order = order.reshape(1, rows)
     vmem = pl.BlockSpec(memory_space=pltpu.VMEM)
-    hbm = pl.BlockSpec(memory_space=pltpu.HBM)
     params = pltpu.CompilerParams(vmem_limit_bytes=32 << 20)
 
     def full(*shape, dtype=jnp.float32):
         return jax.ShapeDtypeStruct(shape, dtype)
 
-    *packs, slot = pl.pallas_call(
+    earlier = pl.pallas_call(
+        earlier_kernel,
+        out_shape=full(rows, rows, dtype=jnp.bfloat16),
+        out_specs=vmem,
+        compiler_params=params,
+        cost_estimate=pl.CostEstimate(flops=1 << 30, bytes_accessed=8 << 20, transcendentals=0),
+        name="earlier",
+    )()
+    packs = pl.pallas_call(
         functools.partial(pack_kernel, owners, capacity, per_owner),
-        out_shape=[full(tall, LANES, dtype=jnp.int16)] * owners + [full(1, rows, dtype=jnp.int32)],
-        in_specs=[vmem] * 3,
-        out_specs=[vmem] * owners + [hbm],
-        scratch_shapes=[pltpu.VMEM((1, rows), jnp.int32), pltpu.SemaphoreType.DMA],
+        out_shape=[full(tall, LANES, dtype=jnp.int16)] * owners,
+        in_specs=[vmem] * 4,
+        out_specs=[vmem] * owners,
         compiler_params=params,
         name="pack",
-    )(embeddings, assign, order)
+    )(embeddings, assign, order, earlier)
     got = [packs[0]] + [None] * (owners - 1)
     for v in range(1, owners):
         got[v] = lax.ppermute(packs[v], ("rows", "feat"), [(i, i ^ v) for i in range(owners)])
-    other = [swapped(chunk, "sub", 0) for chunk in got]
-    near = pl.pallas_call(
+    slot, *near = pl.pallas_call(
         functools.partial(early_kernel, owners, capacity, per_owner, width),
         out_shape=[
+            full(1, rows, dtype=jnp.int32),
             full(slots // 2, width, dtype=jnp.bfloat16),
             full(8, slots // 2),
             full(LANES, slots // LANES),
             full(per_owner, width),
             full(1, slots // 2),
         ],
-        in_specs=[vmem] * half,
-        out_specs=[vmem] * 5,
+        in_specs=[vmem] * (half + 2),
+        out_specs=[vmem] * 6,
         scratch_shapes=[pltpu.VMEM((slots // 2, width), jnp.bfloat16)],
         compiler_params=params,
         name="score_early",
-    )(*[got[v] for v in FIRST[:half]])
+    )(assign, earlier, *[got[v] for v in FIRST[:half]])
+    last = FIRST[-2]
+    held, near = lax.optimization_barrier((got[last], near))
+    other = [swapped(held if v == last else got[v], "sub", 0) for v in range(owners)]
     asked = pl.pallas_call(
         functools.partial(late_kernel, owners, capacity, per_owner, width),
         out_shape=[

time: 43.9 us -> 42.2 us (0.961)
  waiting for transfers between devices: 8.04 us -> 3.59 us
  starting transfers between devices: 15.5 us -> 17.4 us
  blocking collectives: 11.3 us -> 12.5 us
    ppermute x7, waiting for transfers between devices: 8.01 us -> 3.51 us  [exchange_pairs(): lax.ppermute(packs[v], ('rows', 'feat'), [(i, i ^ v) for i in range(owner...]
    ppermute x7, starting transfers between devices: 13.9 us -> 15.8 us  [exchange_pairs(): lax.ppermute(packs[v], ('rows', 'feat'), [(i, i ^ v) for i in range(owner...]
    all_to_all x1, blocking collectives: 11.3 us -> 12.5 us  [exchange_pairs(): lax.all_to_all(back, ('rows', 'feat'), split_axis=0, concat_axis=0, tiled...]
  transfers between devices with their start and end apart: 15 -> 15, of which waited for: 3 -> 5; matrix products, arithmetic and copies ran while one was open for 0% -> 0% of each run, Pallas kernels for 3% -> 4%
where the time goes in v3:
time: 42.2 us; the launch traced here: 42 us
  starting transfers between devices  17.4 us (41%)
  blocking collectives  12.5 us (30%)
  Pallas kernels  6.18 us (15%)
  waiting for transfers between devices  3.59 us (9%)
  local copies, waits for them, and re-layouts  1.61 us (4%)
  between operations  0.74 us (2%)
    ppermute x7, starting transfers between devices, exchange_pairs(): lax.ppermute(packs[v], ('rows', 'feat'), [(i, i ^ v) for i in range(owner...  15.8 us
    all_to_all x1, blocking collectives, exchange_pairs(): lax.all_to_all(back, ('rows', 'feat'), split_axis=0, concat_axis=0, tiled...  12.5 us
    ppermute x7, waiting for transfers between devices, exchange_pairs(): lax.ppermute(packs[v], ('rows', 'feat'), [(i, i ^ v) for i in range(owner...  3.51 us
    pallas_call x1, Pallas kernels, exchange_pairs(): pl.pallas_call(functools.partial(last_kernel, owners, capacity, per_owner...  2.24 us
    unnamed x8, local copies, waits for them, and re-layouts  1.61 us
    ppermute x8, starting transfers between devices, swapped(): lax.ppermute(shard, axis, [(i, i ^ 1 << distance) for i in range(lax.axis...  1.54 us
    pallas_call x1, Pallas kernels, exchange_pairs(): pl.pallas_call(functools.partial(pick_kernel, owners, capacity, per_owner...  1.34 us
    pallas_call x1, Pallas kernels, exchange_pairs(): pl.pallas_call(functools.partial(pack_kernel, owners, capacity, per_owner...  1.08 us
  transfers between devices with their start and end apart: 15, of which 5 were waited for; matrix products, arithmetic and copies ran while one was open for 0% of the time, Pallas kernels for 4%

profile of v3, /device:TPU:0, one launch (start us, length us, event | category | flops | bytes accessed | tf_op | source)
XLA Modules:
  0.0 42.0 jit_solution(6026919350900464128)
XLA Ops:
  0.6 0.0 copy-start
  0.6 0.0 copy-start.2
  0.7 0.0 copy-start.1
  0.7 1.1 %copy-done = f32[256,768]{1,0:T(8,128)S(1)} copy-done((f32[256,768]{1,0:T(8,128)S(1)}, f32[256,768]{1,0:T(8,128)}, u32[]{:S(2)}) %copy-start) | copy-done | bytes 786456
  1.8 0.0 copy-done.2
  1.8 0.0 copy-done.1
  1.8 1.1 %pack.1 = (s16[400,128]{1,0:T(8,128)(2,1)S(1)}, s16[400,128]{1,0:T(8,128)(2,1)S(1)}, s16[400,128]{1,0:T(8,128)(2,1)S(1)}, s16[400,128]{1,0:T(8,128)(2,1)S(1)}, s...) custom-call(f32[256,768]{1,0:T(8,128)S(1)} %copy-done, ...), custom_call_target="tpu_custom_call" | custom-call | tf_op jit(solution)/shard_map/pack/pallas_call | solution.py:331
  2.9 4.1 %collective-permute-start = (s16[400,128]{1,0:T(8,128)(2,1)S(1)}, s16[400,128]{1,0:T(8,128)(2,1)S(1)}, u32[]{:S(2)}, u32[]{:S(2)}) collective-permute-start(s16[400,128]{1,0:T(8,128)(2,1)S(1)} %get-tuple-element.31), channel_id=1, source_target_pairs={{0,8},{2,10},{4,12},{6,14},{8,0},{10,2},{12,4},{14,6},{1,9},{3,11}... | collective-permute-start | bytes 307208 | tf_op jit(solution)/shard_map/ppermute | solution.py:341
  7.0 1.5 %collective-permute-start.2 = (s16[400,128]{1,0:T(8,128)(2,1)S(1)}, s16[400,128]{1,0:T(8,128)(2,1)S(1)}, u32[]{:S(2)}, u32[]{:S(2)}) collective-permute-start(s16[400,128]{1,0:T(8,128)(2,1)S(1)} %get-tuple-element.32), channel_id=1, source_target_pairs={{0,2},{2,0},{4,6},{6,4},{8,10},{10,8},{12,14},{14,12},{1,3},{3,1},... | collective-permute-start | bytes 307208 | tf_op jit(solution)/shard_map/ppermute | solution.py:341
  8.5 0.0 collective-permute-start.4
  8.5 1.8 %collective-permute-start.6 = (s16[400,128]{1,0:T(8,128)(2,1)S(1)}, s16[400,128]{1,0:T(8,128)(2,1)S(1)}, u32[]{:S(2)}, u32[]{:S(2)}) collective-permute-start(s16[400,128]{1,0:T(8,128)(2,1)S(1)} %get-tuple-element.34), channel_id=1, source_target_pairs={{0,4},{2,6},{4,0},{6,2},{8,12},{10,14},{12,8},{14,10},{1,5},{3,7},... | collective-permute-start | bytes 307208 | tf_op jit(solution)/shard_map/ppermute | solution.py:341
  10.3 3.4 %collective-permute-start.12 = (s16[400,128]{1,0:T(8,128)(2,1)S(1)}, s16[400,128]{1,0:T(8,128)(2,1)S(1)}, u32[]{:S(2)}, u32[]{:S(2)}) collective-permute-start(s16[400,128]{1,0:T(8,128)(2,1)S(1)} %get-tuple-element.37), channel_id=1, source_target_pairs={{0,14},{2,12},{4,10},{6,8},{8,6},{10,4},{12,2},{14,0},{1,15},{3,13... | collective-permute-start | bytes 307208 | tf_op jit(solution)/shard_map/ppermute | solution.py:341
  13.7 0.4 collective-permute-done.refs_2_
  14.1 2.6 %collective-permute-start.10 = (s16[400,128]{1,0:T(8,128)(2,1)S(1)}, s16[400,128]{1,0:T(8,128)(2,1)S(1)}, u32[]{:S(2)}, u32[]{:S(2)}) collective-permute-start(s16[400,128]{1,0:T(8,128)(2,1)S(1)} %get-tuple-element.36), channel_id=1, source_target_pairs={{0,6},{2,4},{4,2},{6,0},{8,14},{10,12},{12,10},{14,8},{1,7},{3,5},... | collective-permute-start | bytes 307208 | tf_op jit(solution)/shard_map/ppermute | solution.py:341
  16.7 0.0 collective-permute-done.2.refs_3_
  16.8 2.3 %collective-permute-start.8 = (s16[400,128]{1,0:T(8,128)(2,1)S(1)}, s16[400,128]{1,0:T(8,128)(2,1)S(1)}, u32[]{:S(2)}, u32[]{:S(2)}) collective-permute-start(s16[400,128]{1,0:T(8,128)(2,1)S(1)} %get-tuple-element.35), channel_id=1, source_target_pairs={{0,12},{2,14},{4,8},{6,10},{8,4},{10,6},{12,0},{14,2},{1,13},{3,15... | collective-permute-start | bytes 307208 | tf_op jit(solution)/shard_map/ppermute | solution.py:341
  19.1 1.5 %collective-permute-done.4.refs_4_ = s16[400,128]{1,0:T(8,128)(2,1)S(1)} collective-permute-done((s16[400,128]{1,0:T(8,128)(2,1)S(1)}, s16[400,128]{1,0:T(8,128)(2,1)S(1)}, u32[]{:S(2)}, u32[]{:S(2)}) %collective-permute-start.4) | collective-permute-done | bytes 102432 | tf_op jit(solution)/shard_map/ppermute | solution.py:341
  20.5 0.0 collective-permute-start.14
  20.5 0.0 collective-permute-done.6.refs_5_
  20.5 0.6 %score_early.1 = (s32[1,256]{1,0:T(1,128)S(1)}, bf16[256,768]{1,0:T(8,128)(2,1)S(1)}, f32[8,256]{1,0:T(8,128)S(1)}, f32[128,4]{1,0:T(8,128)S(1)}, f32[128,768]{1,0:T(8,128)S(1)}, /*index=5*/f32[1,256]{1,0:T(1,128)S(1)}) custom-call(s32[1,256]{1,0:T(1,128)S(1)} %bitcast.10, bf16[256,256]{1,0:T(8,128)(2,1)S(1)} %earlier.1.earlier_ref.refs_1_, ...), custom_call_target="tpu_custom_call" | custom-call | tf_op jit(solution)/shard_map/score_early/pallas_call | solution.py:342
  21.2 0.0 copy-start.3
  21.2 0.0 collective-permute-done.12.refs_2_
  21.2 0.5 %copy-done.3 = s32[1,256]{1,0:T(1,128)} copy-done((s32[1,256]{1,0:T(1,128)}, s32[1,256]{1,0:T(1,128)S(1)}, u32[]{:S(2)}) %copy-start.3) | copy-done | bytes 1048
  21.7 0.5 %collective-permute-start.13 = (s16[400,128]{1,0:T(8,128)(2,1)S(1)}, s16[400,128]{1,0:T(8,128)(2,1)S(1)}, u32[]{:S(2)}, u32[]{:S(2)}) collective-permute-start(s16[400,128]{1,0:T(8,128)(2,1)S(1)} %collective-permute-done.12.refs_2_), channel_id=1, source_target_pairs={{0,1},{1,0},{2,3},{3,2},{4,5},{5,4},{6,7},{7,6},{8,9},{9,8},{10,11... | collective-permute-start | bytes 307208 | tf_op jit(solution)/shard_map/ppermute | solution.py:24
  22.3 0.0 collective-permute-start.1
  22.3 0.7 %collective-permute-done.10.refs_1_ = s16[400,128]{1,0:T(8,128)(2,1)S(1)} collective-permute-done((s16[400,128]{1,0:T(8,128)(2,1)S(1)}, s16[400,128]{1,0:T(8,128)(2,1)S(1)}, u32[]{:S(2)}, u32[]{:S(2)}) %collective-permute-start.10) | collective-permute-done | bytes 102432 | tf_op jit(solution)/shard_map/ppermute | solution.py:341
  22.9 0.0 collective-permute-start.3
  22.9 1.0 %collective-permute-done.8.refs_0_ = s16[400,128]{1,0:T(8,128)(2,1)S(1)} collective-permute-done((s16[400,128]{1,0:T(8,128)(2,1)S(1)}, s16[400,128]{1,0:T(8,128)(2,1)S(1)}, u32[]{:S(2)}, u32[]{:S(2)}) %collective-permute-start.8) | collective-permute-done | bytes 102432 | tf_op jit(solution)/shard_map/ppermute | solution.py:341
  23.9 0.0 collective-permute-start.5
  23.9 0.0 collective-permute-done.14.refs_7_
  23.9 0.5 %collective-permute-start.11 = (s16[400,128]{1,0:T(8,128)(2,1)S(1)}, s16[400,128]{1,0:T(8,128)(2,1)S(1)}, u32[]{:S(2)}, u32[]{:S(2)}) collective-permute-start(s16[400,128]{1,0:T(8,128)(2,1)S(1)} %collective-permute-done.10.refs_1_), channel_id=1, source_target_pairs={{0,1},{1,0},{2,3},{3,2},{4,5},{5,4},{6,7},{7,6},{8,9},{9,8},{10,11... | collective-permute-start | bytes 307208 | tf_op jit(solution)/shard_map/ppermute | solution.py:24
  24.4 0.0 collective-permute-done.13.refs_6_
  24.4 0.1 collective-permute-start.7
  24.5 0.0 collective-permute-done.1.refs_0_
  24.5 0.4 %collective-permute-start.9 = (s16[400,128]{1,0:T(8,128)(2,1)S(1)}, s16[400,128]{1,0:T(8,128)(2,1)S(1)}, u32[]{:S(2)}, u32[]{:S(2)}) collective-permute-start(s16[400,128]{1,0:T(8,128)(2,1)S(1)} %collective-permute-done.8.refs_0_), channel_id=1, source_target_pairs={{0,1},{1,0},{2,3},{3,2},{4,5},{5,4},{6,7},{7,6},{8,9},{9,8},{10,11... | collective-permute-start | bytes 307208 | tf_op jit(solution)/shard_map/ppermute | solution.py:24
  25.0 0.8 %score_late.1 = (bf16[512,768]{1,0:T(8,128)(2,1)S(1)}, f32[8,512]{1,0:T(8,128)S(1)}, f32[128,768]{1,0:T(8,128)S(1)}, f32[1,512]{1,0:T(1,128)S(1)}) custom-call(s16[400,128]{1,0:T(8,128)(2,1)S(1)} %collective-permute-done.8.refs_0_, s16[400,128]{1,0:T(8,128)(2,1)S(1)} %collective-permute-done.10.refs_1_, s16[400,128]{1,0:T(8,128)(2,1)S(1)} %collective-permute-done.12.refs_2_, ...), custom_call_target="tpu_custom_call" | custom-call | tf_op jit(solution)/shard_map/score_late/pallas_call | solution.py:361
  25.8 0.0 collective-permute-done.11.refs_5_
  25.8 0.0 collective-permute-done.3.refs_1_
  25.8 0.0 collective-permute-done.5.refs_2_
  25.8 0.0 collective-permute-done.7.refs_3_
  25.9 0.1 collective-permute-done.9.refs_4_
  25.9 2.2 %score_last.1 = (f32[128,768]{1,0:T(8,128)}, f32[8,128]{1,0:T(8,128)S(1)}) custom-call(s16[400,128]{1,0:T(8,128)(2,1)S(1)} %collective-permute-done.1.refs_0_, s16[400,128]{1,0:T(8,128)(2,1)S(1)} %collective-permute-done.3.refs_1_, s16[400,128]{1,0:T(8,128)(2,1)S(1)} %collective-permute-done.5.refs_2_, s16[400,128]{1,0:T(8,128)(2,1)S(1)} %collective-permute-done.7.refs_3_, ...), custom_call_target="tpu_custom_call" | custom-call | tf_op jit(solution)/shard_map/score_last/pallas_call | solution.py:375
  28.2 12.5 %all_to_all.11 = f32[8,1,128]{2,1,0:T(1,128)} all-to-all(f32[8,1,128]{2,1,0:T(1,128)S(1)} %bitcast.11), channel_id=1, replica_groups=mesh['groups'=2,'rows'=4,'feat'=2,'sub'=2] {'rows','feat'}, dimensions={0} | all-to-all | bytes 8192 | tf_op jit(solution)/shard_map/all_to_all | solution.py:384
  40.7 1.3 %pick.1 = (f32[1,256]{1,0:T(1,128)}, f32[1,256]{1,0:T(1,128)}) custom-call(f32[8,128]{1,0:T(8,128)} %bitcast.13, s32[1,256]{1,0:T(1,128)} %bitcast.8, s32[1,256]{1,0:T(1,128)} %copy-done.3), custom_call_target="tpu_custom_call" | custom-call | tf_op jit(solution)/shard_map/pick/pallas_call | solution.py:385
  (1 shorter events, 0.0 us)
Async XLA Ops:
  0.6 1.1 %copy-start = (f32[256,768]{1,0:T(8,128)S(1)}, f32[256,768]{1,0:T(8,128)}, u32[]{:S(2)}) copy-start(f32[256,768]{1,0:T(8,128)} %emb_ref.1) | copy-start | bytes 2359300
  0.6 1.1 %copy-start.2 = (s32[256]{0:T(256)S(1)}, s32[256]{0:T(256)}, u32[]{:S(2)}) copy-start(s32[256]{0:T(256)} %param.5) | copy-start | bytes 3076
  0.7 1.1 %copy-start.1 = (s32[256]{0:T(256)S(1)}, s32[256]{0:T(256)}, u32[]{:S(2)}) copy-start(s32[256]{0:T(256)} %param.4) | copy-start | bytes 3076
  2.9 11.2 %collective-permute-start = (s16[400,128]{1,0:T(8,128)(2,1)S(1)}, s16[400,128]{1,0:T(8,128)(2,1)S(1)}, u32[]{:S(2)}, u32[]{:S(2)}) collective-permute-start(s16[400,128]{1,0:T(8,128)(2,1)S(1)} %get-tuple-element.31), channel_id=1, source_target_pairs={{0,8},{2,10},{4,12},{6,14},{8,0},{10,2},{12,4},{14,6},{1,9},{3,11}... | collective-permute-start | bytes 307208 | tf_op jit(solution)/shard_map/ppermute | solution.py:341
  7.0 9.8 %collective-permute-start.2 = (s16[400,128]{1,0:T(8,128)(2,1)S(1)}, s16[400,128]{1,0:T(8,128)(2,1)S(1)}, u32[]{:S(2)}, u32[]{:S(2)}) collective-permute-start(s16[400,128]{1,0:T(8,128)(2,1)S(1)} %get-tuple-element.32), channel_id=1, source_target_pairs={{0,2},{2,0},{4,6},{6,4},{8,10},{10,8},{12,14},{14,12},{1,3},{3,1},... | collective-permute-start | bytes 307208 | tf_op jit(solution)/shard_map/ppermute | solution.py:341
  8.5 12.1 %collective-permute-start.4 = (s16[400,128]{1,0:T(8,128)(2,1)S(1)}, s16[400,128]{1,0:T(8,128)(2,1)S(1)}, u32[]{:S(2)}, u32[]{:S(2)}) collective-permute-start(s16[400,128]{1,0:T(8,128)(2,1)S(1)} %get-tuple-element.33), channel_id=1, source_target_pairs={{0,10},{2,8},{4,14},{6,12},{8,2},{10,0},{12,6},{14,4},{1,11},{3,9}... | collective-permute-start | bytes 307208 | tf_op jit(solution)/shard_map/ppermute | solution.py:341
  8.5 12.0 %collective-permute-start.6 = (s16[400,128]{1,0:T(8,128)(2,1)S(1)}, s16[400,128]{1,0:T(8,128)(2,1)S(1)}, u32[]{:S(2)}, u32[]{:S(2)}) collective-permute-start(s16[400,128]{1,0:T(8,128)(2,1)S(1)} %get-tuple-element.34), channel_id=1, source_target_pairs={{0,4},{2,6},{4,0},{6,2},{8,12},{10,14},{12,8},{14,10},{1,5},{3,7},... | collective-permute-start | bytes 307208 | tf_op jit(solution)/shard_map/ppermute | solution.py:341
  10.3 10.9 %collective-permute-start.12 = (s16[400,128]{1,0:T(8,128)(2,1)S(1)}, s16[400,128]{1,0:T(8,128)(2,1)S(1)}, u32[]{:S(2)}, u32[]{:S(2)}) collective-permute-start(s16[400,128]{1,0:T(8,128)(2,1)S(1)} %get-tuple-element.37), channel_id=1, source_target_pairs={{0,14},{2,12},{4,10},{6,8},{8,6},{10,4},{12,2},{14,0},{1,15},{3,13... | collective-permute-start | bytes 307208 | tf_op jit(solution)/shard_map/ppermute | solution.py:341
  14.1 8.8 %collective-permute-start.10 = (s16[400,128]{1,0:T(8,128)(2,1)S(1)}, s16[400,128]{1,0:T(8,128)(2,1)S(1)}, u32[]{:S(2)}, u32[]{:S(2)}) collective-permute-start(s16[400,128]{1,0:T(8,128)(2,1)S(1)} %get-tuple-element.36), channel_id=1, source_target_pairs={{0,6},{2,4},{4,2},{6,0},{8,14},{10,12},{12,10},{14,8},{1,7},{3,5},... | collective-permute-start | bytes 307208 | tf_op jit(solution)/shard_map/ppermute | solution.py:341
  16.8 7.2 %collective-permute-start.8 = (s16[400,128]{1,0:T(8,128)(2,1)S(1)}, s16[400,128]{1,0:T(8,128)(2,1)S(1)}, u32[]{:S(2)}, u32[]{:S(2)}) collective-permute-start(s16[400,128]{1,0:T(8,128)(2,1)S(1)} %get-tuple-element.35), channel_id=1, source_target_pairs={{0,12},{2,14},{4,8},{6,10},{8,4},{10,6},{12,0},{14,2},{1,13},{3,15... | collective-permute-start | bytes 307208 | tf_op jit(solution)/shard_map/ppermute | solution.py:341
  20.5 3.4 %collective-permute-start.14 = (s16[400,128]{1,0:T(8,128)(2,1)S(1)}, s16[400,128]{1,0:T(8,128)(2,1)S(1)}, u32[]{:S(2)}, u32[]{:S(2)}) collective-permute-start(s16[400,128]{1,0:T(8,128)(2,1)S(1)} %get-tuple-element.44.refs_3_), channel_id=1, source_target_pairs={{0,1},{1,0},{2,3},{3,2},{4,5},{5,4},{6,7},{7,6},{8,9},{9,8},{10,11... | collective-permute-start | bytes 307208 | tf_op jit(solution)/shard_map/ppermute | solution.py:24
  21.2 0.5 %copy-start.3 = (s32[1,256]{1,0:T(1,128)}, s32[1,256]{1,0:T(1,128)S(1)}, u32[]{:S(2)}) copy-start(s32[1,256]{1,0:T(1,128)S(1)} %get-tuple-element.55.slot_ref) | copy-start | bytes 3076
  21.7 2.7 %collective-permute-start.13 = (s16[400,128]{1,0:T(8,128)(2,1)S(1)}, s16[400,128]{1,0:T(8,128)(2,1)S(1)}, u32[]{:S(2)}, u32[]{:S(2)}) collective-permute-start(s16[400,128]{1,0:T(8,128)(2,1)S(1)} %collective-permute-done.12.refs_2_), channel_id=1, source_target_pairs={{0,1},{1,0},{2,3},{3,2},{4,5},{5,4},{6,7},{7,6},{8,9},{9,8},{10,11... | collective-permute-start | bytes 307208 | tf_op jit(solution)/shard_map/ppermute | solution.py:24
  22.3 2.3 %collective-permute-start.1 = (s16[400,128]{1,0:T(8,128)(2,1)S(1)}, s16[400,128]{1,0:T(8,128)(2,1)S(1)}, u32[]{:S(2)}, u32[]{:S(2)}) collective-permute-start(s16[400,128]{1,0:T(8,128)(2,1)S(1)} %collective-permute-done.refs_2_), channel_id=1, source_target_pairs={{0,1},{1,0},{2,3},{3,2},{4,5},{5,4},{6,7},{7,6},{8,9},{9,8},{10,11... | collective-permute-start | bytes 307208 | tf_op jit(solution)/shard_map/ppermute | solution.py:24
  22.9 2.9 %collective-permute-start.3 = (s16[400,128]{1,0:T(8,128)(2,1)S(1)}, s16[400,128]{1,0:T(8,128)(2,1)S(1)}, u32[]{:S(2)}, u32[]{:S(2)}) collective-permute-start(s16[400,128]{1,0:T(8,128)(2,1)S(1)} %collective-permute-done.2.refs_3_), channel_id=1, source_target_pairs={{0,1},{1,0},{2,3},{3,2},{4,5},{5,4},{6,7},{7,6},{8,9},{9,8},{10,11... | collective-permute-start | bytes 307208 | tf_op jit(solution)/shard_map/ppermute | solution.py:24
  23.9 1.9 %collective-permute-start.5 = (s16[400,128]{1,0:T(8,128)(2,1)S(1)}, s16[400,128]{1,0:T(8,128)(2,1)S(1)}, u32[]{:S(2)}, u32[]{:S(2)}) collective-permute-start(s16[400,128]{1,0:T(8,128)(2,1)S(1)} %collective-permute-done.4.refs_4_), channel_id=1, source_target_pairs={{0,1},{1,0},{2,3},{3,2},{4,5},{5,4},{6,7},{7,6},{8,9},{9,8},{10,11... | collective-permute-start | bytes 307208 | tf_op jit(solution)/shard_map/ppermute | solution.py:24
  23.9 1.9 %collective-permute-start.11 = (s16[400,128]{1,0:T(8,128)(2,1)S(1)}, s16[400,128]{1,0:T(8,128)(2,1)S(1)}, u32[]{:S(2)}, u32[]{:S(2)}) collective-permute-start(s16[400,128]{1,0:T(8,128)(2,1)S(1)} %collective-permute-done.10.refs_1_), channel_id=1, source_target_pairs={{0,1},{1,0},{2,3},{3,2},{4,5},{5,4},{6,7},{7,6},{8,9},{9,8},{10,11... | collective-permute-start | bytes 307208 | tf_op jit(solution)/shard_map/ppermute | solution.py:24
  24.4 1.4 %collective-permute-start.7 = (s16[400,128]{1,0:T(8,128)(2,1)S(1)}, s16[400,128]{1,0:T(8,128)(2,1)S(1)}, u32[]{:S(2)}, u32[]{:S(2)}) collective-permute-start(s16[400,128]{1,0:T(8,128)(2,1)S(1)} %collective-permute-done.6.refs_5_), channel_id=1, source_target_pairs={{0,1},{1,0},{2,3},{3,2},{4,5},{5,4},{6,7},{7,6},{8,9},{9,8},{10,11... | collective-permute-start | bytes 307208 | tf_op jit(solution)/shard_map/ppermute | solution.py:24
  24.5 1.4 %collective-permute-start.9 = (s16[400,128]{1,0:T(8,128)(2,1)S(1)}, s16[400,128]{1,0:T(8,128)(2,1)S(1)}, u32[]{:S(2)}, u32[]{:S(2)}) collective-permute-start(s16[400,128]{1,0:T(8,128)(2,1)S(1)} %collective-permute-done.8.refs_0_), channel_id=1, source_target_pairs={{0,1},{1,0},{2,3},{3,2},{4,5},{5,4},{6,7},{7,6},{8,9},{9,8},{10,11... | collective-permute-start | bytes 307208 | tf_op jit(solution)/shard_map/ppermute | solution.py:24

commit v4 on v3

--- a/solution.py
+++ b/solution.py
@@ -14,10 +14,13 @@
 LANES = 128
 META = 16
 FULL = 32768.0
+GROUP = 128
 STEPS = (32, 16, 8, 4, 2, 1)
 CODE = 65536.0
 NONE = -1e30
-FIRST = (4, 1, 5, 2, 6, 3, 7, 0)
+FIRST = (6, 1, 5, 2, 7, 3, 4, 0)
+HELD = 6
+EARLY = 4
 
 
 def swapped(shard, axis, distance):
@@ -144,15 +147,15 @@
     slot = slots_of(owners, capacity, per_owner, asg, earlier_ref[...])
     place = (iota((slots, rows), 0) == slot).astype(jnp.bfloat16)
     x = emb_ref[...]
-    unit = x * lax.rsqrt(jnp.sum(x * x, axis=1, keepdims=True) + EPSILON)
-    top = jnp.max(jnp.abs(unit), axis=1, keepdims=True)
+    norm = lax.rsqrt(jnp.sum(x * x, axis=1, keepdims=True) + EPSILON)
+    top = jnp.max(jnp.abs(x), axis=1, keepdims=True) * norm
     scale = jnp.ones_like(top)
     power = jnp.zeros_like(top)
     for step in STEPS:
         small = top * (scale * 2.0**step) < 1.0
         scale = jnp.where(small, scale * 2.0**step, scale)
         power = jnp.where(small, power + step, power)
-    coded = jnp.minimum(jnp.round(unit * (scale * FULL)), FULL - 1.0)
+    coded = jnp.minimum(jnp.round(x * (norm * (scale * FULL))), FULL - 1.0)
     high, low = halves(coded)
     power_row = jnp.transpose(jnp.broadcast_to(power, (rows, LANES)))[:1, :]
     facts = jnp.concatenate(
@@ -218,9 +221,16 @@
 
 
 def part_sums(facts, per_owner, high_ref, low_ref):
-    own = iota((per_owner, facts.shape[1]), 0).astype(jnp.float32) == facts[0:1, :]
-    member = jnp.where(own, facts[2:3, :], 0.0).astype(jnp.bfloat16)
-    return dot(member, high_ref[...]) + dot(member, low_ref[...])
+    count = facts.shape[1]
+    step = min(count, GROUP)
+    total = None
+    for first in range(0, count, step):
+        here = slice(first, first + step)
+        own = iota((per_owner, step), 0).astype(jnp.float32) == facts[0:1, here]
+        member = jnp.where(own, facts[2:3, here], 0.0).astype(jnp.bfloat16)
+        part = dot(member, high_ref[here, :]) + dot(member, low_ref[here, :])
+        total = part if total is None else total + part
+    return total
 
 
 def best_of(scores, cols, facts):
@@ -237,8 +247,8 @@
 
 
 def early_kernel(owners, capacity, per_owner, width, *refs):
-    asg_ref, earlier_ref, *chunks = refs[: owners // 2 + 2]
-    slot_ref, high_ref, facts_ref, cols_ref, sums_ref, best_ref, low_ref = refs[owners // 2 + 2 :]
+    asg_ref, earlier_ref, *chunks = refs[: EARLY + 2]
+    slot_ref, high_ref, facts_ref, cols_ref, sums_ref, best_ref, low_ref = refs[EARLY + 2 :]
     slot_ref[...] = slots_of(owners, capacity, per_owner, asg_ref[...], earlier_ref[...])
     facts, cols = digest(chunks, capacity, width, high_ref, low_ref)
     facts_ref[...] = facts
@@ -248,24 +258,25 @@
 
 
 def late_kernel(owners, capacity, per_owner, width, *refs):
-    half = owners // 2
-    chunks = refs[:half]
-    old_ref, old_facts_ref, old_cols_ref, old_sums_ref, old_best_ref = refs[half : half + 5]
-    high_ref, facts_ref, sums_ref, best_ref, low_ref = refs[half + 5 :]
-    count = half * capacity
-    new_ref = high_ref.at[count:, :]
+    count = owners - EARLY
+    chunks = refs[:count]
+    old_ref, old_facts_ref, old_cols_ref, old_sums_ref, old_best_ref = refs[count : count + 5]
+    high_ref, facts_ref, sums_ref, best_ref, low_ref = refs[count + 5 :]
+    old_rows = EARLY * capacity
+    new_ref = high_ref.at[old_rows:, :]
     facts, cols = digest(chunks, capacity, width, new_ref, low_ref)
-    high_ref[:count, :] = old_ref[...]
+    high_ref[:old_rows, :] = old_ref[...]
     old_facts = old_facts_ref[...]
-    facts_ref[:, :count] = old_facts
-    facts_ref[:, count:] = facts
+    facts_ref[:, :old_rows] = old_facts
+    facts_ref[:, old_rows:] = facts
     sums_ref[...] = old_sums_ref[...] + part_sums(facts, per_owner, new_ref, low_ref)
-    scores = dot_t(high_ref[...], new_ref[...])
-    best_ref[:, count:] = jnp.maximum(
-        best_of(scores[:count, :], old_cols_ref[...], facts), best_of(scores[count:, :], cols, facts)
-    )
-    best_ref[:, :count] = jnp.maximum(
-        old_best_ref[...], best_of(dot_t(new_ref[...], old_ref[...]), cols, old_facts)
+    new = new_ref[...]
+    best_ref[:, old_rows:] = jnp.maximum(
+        best_of(dot_t(old_ref[...], new), old_cols_ref[...], facts),
+        best_of(dot_t(new, new), cols, facts),
+    )
+    best_ref[:, :old_rows] = jnp.maximum(
+        old_best_ref[...], best_of(dot_t(new, old_ref[...]), cols, old_facts)
     )
 
 
@@ -292,22 +303,9 @@
         back_ref[pl.ds(me ^ v, 1), :] = jnp.concatenate([best[:, part], near[:, part]], axis=1)
 
 
-def pick_kernel(owners, capacity, per_owner, back_ref, asg_ref, slot_ref, best_ref, near_ref):
-    rows = asg_ref.shape[1]
-    back = back_ref[...]
-    for first in range(0, rows, LANES):
-        here = slice(first, first + LANES)
-        hits = iota((owners, LANES), 0) == lax.div(asg_ref[:, here], jnp.int32(per_owner))
-        pos = jnp.broadcast_to(lax.rem(slot_ref[:, here], jnp.int32(capacity)), (owners, LANES))
-        for start, ref in ((0, best_ref), (capacity, near_ref)):
-            found = jnp.take_along_axis(back, pos + start, axis=1, mode="promise_in_bounds")
-            ref[:, here] = jnp.sum(jnp.where(hits, found, 0.0), axis=0, keepdims=True)
-
-
 def exchange_pairs(embeddings, assign, order):
     owners = lax.axis_size("rows") * lax.axis_size("feat")
     rows, width = embeddings.shape
-    half = owners // 2
     capacity = 2 * rows // owners
     per_owner = K // owners
     slots = owners * capacity
@@ -339,23 +337,24 @@
     got = [packs[0]] + [None] * (owners - 1)
     for v in range(1, owners):
         got[v] = lax.ppermute(packs[v], ("rows", "feat"), [(i, i ^ v) for i in range(owners)])
+    begun = EARLY * capacity
     slot, *near = pl.pallas_call(
         functools.partial(early_kernel, owners, capacity, per_owner, width),
         out_shape=[
             full(1, rows, dtype=jnp.int32),
-            full(slots // 2, width, dtype=jnp.bfloat16),
-            full(8, slots // 2),
-            full(LANES, slots // LANES),
+            full(begun, width, dtype=jnp.bfloat16),
+            full(8, begun),
+            full(LANES, 2 * begun // LANES),
             full(per_owner, width),
-            full(1, slots // 2),
+            full(1, begun),
         ],
-        in_specs=[vmem] * (half + 2),
+        in_specs=[vmem] * (EARLY + 2),
         out_specs=[vmem] * 6,
-        scratch_shapes=[pltpu.VMEM((slots // 2, width), jnp.bfloat16)],
+        scratch_shapes=[pltpu.VMEM((begun, width), jnp.bfloat16)],
         compiler_params=params,
         name="score_early",
-    )(assign, earlier, *[got[v] for v in FIRST[:half]])
-    last = FIRST[-2]
+    )(assign, earlier, *[got[v] for v in FIRST[:EARLY]])
+    last = FIRST[HELD]
     held, near = lax.optimization_barrier((got[last], near))
     other = [swapped(held if v == last else got[v], "sub", 0) for v in range(owners)]
     asked = pl.pallas_call(
@@ -366,12 +365,12 @@
             full(per_owner, width),
             full(1, slots),
         ],
-        in_specs=[vmem] * (half + 5),
+        in_specs=[vmem] * (owners - EARLY + 5),
         out_specs=[vmem] * 4,
-        scratch_shapes=[pltpu.VMEM((slots // 2, width), jnp.bfloat16)],
+        scratch_shapes=[pltpu.VMEM((slots - begun, width), jnp.bfloat16)],
         compiler_params=params,
         name="score_late",
-    )(*[got[v] for v in FIRST[half:]], *near)
+    )(*[got[v] for v in FIRST[EARLY:]], *near)
     cent, back = pl.pallas_call(
         functools.partial(last_kernel, owners, capacity, per_owner, width),
         out_shape=[full(per_owner, width), full(owners, LANES)],
@@ -382,13 +381,14 @@
         name="score_last",
     )(*[other[v] for v in FIRST], *asked)
     back = lax.all_to_all(back, ("rows", "feat"), split_axis=0, concat_axis=0, tiled=True)
-    best, near = pl.pallas_call(
-        functools.partial(pick_kernel, owners, capacity, per_owner),
-        out_shape=[full(1, rows)] * 2,
-        in_specs=[vmem] * 3,
-        out_specs=[vmem] * 2,
-        name="pick",
-    )(back, assign, slot)
+    slot = slot.reshape(rows)
+    pos = lax.rem(slot, jnp.int32(capacity))
+    target = lax.div(assign.reshape(rows), jnp.int32(per_owner))
+    hits = (target[None, :, None] == jnp.arange(owners, dtype=jnp.int32)[:, None, None]) & (
+        pos[None, :, None] == jnp.arange(capacity, dtype=jnp.int32)[None, None, :]
+    )
+    best = jnp.sum(jnp.where(hits, back[:, None, :capacity], 0.0), axis=(0, 2))
+    near = jnp.sum(jnp.where(hits, back[:, None, capacity:], 0.0), axis=(0, 2))
     return best.reshape(rows), near.reshape(rows), cent
 
 

time: 42.2 us -> 40.8 us (0.967)
  blocking collectives: 12.5 us -> 0 us
  waiting for transfers between devices: 3.59 us -> 12.2 us
  starting transfers between devices: 17.4 us -> 21 us
  Pallas kernels: 6.18 us -> 4.71 us
  other arithmetic: 0 us -> 0.82 us
  local copies, waits for them, and re-layouts: 1.61 us -> 1.16 us
    all_to_all x1 -> x0, blocking collectives: 12.5 us -> none  [exchange_pairs(): lax.all_to_all(back, ('rows', 'feat'), split_axis=0, concat_axis=0, tiled...]
    all_to_all x0 -> x1, waiting for transfers between devices: none -> 6.44 us  [exchange_pairs(): lax.all_to_all(back, ('rows', 'feat'), split_axis=0, concat_axis=0, tiled...]
    all_to_all x0 -> x1, starting transfers between devices: none -> 4.19 us  [exchange_pairs(): lax.all_to_all(back, ('rows', 'feat'), split_axis=0, concat_axis=0, tiled...]
    ppermute x7, waiting for transfers between devices: 3.51 us -> 5.66 us  [exchange_pairs(): lax.ppermute(packs[v], ('rows', 'feat'), [(i, i ^ v) for i in range(owner...]
    pallas_call x1 -> x0, Pallas kernels: 1.34 us -> none  [exchange_pairs(): pl.pallas_call(functools.partial(pick_kernel, owners, capacity, per_owner...]
    reduce_sum x0 -> x1, other arithmetic: none -> 0.78 us  [exchange_pairs(): near = jnp.sum(jnp.where(hits, back[:, None, capacity:], 0.0), axis=(0, 2))]
    ppermute x7, starting transfers between devices: 15.8 us -> 15.2 us  [exchange_pairs(): lax.ppermute(packs[v], ('rows', 'feat'), [(i, i ^ v) for i in range(owner...]
    unnamed x8 -> x6, local copies, waits for them, and re-layouts: 1.61 us -> 1.08 us
  transfers between devices with their start and end apart: 15 -> 16, of which waited for: 5 -> 5; matrix products, arithmetic and copies ran while one was open for 0% -> 0% of each run, Pallas kernels for 4% -> 4%
where the time goes in v4:
time: 40.8 us; the launch traced here: 40.6 us
  starting transfers between devices  21 us (51%)
  waiting for transfers between devices  12.2 us (30%)
  Pallas kernels  4.71 us (12%)
  local copies, waits for them, and re-layouts  1.16 us (3%)
  other arithmetic  0.82 us (2%)
  between operations  0.73 us (2%)
    ppermute x7, starting transfers between devices, exchange_pairs(): lax.ppermute(packs[v], ('rows', 'feat'), [(i, i ^ v) for i in range(owner...  15.2 us
    all_to_all x1, waiting for transfers between devices, exchange_pairs(): lax.all_to_all(back, ('rows', 'feat'), split_axis=0, concat_axis=0, tiled...  6.44 us
    ppermute x7, waiting for transfers between devices, exchange_pairs(): lax.ppermute(packs[v], ('rows', 'feat'), [(i, i ^ v) for i in range(owner...  5.66 us
    all_to_all x1, starting transfers between devices, exchange_pairs(): lax.all_to_all(back, ('rows', 'feat'), split_axis=0, concat_axis=0, tiled...  4.19 us
    pallas_call x1, Pallas kernels, exchange_pairs(): pl.pallas_call(functools.partial(last_kernel, owners, capacity, per_owner...  2.16 us
    ppermute x8, starting transfers between devices, swapped(): lax.ppermute(shard, axis, [(i, i ^ 1 << distance) for i in range(lax.axis...  1.6 us
    unnamed x6, local copies, waits for them, and re-layouts  1.08 us
    pallas_call x1, Pallas kernels, exchange_pairs(): pl.pallas_call(functools.partial(pack_kernel, owners, capacity, per_owner...  1.01 us
  transfers between devices with their start and end apart: 16, of which 5 were waited for; matrix products, arithmetic and copies ran while one was open for 0% of the time, Pallas kernels for 4%

profile of v4, /device:TPU:0, one launch (start us, length us, event | category | flops | bytes accessed | tf_op | source)
XLA Modules:
  0.0 40.6 jit_solution(646578433934758640)
XLA Ops:
  0.6 0.0 copy-start
  0.6 0.0 copy-start.2
  0.7 0.0 copy-start.1
  0.7 1.1 %copy-done = f32[256,768]{1,0:T(8,128)S(1)} copy-done((f32[256,768]{1,0:T(8,128)S(1)}, f32[256,768]{1,0:T(8,128)}, u32[]{:S(2)}) %copy-start) | copy-done | bytes 786456
  1.8 0.0 copy-done.2
  1.8 0.0 copy-done.1
  1.8 1.0 %pack.1 = (s16[400,128]{1,0:T(8,128)(2,1)S(1)}, s16[400,128]{1,0:T(8,128)(2,1)S(1)}, s16[400,128]{1,0:T(8,128)(2,1)S(1)}, s16[400,128]{1,0:T(8,128)(2,1)S(1)}, s...) custom-call(f32[256,768]{1,0:T(8,128)S(1)} %copy-done, ...), custom_call_target="tpu_custom_call" | custom-call | tf_op jit(solution)/shard_map/pack/pallas_call | solution.py:329
  2.8 5.1 %collective-permute-start = (s16[400,128]{1,0:T(8,128)(2,1)S(1)}, s16[400,128]{1,0:T(8,128)(2,1)S(1)}, u32[]{:S(2)}, u32[]{:S(2)}) collective-permute-start(s16[400,128]{1,0:T(8,128)(2,1)S(1)} %get-tuple-element.29), channel_id=1, source_target_pairs={{0,12},{2,14},{4,8},{6,10},{8,4},{10,6},{12,0},{14,2},{1,13},{3,15... | collective-permute-start | bytes 307208 | tf_op jit(solution)/shard_map/ppermute | solution.py:339
  7.9 1.5 %collective-permute-start.1 = (s16[400,128]{1,0:T(8,128)(2,1)S(1)}, s16[400,128]{1,0:T(8,128)(2,1)S(1)}, u32[]{:S(2)}, u32[]{:S(2)}) collective-permute-start(s16[400,128]{1,0:T(8,128)(2,1)S(1)} %get-tuple-element.30), channel_id=1, source_target_pairs={{0,2},{2,0},{4,6},{6,4},{8,10},{10,8},{12,14},{14,12},{1,3},{3,1},... | collective-permute-start | bytes 307208 | tf_op jit(solution)/shard_map/ppermute | solution.py:339
  9.4 0.0 collective-permute-start.2
  9.4 0.6 %collective-permute-start.3 = (s16[400,128]{1,0:T(8,128)(2,1)S(1)}, s16[400,128]{1,0:T(8,128)(2,1)S(1)}, u32[]{:S(2)}, u32[]{:S(2)}) collective-permute-start(s16[400,128]{1,0:T(8,128)(2,1)S(1)} %get-tuple-element.32), channel_id=1, source_target_pairs={{0,4},{2,6},{4,0},{6,2},{8,12},{10,14},{12,8},{14,10},{1,5},{3,7},... | collective-permute-start | bytes 307208 | tf_op jit(solution)/shard_map/ppermute | solution.py:339
  10.0 2.3 %collective-permute-start.12 = (s16[400,128]{1,0:T(8,128)(2,1)S(1)}, s16[400,128]{1,0:T(8,128)(2,1)S(1)}, u32[]{:S(2)}, u32[]{:S(2)}) collective-permute-start(s16[400,128]{1,0:T(8,128)(2,1)S(1)} %get-tuple-element.36), channel_id=1, source_target_pairs={{0,8},{2,10},{4,12},{6,14},{8,0},{10,2},{12,4},{14,6},{1,9},{3,11}... | collective-permute-start | bytes 307208 | tf_op jit(solution)/shard_map/ppermute | solution.py:339
  12.3 0.0 collective-permute-done.refs_2_
  12.3 5.1 %collective-permute-start.10 = (s16[400,128]{1,0:T(8,128)(2,1)S(1)}, s16[400,128]{1,0:T(8,128)(2,1)S(1)}, u32[]{:S(2)}, u32[]{:S(2)}) collective-permute-start(s16[400,128]{1,0:T(8,128)(2,1)S(1)} %get-tuple-element.35), channel_id=1, source_target_pairs={{0,6},{2,4},{4,2},{6,0},{8,14},{10,12},{12,10},{14,8},{1,7},{3,5},... | collective-permute-start | bytes 307208 | tf_op jit(solution)/shard_map/ppermute | solution.py:339
  17.4 0.0 collective-permute-done.1.refs_3_
  17.4 0.6 %collective-permute-start.8 = (s16[400,128]{1,0:T(8,128)(2,1)S(1)}, s16[400,128]{1,0:T(8,128)(2,1)S(1)}, u32[]{:S(2)}, u32[]{:S(2)}) collective-permute-start(s16[400,128]{1,0:T(8,128)(2,1)S(1)} %get-tuple-element.34), channel_id=1, source_target_pairs={{0,14},{2,12},{4,10},{6,8},{8,6},{10,4},{12,2},{14,0},{1,15},{3,13... | collective-permute-start | bytes 307208 | tf_op jit(solution)/shard_map/ppermute | solution.py:339
  18.0 3.2 %collective-permute-done.2.refs_4_ = s16[400,128]{1,0:T(8,128)(2,1)S(1)} collective-permute-done((s16[400,128]{1,0:T(8,128)(2,1)S(1)}, s16[400,128]{1,0:T(8,128)(2,1)S(1)}, u32[]{:S(2)}, u32[]{:S(2)}) %collective-permute-start.2) | collective-permute-done | bytes 102432 | tf_op jit(solution)/shard_map/ppermute | solution.py:339
  21.2 0.0 collective-permute-start.14
  21.2 0.0 collective-permute-done.3.refs_5_
  21.2 0.6 %score_early.1 = (s32[1,256]{1,0:T(1,128)S(1)}, bf16[256,768]{1,0:T(8,128)(2,1)S(1)}, f32[8,256]{1,0:T(8,128)S(1)}, f32[128,4]{1,0:T(8,128)S(1)}, f32[128,768]{1,0:T(8,128)S(1)}, /*index=5*/f32[1,256]{1,0:T(1,128)S(1)}) custom-call(s32[1,256]{1,0:T(1,128)S(1)} %bitcast.8, bf16[256,256]{1,0:T(8,128)(2,1)S(1)} %earlier.1.earlier_ref.refs_1_, ...), custom_call_target="tpu_custom_call" | custom-call | tf_op jit(solution)/shard_map/score_early/pallas_call | solution.py:341
  21.9 2.2 %collective-permute-done.12.refs_2_ = s16[400,128]{1,0:T(8,128)(2,1)S(1)} collective-permute-done((s16[400,128]{1,0:T(8,128)(2,1)S(1)}, s16[400,128]{1,0:T(8,128)(2,1)S(1)}, u32[]{:S(2)}, u32[]{:S(2)}) %collective-permute-start.12) | collective-permute-done | bytes 102432 | tf_op jit(solution)/shard_map/ppermute | solution.py:339
  24.1 0.0 collective-permute-start.13
  24.1 0.0 collective-permute-done.10.refs_1_
  24.1 0.5 %collective-permute-start.11 = (s16[400,128]{1,0:T(8,128)(2,1)S(1)}, s16[400,128]{1,0:T(8,128)(2,1)S(1)}, u32[]{:S(2)}, u32[]{:S(2)}) collective-permute-start(s16[400,128]{1,0:T(8,128)(2,1)S(1)} %collective-permute-done.10.refs_1_), channel_id=1, source_target_pairs={{0,1},{1,0},{2,3},{3,2},{4,5},{5,4},{6,7},{7,6},{8,9},{9,8},{10,11... | collective-permute-start | bytes 307208 | tf_op jit(solution)/shard_map/ppermute | solution.py:27
  24.6 0.1 collective-permute-start.4
  24.7 0.3 collective-permute-done.8.refs_0_
  24.9 0.2 collective-permute-start.5
  25.1 0.0 collective-permute-done.14.refs_7_
  25.1 0.3 collective-permute-start.6
  25.4 0.0 collective-permute-done.13.refs_6_
  25.4 0.2 collective-permute-start.7
  25.6 0.0 collective-permute-done.11.refs_5_
  25.6 0.3 collective-permute-start.9
  26.0 0.9 %score_late.1 = (bf16[512,768]{1,0:T(8,128)(2,1)S(1)}, f32[8,512]{1,0:T(8,128)S(1)}, f32[128,768]{1,0:T(8,128)S(1)}, f32[1,512]{1,0:T(1,128)S(1)}) custom-call(s16[400,128]{1,0:T(8,128)(2,1)S(1)} %collective-permute-done.8.refs_0_, s16[400,128]{1,0:T(8,128)(2,1)S(1)} %collective-permute-done.10.refs_1_, s16[400,128]{1,0:T(8,128)(2,1)S(1)} %collective-permute-done.12.refs_2_, ...), custom_call_target="tpu_custom_call" | custom-call | tf_op jit(solution)/shard_map/score_late/pallas_call | solution.py:360
  26.8 0.0 collective-permute-done.4.refs_0_
  26.8 0.0 collective-permute-done.5.refs_1_
  26.8 0.0 collective-permute-done.6.refs_2_
  26.9 0.0 collective-permute-done.7.refs_3_
  26.9 0.1 collective-permute-done.9.refs_4_
  26.9 2.2 %score_last.1 = (f32[128,768]{1,0:T(8,128)}, f32[8,128]{1,0:T(8,128)}) custom-call(s16[400,128]{1,0:T(8,128)(2,1)S(1)} %collective-permute-done.4.refs_0_, s16[400,128]{1,0:T(8,128)(2,1)S(1)} %collective-permute-done.5.refs_1_, s16[400,128]{1,0:T(8,128)(2,1)S(1)} %collective-permute-done.6.refs_2_, s16[400,128]{1,0:T(8,128)(2,1)S(1)} %collective-permute-done.7.refs_3_, ...), custom_call_target="tpu_custom_call" | custom-call | tf_op jit(solution)/shard_map/score_last/pallas_call | solution.py:374
  29.1 4.2 %all-to-all-start = ((f32[8,1,128]{2,1,0:T(1,128)}), f32[8,1,128]{2,1,0:T(1,128)S(1)}, u32[]{:S(2)}, u32[]{:S(2)}) async-start(f32[8,1,128]{2,1,0:T(1,128)} %bitcast.4), calls=%async_computation | async-start | bytes 8192 | tf_op jit(solution)/shard_map/all_to_all | solution.py:383
  33.3 6.4 %all-to-all-done = f32[8,1,128]{2,1,0:T(1,128)S(1)} async-done(((f32[8,1,128]{2,1,0:T(1,128)}), f32[8,1,128]{2,1,0:T(1,128)S(1)}, u32[]{:S(2)}, u32[]{:S(2)}) %all-to-all-start) | async-done | bytes 4128 | tf_op jit(solution)/shard_map/all_to_all | solution.py:383
  39.7 0.1 fusion.4
  39.8 0.8 %fusion.1 = (f32[256]{0:T(256)}, f32[256]{0:T(256)}) fusion(f32[8,64]{1,0:T(8,128)S(1)} %get-tuple-element.58, pred[256,64]{0,1:T(8,128)(4,1)S(1)} %iota_compare_fusion, pred[8,256]{1,0:T(8,128)(4,1)S(1)} %iota_compare_fusion.1, f32[8,64]{1,0:T(8,128)S(1)} %get-tuple-element.57), kind=kLoop, calls=%fused_computation.3 | loop fusion | flops 654848 | bytes 24576 | tf_op jit(solution)/shard_map/reduce_sum | solution.py:391
  (5 shorter events, 0.1 us)
Async XLA Ops:
  0.6 1.1 %copy-start = (f32[256,768]{1,0:T(8,128)S(1)}, f32[256,768]{1,0:T(8,128)}, u32[]{:S(2)}) copy-start(f32[256,768]{1,0:T(8,128)} %emb_ref.1) | copy-start | bytes 2359300
  0.6 1.1 %copy-start.2 = (s32[256]{0:T(256)S(1)}, s32[256]{0:T(256)}, u32[]{:S(2)}) copy-start(s32[256]{0:T(256)} %param.5) | copy-start | bytes 3076
  0.7 1.1 %copy-start.1 = (s32[256]{0:T(256)S(1)}, s32[256]{0:T(256)}, u32[]{:S(2)}) copy-start(s32[256]{0:T(256)} %param.4) | copy-start | bytes 3076
  2.8 9.5 %collective-permute-start = (s16[400,128]{1,0:T(8,128)(2,1)S(1)}, s16[400,128]{1,0:T(8,128)(2,1)S(1)}, u32[]{:S(2)}, u32[]{:S(2)}) collective-permute-start(s16[400,128]{1,0:T(8,128)(2,1)S(1)} %get-tuple-element.29), channel_id=1, source_target_pairs={{0,12},{2,14},{4,8},{6,10},{8,4},{10,6},{12,0},{14,2},{1,13},{3,15... | collective-permute-start | bytes 307208 | tf_op jit(solution)/shard_map/ppermute | solution.py:339
  7.9 9.5 %collective-permute-start.1 = (s16[400,128]{1,0:T(8,128)(2,1)S(1)}, s16[400,128]{1,0:T(8,128)(2,1)S(1)}, u32[]{:S(2)}, u32[]{:S(2)}) collective-permute-start(s16[400,128]{1,0:T(8,128)(2,1)S(1)} %get-tuple-element.30), channel_id=1, source_target_pairs={{0,2},{2,0},{4,6},{6,4},{8,10},{10,8},{12,14},{14,12},{1,3},{3,1},... | collective-permute-start | bytes 307208 | tf_op jit(solution)/shard_map/ppermute | solution.py:339
  9.4 11.8 %collective-permute-start.2 = (s16[400,128]{1,0:T(8,128)(2,1)S(1)}, s16[400,128]{1,0:T(8,128)(2,1)S(1)}, u32[]{:S(2)}, u32[]{:S(2)}) collective-permute-start(s16[400,128]{1,0:T(8,128)(2,1)S(1)} %get-tuple-element.31), channel_id=1, source_target_pairs={{0,10},{2,8},{4,14},{6,12},{8,2},{10,0},{12,6},{14,4},{1,11},{3,9}... | collective-permute-start | bytes 307208 | tf_op jit(solution)/shard_map/ppermute | solution.py:339
  9.4 11.8 %collective-permute-start.3 = (s16[400,128]{1,0:T(8,128)(2,1)S(1)}, s16[400,128]{1,0:T(8,128)(2,1)S(1)}, u32[]{:S(2)}, u32[]{:S(2)}) collective-permute-start(s16[400,128]{1,0:T(8,128)(2,1)S(1)} %get-tuple-element.32), channel_id=1, source_target_pairs={{0,4},{2,6},{4,0},{6,2},{8,12},{10,14},{12,8},{14,10},{1,5},{3,7},... | collective-permute-start | bytes 307208 | tf_op jit(solution)/shard_map/ppermute | solution.py:339
  10.0 14.1 %collective-permute-start.12 = (s16[400,128]{1,0:T(8,128)(2,1)S(1)}, s16[400,128]{1,0:T(8,128)(2,1)S(1)}, u32[]{:S(2)}, u32[]{:S(2)}) collective-permute-start(s16[400,128]{1,0:T(8,128)(2,1)S(1)} %get-tuple-element.36), channel_id=1, source_target_pairs={{0,8},{2,10},{4,12},{6,14},{8,0},{10,2},{12,4},{14,6},{1,9},{3,11}... | collective-permute-start | bytes 307208 | tf_op jit(solution)/shard_map/ppermute | solution.py:339
  12.3 11.8 %collective-permute-start.10 = (s16[400,128]{1,0:T(8,128)(2,1)S(1)}, s16[400,128]{1,0:T(8,128)(2,1)S(1)}, u32[]{:S(2)}, u32[]{:S(2)}) collective-permute-start(s16[400,128]{1,0:T(8,128)(2,1)S(1)} %get-tuple-element.35), channel_id=1, source_target_pairs={{0,6},{2,4},{4,2},{6,0},{8,14},{10,12},{12,10},{14,8},{1,7},{3,5},... | collective-permute-start | bytes 307208 | tf_op jit(solution)/shard_map/ppermute | solution.py:339
  17.4 7.5 %collective-permute-start.8 = (s16[400,128]{1,0:T(8,128)(2,1)S(1)}, s16[400,128]{1,0:T(8,128)(2,1)S(1)}, u32[]{:S(2)}, u32[]{:S(2)}) collective-permute-start(s16[400,128]{1,0:T(8,128)(2,1)S(1)} %get-tuple-element.34), channel_id=1, source_target_pairs={{0,14},{2,12},{4,10},{6,8},{8,6},{10,4},{12,2},{14,0},{1,15},{3,13... | collective-permute-start | bytes 307208 | tf_op jit(solution)/shard_map/ppermute | solution.py:339
  21.2 3.9 %collective-permute-start.14 = (s16[400,128]{1,0:T(8,128)(2,1)S(1)}, s16[400,128]{1,0:T(8,128)(2,1)S(1)}, u32[]{:S(2)}, u32[]{:S(2)}) collective-permute-start(s16[400,128]{1,0:T(8,128)(2,1)S(1)} %get-tuple-element.43.refs_3_), channel_id=1, source_target_pairs={{0,1},{1,0},{2,3},{3,2},{4,5},{5,4},{6,7},{7,6},{8,9},{9,8},{10,11... | collective-permute-start | bytes 307208 | tf_op jit(solution)/shard_map/ppermute | solution.py:27
  24.1 1.4 %collective-permute-start.13 = (s16[400,128]{1,0:T(8,128)(2,1)S(1)}, s16[400,128]{1,0:T(8,128)(2,1)S(1)}, u32[]{:S(2)}, u32[]{:S(2)}) collective-permute-start(s16[400,128]{1,0:T(8,128)(2,1)S(1)} %collective-permute-done.12.refs_2_), channel_id=1, source_target_pairs={{0,1},{1,0},{2,3},{3,2},{4,5},{5,4},{6,7},{7,6},{8,9},{9,8},{10,11... | collective-permute-start | bytes 307208 | tf_op jit(solution)/shard_map/ppermute | solution.py:27
  24.1 1.6 %collective-permute-start.11 = (s16[400,128]{1,0:T(8,128)(2,1)S(1)}, s16[400,128]{1,0:T(8,128)(2,1)S(1)}, u32[]{:S(2)}, u32[]{:S(2)}) collective-permute-start(s16[400,128]{1,0:T(8,128)(2,1)S(1)} %collective-permute-done.10.refs_1_), channel_id=1, source_target_pairs={{0,1},{1,0},{2,3},{3,2},{4,5},{5,4},{6,7},{7,6},{8,9},{9,8},{10,11... | collective-permute-start | bytes 307208 | tf_op jit(solution)/shard_map/ppermute | solution.py:27
  24.6 2.2 %collective-permute-start.4 = (s16[400,128]{1,0:T(8,128)(2,1)S(1)}, s16[400,128]{1,0:T(8,128)(2,1)S(1)}, u32[]{:S(2)}, u32[]{:S(2)}) collective-permute-start(s16[400,128]{1,0:T(8,128)(2,1)S(1)} %collective-permute-done.refs_2_), channel_id=1, source_target_pairs={{0,1},{1,0},{2,3},{3,2},{4,5},{5,4},{6,7},{7,6},{8,9},{9,8},{10,11... | collective-permute-start | bytes 307208 | tf_op jit(solution)/shard_map/ppermute | solution.py:27
  24.9 1.9 %collective-permute-start.5 = (s16[400,128]{1,0:T(8,128)(2,1)S(1)}, s16[400,128]{1,0:T(8,128)(2,1)S(1)}, u32[]{:S(2)}, u32[]{:S(2)}) collective-permute-start(s16[400,128]{1,0:T(8,128)(2,1)S(1)} %collective-permute-done.1.refs_3_), channel_id=1, source_target_pairs={{0,1},{1,0},{2,3},{3,2},{4,5},{5,4},{6,7},{7,6},{8,9},{9,8},{10,11... | collective-permute-start | bytes 307208 | tf_op jit(solution)/shard_map/ppermute | solution.py:27
  25.1 1.8 %collective-permute-start.6 = (s16[400,128]{1,0:T(8,128)(2,1)S(1)}, s16[400,128]{1,0:T(8,128)(2,1)S(1)}, u32[]{:S(2)}, u32[]{:S(2)}) collective-permute-start(s16[400,128]{1,0:T(8,128)(2,1)S(1)} %collective-permute-done.2.refs_4_), channel_id=1, source_target_pairs={{0,1},{1,0},{2,3},{3,2},{4,5},{5,4},{6,7},{7,6},{8,9},{9,8},{10,11... | collective-permute-start | bytes 307208 | tf_op jit(solution)/shard_map/ppermute | solution.py:27
  25.4 1.4 %collective-permute-start.7 = (s16[400,128]{1,0:T(8,128)(2,1)S(1)}, s16[400,128]{1,0:T(8,128)(2,1)S(1)}, u32[]{:S(2)}, u32[]{:S(2)}) collective-permute-start(s16[400,128]{1,0:T(8,128)(2,1)S(1)} %collective-permute-done.3.refs_5_), channel_id=1, source_target_pairs={{0,1},{1,0},{2,3},{3,2},{4,5},{5,4},{6,7},{7,6},{8,9},{9,8},{10,11... | collective-permute-start | bytes 307208 | tf_op jit(solution)/shard_map/ppermute | solution.py:27
  25.6 1.3 %collective-permute-start.9 = (s16[400,128]{1,0:T(8,128)(2,1)S(1)}, s16[400,128]{1,0:T(8,128)(2,1)S(1)}, u32[]{:S(2)}, u32[]{:S(2)}) collective-permute-start(s16[400,128]{1,0:T(8,128)(2,1)S(1)} %collective-permute-done.8.refs_0_), channel_id=1, source_target_pairs={{0,1},{1,0},{2,3},{3,2},{4,5},{5,4},{6,7},{7,6},{8,9},{9,8},{10,11... | collective-permute-start | bytes 307208 | tf_op jit(solution)/shard_map/ppermute | solution.py:27
  29.1 10.6 %all-to-all-start = ((f32[8,1,128]{2,1,0:T(1,128)}), f32[8,1,128]{2,1,0:T(1,128)S(1)}, u32[]{:S(2)}, u32[]{:S(2)}) async-start(f32[8,1,128]{2,1,0:T(1,128)} %bitcast.4), calls=%async_computation | async-start | bytes 8192 | tf_op jit(solution)/shard_map/all_to_all | solution.py:383

commit v5 on v4

--- a/solution.py
+++ b/solution.py
@@ -14,12 +14,11 @@
 LANES = 128
 META = 16
 FULL = 32768.0
-GROUP = 128
 STEPS = (32, 16, 8, 4, 2, 1)
 CODE = 65536.0
 NONE = -1e30
-FIRST = (6, 1, 5, 2, 7, 3, 4, 0)
-HELD = 6
+FIRST = (6, 1, 5, 2, 7, 3, 0, 4)
+HELD = 7
 EARLY = 4
 
 
@@ -183,9 +182,10 @@
         packs[v][tiles * capacity :, :] = notes.astype(jnp.int32).astype(jnp.int16)
 
 
-def digest(chunks, capacity, width, high_ref, low_ref):
+def digest(chunks, capacity, width, per_owner, high_ref):
     tiles = width // LANES
     clus, codes, scales = [], [], []
+    sums = None
     for pair in range(len(chunks) // 2):
         notes = [
             ref[tiles * capacity :, :].astype(jnp.int32).astype(jnp.float32)[:8, :capacity]
@@ -203,34 +203,33 @@
         clus.append(clu)
         codes.append(jnp.where(clu >= 0.0, clu * CODE + rank, -1.0))
         scales.append(scale)
+        own = iota((per_owner, LANES), 0).astype(jnp.float32) == clu
+        member = jnp.where(own, scale, 0.0).astype(jnp.bfloat16)
+        highs, lows = [], []
+        for i in (2 * pair, 2 * pair + 1):
+            ref = chunks[i]
+            here = slice(i * capacity, (i + 1) * capacity)
+            pieces = [
+                halves(ref[c * capacity : (c + 1) * capacity, :].astype(jnp.int32).astype(jnp.float32))
+                for c in range(tiles)
+            ]
+            high = jnp.concatenate([piece[0] for piece in pieces], axis=1)
+            high_ref[here, :] = high
+            highs.append(high)
+            lows.append(jnp.concatenate([piece[1] for piece in pieces], axis=1))
+        part = dot(member, jnp.concatenate(highs, axis=0)) + dot(
+            member, jnp.concatenate(lows, axis=0)
+        )
+        sums = part if sums is None else sums + part
     blocks = len(clus)
     cols = jnp.transpose(
         jnp.concatenate(
             codes + scales + [jnp.zeros((LANES - 2 * blocks, LANES), jnp.float32)], axis=0
         )
     )[:, : 2 * blocks]
-    for i, ref in enumerate(chunks):
-        here = slice(i * capacity, (i + 1) * capacity)
-        for c in range(tiles):
-            tile = ref[c * capacity : (c + 1) * capacity, :]
-            high, low = halves(tile.astype(jnp.int32).astype(jnp.float32))
-            high_ref[here, c * LANES : (c + 1) * LANES] = high
-            low_ref[here, c * LANES : (c + 1) * LANES] = low
     rows = [jnp.concatenate(x, axis=1) for x in (clus, codes, scales)]
-    return jnp.concatenate(rows + [jnp.zeros((5, rows[0].shape[1]), jnp.float32)], axis=0), cols
-
-
-def part_sums(facts, per_owner, high_ref, low_ref):
-    count = facts.shape[1]
-    step = min(count, GROUP)
-    total = None
-    for first in range(0, count, step):
-        here = slice(first, first + step)
-        own = iota((per_owner, step), 0).astype(jnp.float32) == facts[0:1, here]
-        member = jnp.where(own, facts[2:3, here], 0.0).astype(jnp.bfloat16)
-        part = dot(member, high_ref[here, :]) + dot(member, low_ref[here, :])
-        total = part if total is None else total + part
-    return total
+    rows = jnp.concatenate(rows + [jnp.zeros((5, rows[0].shape[1]), jnp.float32)], axis=0)
+    return rows, cols, sums
 
 
 def best_of(scores, cols, facts):
@@ -248,54 +247,75 @@
 
 def early_kernel(owners, capacity, per_owner, width, *refs):
     asg_ref, earlier_ref, *chunks = refs[: EARLY + 2]
-    slot_ref, high_ref, facts_ref, cols_ref, sums_ref, best_ref, low_ref = refs[EARLY + 2 :]
+    slot_ref, high_ref, facts_ref, cols_ref, sums_ref, best_ref = refs[EARLY + 2 :]
     slot_ref[...] = slots_of(owners, capacity, per_owner, asg_ref[...], earlier_ref[...])
-    facts, cols = digest(chunks, capacity, width, high_ref, low_ref)
+    facts, cols, sums = digest(chunks, capacity, width, per_owner, high_ref)
     facts_ref[...] = facts
     cols_ref[...] = cols
-    sums_ref[...] = part_sums(facts, per_owner, high_ref, low_ref)
+    sums_ref[...] = sums
     best_ref[...] = best_of(dot_t(high_ref[...], high_ref[...]), cols, facts)
 
 
+def cross_kernel(owners, capacity, per_owner, width, *refs):
+    chunks = refs[:EARLY]
+    old_ref, old_facts_ref, old_cols_ref, old_sums_ref, old_best_ref = refs[EARLY : EARLY + 5]
+    high_ref, facts_ref, cols_ref, sums_ref, best_ref = refs[EARLY + 5 :]
+    count = EARLY * capacity
+    new_ref = high_ref.at[count:, :]
+    facts, cols, sums = digest(chunks, capacity, width, per_owner, new_ref)
+    high_ref[:count, :] = old_ref[...]
+    old_facts = old_facts_ref[...]
+    facts_ref[:, :count] = old_facts
+    facts_ref[:, count:] = facts
+    old_cols = old_cols_ref[...]
+    blocks = EARLY // 2
+    cols_ref[...] = jnp.concatenate(
+        [old_cols[:, :blocks], cols[:, :blocks], old_cols[:, blocks:], cols[:, blocks:]], axis=1
+    )
+    sums_ref[...] = old_sums_ref[...] + sums
+    best = best_of(dot_t(new_ref[...], old_ref[...]), cols, old_facts)
+    best_ref[...] = jnp.maximum(old_best_ref[...], best)
+
+
 def late_kernel(owners, capacity, per_owner, width, *refs):
+    chunks = refs[: owners - EARLY]
+    old_ref, old_facts_ref, old_cols_ref, old_sums_ref, old_best_ref = refs[len(chunks) : len(chunks) + 5]
+    high_ref, facts_ref, sums_ref, best_ref = refs[len(chunks) + 5 :]
+    asked = EARLY * capacity
+    new_ref = high_ref.at[asked:, :]
+    facts, cols, sums = digest(chunks, capacity, width, per_owner, new_ref)
+    high_ref[:asked, :] = old_ref[:asked, :]
+    old_facts = old_facts_ref[:, :asked]
+    facts_ref[:, :asked] = old_facts
+    facts_ref[:, asked:] = facts
+    sums_ref[...] = old_sums_ref[...] + sums
+    new = new_ref[...]
+    best_ref[:, asked:] = jnp.maximum(
+        best_of(dot_t(old_ref[...], new), old_cols_ref[...], facts),
+        best_of(dot_t(new, new), cols, facts),
+    )
+    best_ref[:, :asked] = jnp.maximum(
+        old_best_ref[...], best_of(dot_t(new, old_ref[:asked, :]), cols, old_facts)
+    )
+
+
+def last_kernel(owners, capacity, per_owner, width, *refs):
     count = owners - EARLY
     chunks = refs[:count]
-    old_ref, old_facts_ref, old_cols_ref, old_sums_ref, old_best_ref = refs[count : count + 5]
-    high_ref, facts_ref, sums_ref, best_ref, low_ref = refs[count + 5 :]
-    old_rows = EARLY * capacity
-    new_ref = high_ref.at[old_rows:, :]
-    facts, cols = digest(chunks, capacity, width, new_ref, low_ref)
-    high_ref[:old_rows, :] = old_ref[...]
-    old_facts = old_facts_ref[...]
-    facts_ref[:, :old_rows] = old_facts
-    facts_ref[:, old_rows:] = facts
-    sums_ref[...] = old_sums_ref[...] + part_sums(facts, per_owner, new_ref, low_ref)
-    new = new_ref[...]
-    best_ref[:, old_rows:] = jnp.maximum(
-        best_of(dot_t(old_ref[...], new), old_cols_ref[...], facts),
-        best_of(dot_t(new, new), cols, facts),
-    )
-    best_ref[:, :old_rows] = jnp.maximum(
-        old_best_ref[...], best_of(dot_t(new, old_ref[...]), cols, old_facts)
-    )
-
-
-def last_kernel(owners, capacity, per_owner, width, *refs):
-    chunks = refs[:owners]
-    asked_ref, asked_facts_ref, old_sums_ref, old_best_ref = refs[owners : owners + 4]
-    cent_ref, back_ref, high_ref, low_ref = refs[owners + 4 :]
+    asked_ref, asked_facts_ref, old_sums_ref, old_best_ref = refs[count : count + 4]
+    cent_ref, back_ref, high_ref = refs[count + 4 :]
     me = lax.axis_index(("rows", "feat"))
-    facts, cols = digest(chunks, capacity, width, high_ref, low_ref)
-    sums = old_sums_ref[...] + part_sums(facts, per_owner, high_ref, low_ref)
-    cent = sums * lax.rsqrt(jnp.sum(sums * sums, axis=1, keepdims=True) + EPSILON)
-    cent_ref[...] = cent
+    facts, cols, sums = digest(chunks, capacity, width, per_owner, high_ref)
+    sums = old_sums_ref[...] + sums
+    norm = lax.rsqrt(jnp.sum(sums * sums, axis=1, keepdims=True) + EPSILON)
+    cent_ref[...] = sums * norm
     asked = asked_ref[...]
     asked_facts = asked_facts_ref[...]
     scale = asked_facts[2:3, :]
     best = best_of(dot_t(high_ref[...], asked), cols, asked_facts)
     best = jnp.maximum(jnp.maximum(best, old_best_ref[...]) * scale, -1.0)
-    fits = dot_t(jnp.concatenate(halves(cent), axis=0), asked)
-    fits = fits[:per_owner, :] + fits[per_owner:, :]
+    fits = dot_t(jnp.concatenate(halves(sums), axis=0), asked)
+    fits = (fits[:per_owner, :] + fits[per_owner:, :]) * norm
     own = iota(fits.shape, 0).astype(jnp.float32) == asked_facts[0:1, :]
     near = jnp.sum(jnp.where(own, fits, 0.0), axis=0, keepdims=True) * scale
     for i, v in enumerate(FIRST):
@@ -338,7 +358,7 @@
     for v in range(1, owners):
         got[v] = lax.ppermute(packs[v], ("rows", "feat"), [(i, i ^ v) for i in range(owners)])
     begun = EARLY * capacity
-    slot, *near = pl.pallas_call(
+    slot, *old = pl.pallas_call(
         functools.partial(early_kernel, owners, capacity, per_owner, width),
         out_shape=[
             full(1, rows, dtype=jnp.int32),
@@ -350,13 +370,27 @@
         ],
         in_specs=[vmem] * (EARLY + 2),
         out_specs=[vmem] * 6,
-        scratch_shapes=[pltpu.VMEM((begun, width), jnp.bfloat16)],
         compiler_params=params,
         name="score_early",
     )(assign, earlier, *[got[v] for v in FIRST[:EARLY]])
-    last = FIRST[HELD]
-    held, near = lax.optimization_barrier((got[last], near))
-    other = [swapped(held if v == last else got[v], "sub", 0) for v in range(owners)]
+    other = {v: swapped(got[v], "sub", 0) for v in FIRST[:EARLY]}
+    old = pl.pallas_call(
+        functools.partial(cross_kernel, owners, capacity, per_owner, width),
+        out_shape=[
+            full(2 * begun, width, dtype=jnp.bfloat16),
+            full(8, 2 * begun),
+            full(LANES, 4 * begun // LANES),
+            full(per_owner, width),
+            full(1, begun),
+        ],
+        in_specs=[vmem] * (EARLY + 5),
+        out_specs=[vmem] * 5,
+        compiler_params=params,
+        name="score_cross",
+    )(*other.values(), *old)
+    held, old = lax.optimization_barrier((got[FIRST[HELD]], old))
+    rest = FIRST[EARLY:]
+    other = [swapped(held if v == FIRST[HELD] else got[v], "sub", 0) for v in rest]
     asked = pl.pallas_call(
         functools.partial(late_kernel, owners, capacity, per_owner, width),
         out_shape=[
@@ -365,21 +399,20 @@
             full(per_owner, width),
             full(1, slots),
         ],
-        in_specs=[vmem] * (owners - EARLY + 5),
+        in_specs=[vmem] * (len(rest) + 5),
         out_specs=[vmem] * 4,
-        scratch_shapes=[pltpu.VMEM((slots - begun, width), jnp.bfloat16)],
         compiler_params=params,
         name="score_late",
-    )(*[got[v] for v in FIRST[EARLY:]], *near)
+    )(*[got[v] for v in rest], *old)
     cent, back = pl.pallas_call(
         functools.partial(last_kernel, owners, capacity, per_owner, width),
         out_shape=[full(per_owner, width), full(owners, LANES)],
-        in_specs=[vmem] * (owners + 4),
+        in_specs=[vmem] * (len(rest) + 4),
         out_specs=[vmem] * 2,
-        scratch_shapes=[pltpu.VMEM((slots, width), jnp.bfloat16)] * 2,
+        scratch_shapes=[pltpu.VMEM((len(rest) * capacity, width), jnp.bfloat16)],
         compiler_params=params,
         name="score_last",
-    )(*[other[v] for v in FIRST], *asked)
+    )(*other, *asked)
     back = lax.all_to_all(back, ("rows", "feat"), split_axis=0, concat_axis=0, tiled=True)
     slot = slot.reshape(rows)
     pos = lax.rem(slot, jnp.int32(capacity))

time: 40.8 us -> 40.4 us (level)
  waiting for transfers between devices: 12.2 us -> 11.6 us
    ppermute x7, waiting for transfers between devices: 5.66 us -> 4.85 us  [exchange_pairs(): lax.ppermute(packs[v], ('rows', 'feat'), [(i, i ^ v) for i in range(owner...]
    pallas_call x0 -> x1, Pallas kernels: none -> 0.63 us  [exchange_pairs(): pl.pallas_call(functools.partial(cross_kernel, owners, capacity, per_owne...]
    ppermute x7, starting transfers between devices: 15.2 us -> 14.7 us  [exchange_pairs(): lax.ppermute(packs[v], ('rows', 'feat'), [(i, i ^ v) for i in range(owner...]
    pallas_call x1, Pallas kernels: 2.16 us -> 1.62 us  [exchange_pairs(): pl.pallas_call(functools.partial(last_kernel, owners, capacity, per_owner...]
    all_to_all x1, starting transfers between devices: 4.19 us -> 4.72 us  [exchange_pairs(): lax.all_to_all(back, ('rows', 'feat'), split_axis=0, concat_axis=0, tiled...]
  transfers between devices with their start and end apart: 16 -> 16, of which waited for: 5 -> 4; matrix products, arithmetic and copies ran while one was open for 0% -> 0% of each run, Pallas kernels for 4% -> 5%
where the time goes in v5:
time: 40.4 us; the launch traced here: 40.3 us
  starting transfers between devices  21.1 us (52%)
  waiting for transfers between devices  11.6 us (29%)
  Pallas kernels  4.86 us (12%)
  local copies, waits for them, and re-layouts  1.16 us (3%)
  other arithmetic  0.82 us (2%)
  between operations  0.74 us (2%)
    ppermute x7, starting transfers between devices, exchange_pairs(): lax.ppermute(packs[v], ('rows', 'feat'), [(i, i ^ v) for i in range(owner...  14.7 us
    all_to_all x1, waiting for transfers between devices, exchange_pairs(): lax.all_to_all(back, ('rows', 'feat'), split_axis=0, concat_axis=0, tiled...  6.44 us
    ppermute x7, waiting for transfers between devices, exchange_pairs(): lax.ppermute(packs[v], ('rows', 'feat'), [(i, i ^ v) for i in range(owner...  4.85 us
    all_to_all x1, starting transfers between devices, exchange_pairs(): lax.all_to_all(back, ('rows', 'feat'), split_axis=0, concat_axis=0, tiled...  4.72 us
    ppermute x8, starting transfers between devices, swapped(): lax.ppermute(shard, axis, [(i, i ^ 1 << distance) for i in range(lax.axis...  1.69 us
    pallas_call x1, Pallas kernels, exchange_pairs(): pl.pallas_call(functools.partial(last_kernel, owners, capacity, per_owner...  1.62 us
    unnamed x6, local copies, waits for them, and re-layouts  1.08 us
    pallas_call x1, Pallas kernels, exchange_pairs(): pl.pallas_call(functools.partial(pack_kernel, owners, capacity, per_owner...  1.01 us
  transfers between devices with their start and end apart: 16, of which 4 were waited for; matrix products, arithmetic and copies ran while one was open for 0% of the time, Pallas kernels for 5%

profile of v5, /device:TPU:0, one launch (start us, length us, event | category | flops | bytes accessed | tf_op | source)
XLA Modules:
  0.0 40.3 jit_solution(9888516201210513780)
XLA Ops:
  0.6 0.0 copy-start
  0.6 0.0 copy-start.2
  0.7 0.0 copy-start.1
  0.7 1.1 %copy-done = f32[256,768]{1,0:T(8,128)S(1)} copy-done((f32[256,768]{1,0:T(8,128)S(1)}, f32[256,768]{1,0:T(8,128)}, u32[]{:S(2)}) %copy-start) | copy-done | bytes 786456
  1.8 0.0 copy-done.2
  1.8 0.0 copy-done.1
  1.8 1.0 %pack.1 = (s16[400,128]{1,0:T(8,128)(2,1)S(1)}, s16[400,128]{1,0:T(8,128)(2,1)S(1)}, s16[400,128]{1,0:T(8,128)(2,1)S(1)}, s16[400,128]{1,0:T(8,128)(2,1)S(1)}, s...) custom-call(f32[256,768]{1,0:T(8,128)S(1)} %copy-done, ...), custom_call_target="tpu_custom_call" | custom-call | tf_op jit(solution)/shard_map/pack/pallas_call | solution.py:349
  2.8 5.1 %collective-permute-start = (s16[400,128]{1,0:T(8,128)(2,1)S(1)}, s16[400,128]{1,0:T(8,128)(2,1)S(1)}, u32[]{:S(2)}, u32[]{:S(2)}) collective-permute-start(s16[400,128]{1,0:T(8,128)(2,1)S(1)} %get-tuple-element.34), channel_id=1, source_target_pairs={{0,12},{2,14},{4,8},{6,10},{8,4},{10,6},{12,0},{14,2},{1,13},{3,15... | collective-permute-start | bytes 307208 | tf_op jit(solution)/shard_map/ppermute | solution.py:359
  7.9 1.5 %collective-permute-start.1 = (s16[400,128]{1,0:T(8,128)(2,1)S(1)}, s16[400,128]{1,0:T(8,128)(2,1)S(1)}, u32[]{:S(2)}, u32[]{:S(2)}) collective-permute-start(s16[400,128]{1,0:T(8,128)(2,1)S(1)} %get-tuple-element.35), channel_id=1, source_target_pairs={{0,2},{2,0},{4,6},{6,4},{8,10},{10,8},{12,14},{14,12},{1,3},{3,1},... | collective-permute-start | bytes 307208 | tf_op jit(solution)/shard_map/ppermute | solution.py:359
  9.4 0.0 collective-permute-start.2
  9.4 0.6 %collective-permute-start.3 = (s16[400,128]{1,0:T(8,128)(2,1)S(1)}, s16[400,128]{1,0:T(8,128)(2,1)S(1)}, u32[]{:S(2)}, u32[]{:S(2)}) collective-permute-start(s16[400,128]{1,0:T(8,128)(2,1)S(1)} %get-tuple-element.37), channel_id=1, source_target_pairs={{0,4},{2,6},{4,0},{6,2},{8,12},{10,14},{12,8},{14,10},{1,5},{3,7},... | collective-permute-start | bytes 307208 | tf_op jit(solution)/shard_map/ppermute | solution.py:359
  10.0 4.7 %collective-permute-start.4 = (s16[400,128]{1,0:T(8,128)(2,1)S(1)}, s16[400,128]{1,0:T(8,128)(2,1)S(1)}, u32[]{:S(2)}, u32[]{:S(2)}) collective-permute-start(s16[400,128]{1,0:T(8,128)(2,1)S(1)} %get-tuple-element.39), channel_id=1, source_target_pairs={{0,14},{2,12},{4,10},{6,8},{8,6},{10,4},{12,2},{14,0},{1,15},{3,13... | collective-permute-start | bytes 307208 | tf_op jit(solution)/shard_map/ppermute | solution.py:359
  14.7 0.0 collective-permute-done.refs_2_
  14.7 2.7 %collective-permute-start.6 = (s16[400,128]{1,0:T(8,128)(2,1)S(1)}, s16[400,128]{1,0:T(8,128)(2,1)S(1)}, u32[]{:S(2)}, u32[]{:S(2)}) collective-permute-start(s16[400,128]{1,0:T(8,128)(2,1)S(1)} %get-tuple-element.40), channel_id=1, source_target_pairs={{0,6},{2,4},{4,2},{6,0},{8,14},{10,12},{12,10},{14,8},{1,7},{3,5},... | collective-permute-start | bytes 307208 | tf_op jit(solution)/shard_map/ppermute | solution.py:359
  17.4 0.0 collective-permute-done.1.refs_3_
  17.4 0.1 collective-permute-start.9
  17.5 3.7 %collective-permute-done.2.refs_4_ = s16[400,128]{1,0:T(8,128)(2,1)S(1)} collective-permute-done((s16[400,128]{1,0:T(8,128)(2,1)S(1)}, s16[400,128]{1,0:T(8,128)(2,1)S(1)}, u32[]{:S(2)}, u32[]{:S(2)}) %collective-permute-start.2) | collective-permute-done | bytes 102432 | tf_op jit(solution)/shard_map/ppermute | solution.py:359
  21.2 0.0 collective-permute-start.10
  21.2 0.0 collective-permute-done.3.refs_5_
  21.2 0.5 %collective-permute-start.11 = (s16[400,128]{1,0:T(8,128)(2,1)S(1)}, s16[400,128]{1,0:T(8,128)(2,1)S(1)}, u32[]{:S(2)}, u32[]{:S(2)}) collective-permute-start(s16[400,128]{1,0:T(8,128)(2,1)S(1)} %collective-permute-done.1.refs_3_), channel_id=1, source_target_pairs={{0,1},{1,0},{2,3},{3,2},{4,5},{5,4},{6,7},{7,6},{8,9},{9,8},{10,11... | collective-permute-start | bytes 307208 | tf_op jit(solution)/shard_map/ppermute | solution.py:26
  21.7 0.0 collective-permute-done.4.refs_0_
  21.7 0.1 collective-permute-start.12
  21.8 0.0 collective-permute-done.6.refs_1_
  21.8 0.4 %collective-permute-start.13 = (s16[400,128]{1,0:T(8,128)(2,1)S(1)}, s16[400,128]{1,0:T(8,128)(2,1)S(1)}, u32[]{:S(2)}, u32[]{:S(2)}) collective-permute-start(s16[400,128]{1,0:T(8,128)(2,1)S(1)} %collective-permute-done.3.refs_5_), channel_id=1, source_target_pairs={{0,1},{1,0},{2,3},{3,2},{4,5},{5,4},{6,7},{7,6},{8,9},{9,8},{10,11... | collective-permute-start | bytes 307208 | tf_op jit(solution)/shard_map/ppermute | solution.py:26
  22.3 0.6 %score_early.1 = (s32[1,256]{1,0:T(1,128)S(1)}, bf16[256,768]{1,0:T(8,128)(2,1)S(1)}, f32[8,256]{1,0:T(8,128)S(1)}, f32[128,4]{1,0:T(8,128)S(1)}, f32[128,768]{1,0:T(8,128)S(1)}, /*index=5*/f32[1,256]{1,0:T(1,128)S(1)}) custom-call(s32[1,256]{1,0:T(1,128)S(1)} %bitcast.8, bf16[256,256]{1,0:T(8,128)(2,1)S(1)} %earlier.1.earlier_ref.refs_1_, ...), custom_call_target="tpu_custom_call" | custom-call | tf_op jit(solution)/shard_map/score_early/pallas_call | solution.py:361
  22.9 0.0 collective-permute-done.10.refs_0_
  22.9 0.1 collective-permute-start.8
  23.0 0.0 collective-permute-done.11.refs_1_
  23.0 0.4 %collective-permute-start.5 = (s16[400,128]{1,0:T(8,128)(2,1)S(1)}, s16[400,128]{1,0:T(8,128)(2,1)S(1)}, u32[]{:S(2)}, u32[]{:S(2)}) collective-permute-start(s16[400,128]{1,0:T(8,128)(2,1)S(1)} %collective-permute-done.4.refs_0_), channel_id=1, source_target_pairs={{0,1},{1,0},{2,3},{3,2},{4,5},{5,4},{6,7},{7,6},{8,9},{9,8},{10,11... | collective-permute-start | bytes 307208 | tf_op jit(solution)/shard_map/ppermute | solution.py:26
  23.5 0.0 collective-permute-done.12.refs_2_
  23.5 0.1 collective-permute-start.7
  23.6 0.0 collective-permute-done.13.refs_3_
  23.6 0.6 %score_cross.1 = (bf16[512,768]{1,0:T(8,128)(2,1)S(1)}, f32[8,512]{1,0:T(8,128)S(1)}, f32[128,8]{1,0:T(8,128)S(1)}, f32[128,768]{1,0:T(8,128)S(1)}, f32[1,256]{1,0:T(1,128)S(1)}) custom-call(s16[400,128]{1,0:T(8,128)(2,1)S(1)} %collective-permute-done.10.refs_0_, s16[400,128]{1,0:T(8,128)(2,1)S(1)} %collective-permute-done.11.refs_1_, ...), custom_call_target="tpu_custom_call" | custom-call | tf_op jit(solution)/shard_map/score_cross/pallas_call | solution.py:377
  24.2 1.1 %collective-permute-done.9.refs_3_ = s16[400,128]{1,0:T(8,128)(2,1)S(1)} collective-permute-done((s16[400,128]{1,0:T(8,128)(2,1)S(1)}, s16[400,128]{1,0:T(8,128)(2,1)S(1)}, u32[]{:S(2)}, u32[]{:S(2)}) %collective-permute-start.9) | collective-permute-done | bytes 102432 | tf_op jit(solution)/shard_map/ppermute | solution.py:359
  25.3 0.0 collective-permute-start.14
  25.3 1.0 %score_late.1 = (bf16[512,768]{1,0:T(8,128)(2,1)S(1)}, f32[8,512]{1,0:T(8,128)S(1)}, f32[128,768]{1,0:T(8,128)S(1)}, f32[1,512]{1,0:T(1,128)S(1)}) custom-call(s16[400,128]{1,0:T(8,128)(2,1)S(1)} %collective-permute-done.4.refs_0_, s16[400,128]{1,0:T(8,128)(2,1)S(1)} %collective-permute-done.6.refs_1_, s16[400,128]{1,0:T(8,128)(2,1)S(1)} %get-tuple-element.41.refs_2_, ...), custom_call_target="tpu_custom_call" | custom-call | tf_op jit(solution)/shard_map/score_late/pallas_call | solution.py:394
  26.3 0.0 collective-permute-done.8.refs_2_
  26.3 0.0 collective-permute-done.5.refs_0_
  26.3 0.0 collective-permute-done.7.refs_1_
  26.3 0.3 collective-permute-done.14.refs_3_
  26.6 1.6 %score_last.1 = (f32[128,768]{1,0:T(8,128)}, f32[8,128]{1,0:T(8,128)}) custom-call(s16[400,128]{1,0:T(8,128)(2,1)S(1)} %collective-permute-done.5.refs_0_, s16[400,128]{1,0:T(8,128)(2,1)S(1)} %collective-permute-done.7.refs_1_, s16[400,128]{1,0:T(8,128)(2,1)S(1)} %collective-permute-done.8.refs_2_, s16[400,128]{1,0:T(8,128)(2,1)S(1)} %collective-permute-done.14.refs_3_, ...), custom_call_target="tpu_custom_call" | custom-call | tf_op jit(solution)/shard_map/score_last/pallas_call | solution.py:407
  28.2 4.7 %all-to-all-start = ((f32[8,1,128]{2,1,0:T(1,128)}), f32[8,1,128]{2,1,0:T(1,128)S(1)}, u32[]{:S(2)}, u32[]{:S(2)}) async-start(f32[8,1,128]{2,1,0:T(1,128)} %bitcast.4), calls=%async_computation | async-start | bytes 8192 | tf_op jit(solution)/shard_map/all_to_all | solution.py:416
  33.0 6.4 %all-to-all-done = f32[8,1,128]{2,1,0:T(1,128)S(1)} async-done(((f32[8,1,128]{2,1,0:T(1,128)}), f32[8,1,128]{2,1,0:T(1,128)S(1)}, u32[]{:S(2)}, u32[]{:S(2)}) %all-to-all-start) | async-done | bytes 4128 | tf_op jit(solution)/shard_map/all_to_all | solution.py:416
  39.4 0.1 fusion.4
  39.5 0.8 %fusion.1 = (f32[256]{0:T(256)}, f32[256]{0:T(256)}) fusion(f32[8,64]{1,0:T(8,128)S(1)} %get-tuple-element.68, pred[256,64]{0,1:T(8,128)(4,1)S(1)} %iota_compare_fusion, pred[8,256]{1,0:T(8,128)(4,1)S(1)} %iota_compare_fusion.1, f32[8,64]{1,0:T(8,128)S(1)} %get-tuple-element.67), kind=kLoop, calls=%fused_computation.3 | loop fusion | flops 654848 | bytes 24576 | tf_op jit(solution)/shard_map/reduce_sum | solution.py:424
  (5 shorter events, 0.1 us)
Async XLA Ops:
  0.6 1.1 %copy-start = (f32[256,768]{1,0:T(8,128)S(1)}, f32[256,768]{1,0:T(8,128)}, u32[]{:S(2)}) copy-start(f32[256,768]{1,0:T(8,128)} %emb_ref.1) | copy-start | bytes 2359300
  0.6 1.1 %copy-start.2 = (s32[256]{0:T(256)S(1)}, s32[256]{0:T(256)}, u32[]{:S(2)}) copy-start(s32[256]{0:T(256)} %param.5) | copy-start | bytes 3076
  0.7 1.1 %copy-start.1 = (s32[256]{0:T(256)S(1)}, s32[256]{0:T(256)}, u32[]{:S(2)}) copy-start(s32[256]{0:T(256)} %param.4) | copy-start | bytes 3076
  2.8 11.9 %collective-permute-start = (s16[400,128]{1,0:T(8,128)(2,1)S(1)}, s16[400,128]{1,0:T(8,128)(2,1)S(1)}, u32[]{:S(2)}, u32[]{:S(2)}) collective-permute-start(s16[400,128]{1,0:T(8,128)(2,1)S(1)} %get-tuple-element.34), channel_id=1, source_target_pairs={{0,12},{2,14},{4,8},{6,10},{8,4},{10,6},{12,0},{14,2},{1,13},{3,15... | collective-permute-start | bytes 307208 | tf_op jit(solution)/shard_map/ppermute | solution.py:359
  7.9 9.5 %collective-permute-start.1 = (s16[400,128]{1,0:T(8,128)(2,1)S(1)}, s16[400,128]{1,0:T(8,128)(2,1)S(1)}, u32[]{:S(2)}, u32[]{:S(2)}) collective-permute-start(s16[400,128]{1,0:T(8,128)(2,1)S(1)} %get-tuple-element.35), channel_id=1, source_target_pairs={{0,2},{2,0},{4,6},{6,4},{8,10},{10,8},{12,14},{14,12},{1,3},{3,1},... | collective-permute-start | bytes 307208 | tf_op jit(solution)/shard_map/ppermute | solution.py:359
  9.4 11.8 %collective-permute-start.2 = (s16[400,128]{1,0:T(8,128)(2,1)S(1)}, s16[400,128]{1,0:T(8,128)(2,1)S(1)}, u32[]{:S(2)}, u32[]{:S(2)}) collective-permute-start(s16[400,128]{1,0:T(8,128)(2,1)S(1)} %get-tuple-element.36), channel_id=1, source_target_pairs={{0,10},{2,8},{4,14},{6,12},{8,2},{10,0},{12,6},{14,4},{1,11},{3,9}... | collective-permute-start | bytes 307208 | tf_op jit(solution)/shard_map/ppermute | solution.py:359
  9.4 11.8 %collective-permute-start.3 = (s16[400,128]{1,0:T(8,128)(2,1)S(1)}, s16[400,128]{1,0:T(8,128)(2,1)S(1)}, u32[]{:S(2)}, u32[]{:S(2)}) collective-permute-start(s16[400,128]{1,0:T(8,128)(2,1)S(1)} %get-tuple-element.37), channel_id=1, source_target_pairs={{0,4},{2,6},{4,0},{6,2},{8,12},{10,14},{12,8},{14,10},{1,5},{3,7},... | collective-permute-start | bytes 307208 | tf_op jit(solution)/shard_map/ppermute | solution.py:359
  10.0 11.7 %collective-permute-start.4 = (s16[400,128]{1,0:T(8,128)(2,1)S(1)}, s16[400,128]{1,0:T(8,128)(2,1)S(1)}, u32[]{:S(2)}, u32[]{:S(2)}) collective-permute-start(s16[400,128]{1,0:T(8,128)(2,1)S(1)} %get-tuple-element.39), channel_id=1, source_target_pairs={{0,14},{2,12},{4,10},{6,8},{8,6},{10,4},{12,2},{14,0},{1,15},{3,13... | collective-permute-start | bytes 307208 | tf_op jit(solution)/shard_map/ppermute | solution.py:359
  14.7 7.1 %collective-permute-start.6 = (s16[400,128]{1,0:T(8,128)(2,1)S(1)}, s16[400,128]{1,0:T(8,128)(2,1)S(1)}, u32[]{:S(2)}, u32[]{:S(2)}) collective-permute-start(s16[400,128]{1,0:T(8,128)(2,1)S(1)} %get-tuple-element.40), channel_id=1, source_target_pairs={{0,6},{2,4},{4,2},{6,0},{8,14},{10,12},{12,10},{14,8},{1,7},{3,5},... | collective-permute-start | bytes 307208 | tf_op jit(solution)/shard_map/ppermute | solution.py:359
  17.4 7.9 %collective-permute-start.9 = (s16[400,128]{1,0:T(8,128)(2,1)S(1)}, s16[400,128]{1,0:T(8,128)(2,1)S(1)}, u32[]{:S(2)}, u32[]{:S(2)}) collective-permute-start(s16[400,128]{1,0:T(8,128)(2,1)S(1)} %get-tuple-element.42), channel_id=1, source_target_pairs={{0,8},{2,10},{4,12},{6,14},{8,0},{10,2},{12,4},{14,6},{1,9},{3,11}... | collective-permute-start | bytes 307208 | tf_op jit(solution)/shard_map/ppermute | solution.py:359
  21.2 1.7 %collective-permute-start.10 = (s16[400,128]{1,0:T(8,128)(2,1)S(1)}, s16[400,128]{1,0:T(8,128)(2,1)S(1)}, u32[]{:S(2)}, u32[]{:S(2)}) collective-permute-start(s16[400,128]{1,0:T(8,128)(2,1)S(1)} %collective-permute-done.refs_2_), channel_id=1, source_target_pairs={{0,1},{1,0},{2,3},{3,2},{4,5},{5,4},{6,7},{7,6},{8,9},{9,8},{10,11... | collective-permute-start | bytes 307208 | tf_op jit(solution)/shard_map/ppermute | solution.py:26
  21.2 1.8 %collective-permute-start.11 = (s16[400,128]{1,0:T(8,128)(2,1)S(1)}, s16[400,128]{1,0:T(8,128)(2,1)S(1)}, u32[]{:S(2)}, u32[]{:S(2)}) collective-permute-start(s16[400,128]{1,0:T(8,128)(2,1)S(1)} %collective-permute-done.1.refs_3_), channel_id=1, source_target_pairs={{0,1},{1,0},{2,3},{3,2},{4,5},{5,4},{6,7},{7,6},{8,9},{9,8},{10,11... | collective-permute-start | bytes 307208 | tf_op jit(solution)/shard_map/ppermute | solution.py:26
  21.7 1.7 %collective-permute-start.12 = (s16[400,128]{1,0:T(8,128)(2,1)S(1)}, s16[400,128]{1,0:T(8,128)(2,1)S(1)}, u32[]{:S(2)}, u32[]{:S(2)}) collective-permute-start(s16[400,128]{1,0:T(8,128)(2,1)S(1)} %collective-permute-done.2.refs_4_), channel_id=1, source_target_pairs={{0,1},{1,0},{2,3},{3,2},{4,5},{5,4},{6,7},{7,6},{8,9},{9,8},{10,11... | collective-permute-start | bytes 307208 | tf_op jit(solution)/shard_map/ppermute | solution.py:26
  21.8 1.7 %collective-permute-start.13 = (s16[400,128]{1,0:T(8,128)(2,1)S(1)}, s16[400,128]{1,0:T(8,128)(2,1)S(1)}, u32[]{:S(2)}, u32[]{:S(2)}) collective-permute-start(s16[400,128]{1,0:T(8,128)(2,1)S(1)} %collective-permute-done.3.refs_5_), channel_id=1, source_target_pairs={{0,1},{1,0},{2,3},{3,2},{4,5},{5,4},{6,7},{7,6},{8,9},{9,8},{10,11... | collective-permute-start | bytes 307208 | tf_op jit(solution)/shard_map/ppermute | solution.py:26
  22.9 3.4 %collective-permute-start.8 = (s16[400,128]{1,0:T(8,128)(2,1)S(1)}, s16[400,128]{1,0:T(8,128)(2,1)S(1)}, u32[]{:S(2)}, u32[]{:S(2)}) collective-permute-start(s16[400,128]{1,0:T(8,128)(2,1)S(1)} %get-tuple-element.41.refs_2_), channel_id=1, source_target_pairs={{0,1},{1,0},{2,3},{3,2},{4,5},{5,4},{6,7},{7,6},{8,9},{9,8},{10,11... | collective-permute-start | bytes 307208 | tf_op jit(solution)/shard_map/ppermute | solution.py:26
  23.0 3.3 %collective-permute-start.5 = (s16[400,128]{1,0:T(8,128)(2,1)S(1)}, s16[400,128]{1,0:T(8,128)(2,1)S(1)}, u32[]{:S(2)}, u32[]{:S(2)}) collective-permute-start(s16[400,128]{1,0:T(8,128)(2,1)S(1)} %collective-permute-done.4.refs_0_), channel_id=1, source_target_pairs={{0,1},{1,0},{2,3},{3,2},{4,5},{5,4},{6,7},{7,6},{8,9},{9,8},{10,11... | collective-permute-start | bytes 307208 | tf_op jit(solution)/shard_map/ppermute | solution.py:26
  23.5 2.8 %collective-permute-start.7 = (s16[400,128]{1,0:T(8,128)(2,1)S(1)}, s16[400,128]{1,0:T(8,128)(2,1)S(1)}, u32[]{:S(2)}, u32[]{:S(2)}) collective-permute-start(s16[400,128]{1,0:T(8,128)(2,1)S(1)} %collective-permute-done.6.refs_1_), channel_id=1, source_target_pairs={{0,1},{1,0},{2,3},{3,2},{4,5},{5,4},{6,7},{7,6},{8,9},{9,8},{10,11... | collective-permute-start | bytes 307208 | tf_op jit(solution)/shard_map/ppermute | solution.py:26
  25.3 1.3 %collective-permute-start.14 = (s16[400,128]{1,0:T(8,128)(2,1)S(1)}, s16[400,128]{1,0:T(8,128)(2,1)S(1)}, u32[]{:S(2)}, u32[]{:S(2)}) collective-permute-start(s16[400,128]{1,0:T(8,128)(2,1)S(1)} %collective-permute-done.9.refs_3_), channel_id=1, source_target_pairs={{0,1},{1,0},{2,3},{3,2},{4,5},{5,4},{6,7},{7,6},{8,9},{9,8},{10,11... | collective-permute-start | bytes 307208 | tf_op jit(solution)/shard_map/ppermute | solution.py:26
  28.2 11.2 %all-to-all-start = ((f32[8,1,128]{2,1,0:T(1,128)}), f32[8,1,128]{2,1,0:T(1,128)S(1)}, u32[]{:S(2)}, u32[]{:S(2)}) async-start(f32[8,1,128]{2,1,0:T(1,128)} %bitcast.4), calls=%async_computation | async-start | bytes 8192 | tf_op jit(solution)/shard_map/all_to_all | solution.py:416

commit v6 on v5

--- a/solution.py
+++ b/solution.py
@@ -17,9 +17,11 @@
 STEPS = (32, 16, 8, 4, 2, 1)
 CODE = 65536.0
 NONE = -1e30
-FIRST = (6, 1, 5, 2, 7, 3, 0, 4)
-HELD = 7
+FIRST = (6, 1, 5, 2, 4, 3, 0, 7)
+HELD = 4
 EARLY = 4
+TIED = (6, 1,)
+CROSSED = (6, 1,)
 
 
 def swapped(shard, axis, distance):
@@ -257,9 +259,10 @@
 
 
 def cross_kernel(owners, capacity, per_owner, width, *refs):
-    chunks = refs[:EARLY]
-    old_ref, old_facts_ref, old_cols_ref, old_sums_ref, old_best_ref = refs[EARLY : EARLY + 5]
-    high_ref, facts_ref, cols_ref, sums_ref, best_ref = refs[EARLY + 5 :]
+    cut = len(CROSSED)
+    chunks = refs[:cut]
+    old_ref, old_facts_ref, old_cols_ref, old_sums_ref, old_best_ref = refs[cut : cut + 5]
+    high_ref, facts_ref, cols_ref, sums_ref, best_ref = refs[cut + 5 :]
     count = EARLY * capacity
     new_ref = high_ref.at[count:, :]
     facts, cols, sums = digest(chunks, capacity, width, per_owner, new_ref)
@@ -270,7 +273,7 @@
     old_cols = old_cols_ref[...]
     blocks = EARLY // 2
     cols_ref[...] = jnp.concatenate(
-        [old_cols[:, :blocks], cols[:, :blocks], old_cols[:, blocks:], cols[:, blocks:]], axis=1
+        [old_cols[:, :blocks], cols[:, : cut // 2], old_cols[:, blocks:], cols[:, cut // 2 :]], axis=1
     )
     sums_ref[...] = old_sums_ref[...] + sums
     best = best_of(dot_t(new_ref[...], old_ref[...]), cols, old_facts)
@@ -300,7 +303,7 @@
 
 
 def last_kernel(owners, capacity, per_owner, width, *refs):
-    count = owners - EARLY
+    count = owners - len(CROSSED)
     chunks = refs[:count]
     asked_ref, asked_facts_ref, old_sums_ref, old_best_ref = refs[count : count + 4]
     cent_ref, back_ref, high_ref = refs[count + 4 :]
@@ -373,24 +376,28 @@
         compiler_params=params,
         name="score_early",
     )(assign, earlier, *[got[v] for v in FIRST[:EARLY]])
-    other = {v: swapped(got[v], "sub", 0) for v in FIRST[:EARLY]}
+    tied, old = lax.optimization_barrier(([got[v] for v in TIED], old))
+    tied = dict(zip(TIED, tied))
+    other = [swapped(tied.get(v, got[v]), "sub", 0) for v in CROSSED]
+    met = begun + len(CROSSED) * capacity
     old = pl.pallas_call(
         functools.partial(cross_kernel, owners, capacity, per_owner, width),
         out_shape=[
-            full(2 * begun, width, dtype=jnp.bfloat16),
-            full(8, 2 * begun),
-            full(LANES, 4 * begun // LANES),
+            full(met, width, dtype=jnp.bfloat16),
+            full(8, met),
+            full(LANES, 2 * met // LANES),
             full(per_owner, width),
             full(1, begun),
         ],
-        in_specs=[vmem] * (EARLY + 5),
+        in_specs=[vmem] * (len(CROSSED) + 5),
         out_specs=[vmem] * 5,
         compiler_params=params,
         name="score_cross",
-    )(*other.values(), *old)
+    )(*other, *old)
     held, old = lax.optimization_barrier((got[FIRST[HELD]], old))
+    tied[FIRST[HELD]] = held
+    other = [swapped(tied.get(v, got[v]), "sub", 0) for v in FIRST if v not in CROSSED]
     rest = FIRST[EARLY:]
-    other = [swapped(held if v == FIRST[HELD] else got[v], "sub", 0) for v in rest]
     asked = pl.pallas_call(
         functools.partial(late_kernel, owners, capacity, per_owner, width),
         out_shape=[
@@ -407,9 +414,9 @@
     cent, back = pl.pallas_call(
         functools.partial(last_kernel, owners, capacity, per_owner, width),
         out_shape=[full(per_owner, width), full(owners, LANES)],
-        in_specs=[vmem] * (len(rest) + 4),
+        in_specs=[vmem] * (len(other) + 4),
         out_specs=[vmem] * 2,
-        scratch_shapes=[pltpu.VMEM((len(rest) * capacity, width), jnp.bfloat16)],
+        scratch_shapes=[pltpu.VMEM((len(other) * capacity, width), jnp.bfloat16)],
         compiler_params=params,
         name="score_last",
     )(*other, *asked)

time: 40.4 us -> 40.2 us (level)
    ppermute x8, waiting for transfers between devices: 0.31 us -> 1.9 us  [swapped(): lax.ppermute(shard, axis, [(i, i ^ 1 << distance) for i in range(lax.axis...]
    ppermute x7, waiting for transfers between devices: 4.85 us -> 3.29 us  [exchange_pairs(): lax.ppermute(packs[v], ('rows', 'feat'), [(i, i ^ v) for i in range(owner...]
    all_to_all x1, starting transfers between devices: 4.72 us -> 3.26 us  [exchange_pairs(): lax.all_to_all(back, ('rows', 'feat'), split_axis=0, concat_axis=0, tiled...]
    ppermute x8, starting transfers between devices: 1.69 us -> 2.38 us  [swapped(): lax.ppermute(shard, axis, [(i, i ^ 1 << distance) for i in range(lax.axis...]
    ppermute x7, starting transfers between devices: 14.7 us -> 15.2 us  [exchange_pairs(): lax.ppermute(packs[v], ('rows', 'feat'), [(i, i ^ v) for i in range(owner...]
where the time goes in v6:
time: 40.2 us; the launch traced here: 40 us
  starting transfers between devices  20.8 us (52%)
  waiting for transfers between devices  11.6 us (29%)
  Pallas kernels  4.88 us (12%)
  local copies, waits for them, and re-layouts  1.16 us (3%)
  other arithmetic  0.82 us (2%)
  between operations  0.76 us (2%)
    ppermute x7, starting transfers between devices, exchange_pairs(): lax.ppermute(packs[v], ('rows', 'feat'), [(i, i ^ v) for i in range(owner...  15.2 us
    all_to_all x1, waiting for transfers between devices, exchange_pairs(): lax.all_to_all(back, ('rows', 'feat'), split_axis=0, concat_axis=0, tiled...  6.37 us
    ppermute x7, waiting for transfers between devices, exchange_pairs(): lax.ppermute(packs[v], ('rows', 'feat'), [(i, i ^ v) for i in range(owner...  3.29 us
    all_to_all x1, starting transfers between devices, exchange_pairs(): lax.all_to_all(back, ('rows', 'feat'), split_axis=0, concat_axis=0, tiled...  3.26 us
    ppermute x8, starting transfers between devices, swapped(): lax.ppermute(shard, axis, [(i, i ^ 1 << distance) for i in range(lax.axis...  2.38 us
    ppermute x8, waiting for transfers between devices, swapped(): lax.ppermute(shard, axis, [(i, i ^ 1 << distance) for i in range(lax.axis...  1.9 us
    pallas_call x1, Pallas kernels, exchange_pairs(): pl.pallas_call(functools.partial(last_kernel, owners, capacity, per_owner...  1.83 us
    unnamed x6, local copies, waits for them, and re-layouts  1.08 us
  transfers between devices with their start and end apart: 16, of which 4 were waited for; matrix products, arithmetic and copies ran while one was open for 0% of the time, Pallas kernels for 5%

profile of v6, /device:TPU:0, one launch (start us, length us, event | category | flops | bytes accessed | tf_op | source)
XLA Modules:
  0.0 40.0 jit_solution(736694103912294500)
XLA Ops:
  0.6 0.0 copy-start
  0.6 0.0 copy-start.2
  0.7 0.0 copy-start.1
  0.7 1.1 %copy-done = f32[256,768]{1,0:T(8,128)S(1)} copy-done((f32[256,768]{1,0:T(8,128)S(1)}, f32[256,768]{1,0:T(8,128)}, u32[]{:S(2)}) %copy-start) | copy-done | bytes 786456
  1.8 0.0 copy-done.2
  1.8 0.0 copy-done.1
  1.8 1.0 %pack.1 = (s16[400,128]{1,0:T(8,128)(2,1)S(1)}, s16[400,128]{1,0:T(8,128)(2,1)S(1)}, s16[400,128]{1,0:T(8,128)(2,1)S(1)}, s16[400,128]{1,0:T(8,128)(2,1)S(1)}, s...) custom-call(f32[256,768]{1,0:T(8,128)S(1)} %copy-done, ...), custom_call_target="tpu_custom_call" | custom-call | tf_op jit(solution)/shard_map/pack/pallas_call | solution.py:352
  2.8 5.1 %collective-permute-start = (s16[400,128]{1,0:T(8,128)(2,1)S(1)}, s16[400,128]{1,0:T(8,128)(2,1)S(1)}, u32[]{:S(2)}, u32[]{:S(2)}) collective-permute-start(s16[400,128]{1,0:T(8,128)(2,1)S(1)} %get-tuple-element.41), channel_id=1, source_target_pairs={{0,12},{2,14},{4,8},{6,10},{8,4},{10,6},{12,0},{14,2},{1,13},{3,15... | collective-permute-start | bytes 307208 | tf_op jit(solution)/shard_map/ppermute | solution.py:362
  7.9 1.5 %collective-permute-start.1 = (s16[400,128]{1,0:T(8,128)(2,1)S(1)}, s16[400,128]{1,0:T(8,128)(2,1)S(1)}, u32[]{:S(2)}, u32[]{:S(2)}) collective-permute-start(s16[400,128]{1,0:T(8,128)(2,1)S(1)} %get-tuple-element.42), channel_id=1, source_target_pairs={{0,2},{2,0},{4,6},{6,4},{8,10},{10,8},{12,14},{14,12},{1,3},{3,1},... | collective-permute-start | bytes 307208 | tf_op jit(solution)/shard_map/ppermute | solution.py:362
  9.4 0.0 collective-permute-start.2
  9.4 0.6 %collective-permute-start.3 = (s16[400,128]{1,0:T(8,128)(2,1)S(1)}, s16[400,128]{1,0:T(8,128)(2,1)S(1)}, u32[]{:S(2)}, u32[]{:S(2)}) collective-permute-start(s16[400,128]{1,0:T(8,128)(2,1)S(1)} %get-tuple-element.44), channel_id=1, source_target_pairs={{0,4},{2,6},{4,0},{6,2},{8,12},{10,14},{12,8},{14,10},{1,5},{3,7},... | collective-permute-start | bytes 307208 | tf_op jit(solution)/shard_map/ppermute | solution.py:362
  10.0 2.3 %collective-permute-start.6 = (s16[400,128]{1,0:T(8,128)(2,1)S(1)}, s16[400,128]{1,0:T(8,128)(2,1)S(1)}, u32[]{:S(2)}, u32[]{:S(2)}) collective-permute-start(s16[400,128]{1,0:T(8,128)(2,1)S(1)} %get-tuple-element.46), channel_id=1, source_target_pairs={{0,8},{2,10},{4,12},{6,14},{8,0},{10,2},{12,4},{14,6},{1,9},{3,11}... | collective-permute-start | bytes 307208 | tf_op jit(solution)/shard_map/ppermute | solution.py:362
  12.3 0.0 collective-permute-done.refs_2_
  12.3 5.1 %collective-permute-start.10 = (s16[400,128]{1,0:T(8,128)(2,1)S(1)}, s16[400,128]{1,0:T(8,128)(2,1)S(1)}, u32[]{:S(2)}, u32[]{:S(2)}) collective-permute-start(s16[400,128]{1,0:T(8,128)(2,1)S(1)} %get-tuple-element.65), channel_id=1, source_target_pairs={{0,6},{2,4},{4,2},{6,0},{8,14},{10,12},{12,10},{14,8},{1,7},{3,5},... | collective-permute-start | bytes 307208 | tf_op jit(solution)/shard_map/ppermute | solution.py:362
  17.4 0.0 collective-permute-done.1.refs_3_
  17.4 0.6 %collective-permute-start.13 = (s16[400,128]{1,0:T(8,128)(2,1)S(1)}, s16[400,128]{1,0:T(8,128)(2,1)S(1)}, u32[]{:S(2)}, u32[]{:S(2)}) collective-permute-start(s16[400,128]{1,0:T(8,128)(2,1)S(1)} %get-tuple-element.67), channel_id=1, source_target_pairs={{0,14},{2,12},{4,10},{6,8},{8,6},{10,4},{12,2},{14,0},{1,15},{3,13... | collective-permute-start | bytes 307208 | tf_op jit(solution)/shard_map/ppermute | solution.py:362
  18.0 3.3 %collective-permute-done.2.refs_4_ = s16[400,128]{1,0:T(8,128)(2,1)S(1)} collective-permute-done((s16[400,128]{1,0:T(8,128)(2,1)S(1)}, s16[400,128]{1,0:T(8,128)(2,1)S(1)}, u32[]{:S(2)}, u32[]{:S(2)}) %collective-permute-start.2) | collective-permute-done | bytes 102432 | tf_op jit(solution)/shard_map/ppermute | solution.py:362
  21.2 0.0 collective-permute-start.12
  21.2 0.0 collective-permute-done.3.refs_5_
  21.2 0.6 %score_early.1 = (s32[1,256]{1,0:T(1,128)S(1)}, bf16[256,768]{1,0:T(8,128)(2,1)S(1)}, f32[8,256]{1,0:T(8,128)S(1)}, f32[128,4]{1,0:T(8,128)S(1)}, f32[128,768]{1,0:T(8,128)S(1)}, /*index=5*/f32[1,256]{1,0:T(1,128)S(1)}) custom-call(s32[1,256]{1,0:T(1,128)S(1)} %bitcast.8, bf16[256,256]{1,0:T(8,128)(2,1)S(1)} %earlier.1.earlier_ref.refs_1_, ...), custom_call_target="tpu_custom_call" | custom-call | tf_op jit(solution)/shard_map/score_early/pallas_call | solution.py:364
  21.8 0.6 %collective-permute-start.7 = (s16[400,128]{1,0:T(8,128)(2,1)S(1)}, s16[400,128]{1,0:T(8,128)(2,1)S(1)}, u32[]{:S(2)}, u32[]{:S(2)}) collective-permute-start(s16[400,128]{1,0:T(8,128)(2,1)S(1)} %collective-permute-done.refs_2_), channel_id=1, source_target_pairs={{0,1},{1,0},{2,3},{3,2},{4,5},{5,4},{6,7},{7,6},{8,9},{9,8},{10,11... | collective-permute-start | bytes 307208 | tf_op jit(solution)/shard_map/ppermute | solution.py:28
  22.4 0.9 %collective-permute-done.7.refs_0_ = s16[400,128]{1,0:T(8,128)(2,1)S(1)} collective-permute-done((s16[400,128]{1,0:T(8,128)(2,1)S(1)}, s16[400,128]{1,0:T(8,128)(2,1)S(1)}, u32[]{:S(2)}, u32[]{:S(2)}) %collective-permute-start.7) | collective-permute-done | bytes 102432 | tf_op jit(solution)/shard_map/ppermute | solution.py:28
  23.4 0.4 collective-permute-start.8
  23.7 0.9 %collective-permute-done.8.refs_1_ = s16[400,128]{1,0:T(8,128)(2,1)S(1)} collective-permute-done((s16[400,128]{1,0:T(8,128)(2,1)S(1)}, s16[400,128]{1,0:T(8,128)(2,1)S(1)}, u32[]{:S(2)}, u32[]{:S(2)}) %collective-permute-start.8) | collective-permute-done | bytes 102432 | tf_op jit(solution)/shard_map/ppermute | solution.py:28
  24.7 0.4 collective-permute-start.4
  25.0 0.5 %score_cross.1 = (bf16[384,768]{1,0:T(8,128)(2,1)S(1)}, f32[8,384]{1,0:T(8,128)S(1)}, f32[128,6]{1,0:T(8,128)S(1)}, f32[128,768]{1,0:T(8,128)S(1)}, f32[1,256]{1,0:T(1,128)S(1)}) custom-call(s16[400,128]{1,0:T(8,128)(2,1)S(1)} %collective-permute-done.7.refs_0_, s16[400,128]{1,0:T(8,128)(2,1)S(1)} %collective-permute-done.8.refs_1_, ...), custom_call_target="tpu_custom_call" | custom-call | tf_op jit(solution)/shard_map/score_cross/pallas_call | solution.py:383
  25.5 0.0 collective-permute-done.6.refs_0_
  25.6 0.2 collective-permute-start.5
  25.8 0.0 collective-permute-done.10.refs_1_
  25.8 0.4 collective-permute-start.11
  26.1 0.0 collective-permute-done.13.refs_3_
  26.1 0.2 collective-permute-start.14
  26.3 0.0 collective-permute-done.12.refs_4_
  26.3 0.4 collective-permute-start.9
  26.7 0.9 %score_late.1 = (bf16[512,768]{1,0:T(8,128)(2,1)S(1)}, f32[8,512]{1,0:T(8,128)S(1)}, f32[128,768]{1,0:T(8,128)S(1)}, f32[1,512]{1,0:T(1,128)S(1)}) custom-call(s16[400,128]{1,0:T(8,128)(2,1)S(1)} %collective-permute-done.6.refs_0_, s16[400,128]{1,0:T(8,128)(2,1)S(1)} %collective-permute-done.10.refs_1_, s16[400,128]{1,0:T(8,128)(2,1)S(1)} %get-tuple-element.66.refs_2_, ...), custom_call_target="tpu_custom_call" | custom-call | tf_op jit(solution)/shard_map/score_late/pallas_call | solution.py:401
  27.6 0.0 collective-permute-done.11.refs_3_
  27.6 0.0 collective-permute-done.14.refs_5_
  27.6 0.0 collective-permute-done.4.refs_0_
  27.6 0.0 collective-permute-done.5.refs_1_
  27.6 0.0 collective-permute-done.9.refs_2_
  27.6 1.8 %score_last.1 = (f32[128,768]{1,0:T(8,128)}, f32[8,128]{1,0:T(8,128)}) custom-call(s16[400,128]{1,0:T(8,128)(2,1)S(1)} %collective-permute-done.4.refs_0_, s16[400,128]{1,0:T(8,128)(2,1)S(1)} %collective-permute-done.5.refs_1_, s16[400,128]{1,0:T(8,128)(2,1)S(1)} %collective-permute-done.9.refs_2_, s16[400,128]{1,0:T(8,128)(2,1)S(1)} %collective-permute-done.11.refs_3_, ...), custom_call_target="tpu_custom_call" | custom-call | tf_op jit(solution)/shard_map/score_last/pallas_call | solution.py:414
  29.4 3.3 %all-to-all-start = ((f32[8,1,128]{2,1,0:T(1,128)}), f32[8,1,128]{2,1,0:T(1,128)S(1)}, u32[]{:S(2)}, u32[]{:S(2)}) async-start(f32[8,1,128]{2,1,0:T(1,128)} %bitcast.4), calls=%async_computation | async-start | bytes 8192 | tf_op jit(solution)/shard_map/all_to_all | solution.py:423
  32.7 6.4 %all-to-all-done = f32[8,1,128]{2,1,0:T(1,128)S(1)} async-done(((f32[8,1,128]{2,1,0:T(1,128)}), f32[8,1,128]{2,1,0:T(1,128)S(1)}, u32[]{:S(2)}, u32[]{:S(2)}) %all-to-all-start) | async-done | bytes 4128 | tf_op jit(solution)/shard_map/all_to_all | solution.py:423
  39.1 0.1 fusion.4
  39.2 0.8 %fusion.1 = (f32[256]{0:T(256)}, f32[256]{0:T(256)}) fusion(f32[8,64]{1,0:T(8,128)S(1)} %get-tuple-element.82, pred[256,64]{0,1:T(8,128)(4,1)S(1)} %iota_compare_fusion, pred[8,256]{1,0:T(8,128)(4,1)S(1)} %iota_compare_fusion.1, f32[8,64]{1,0:T(8,128)S(1)} %get-tuple-element.81), kind=kLoop, calls=%fused_computation.3 | loop fusion | flops 654848 | bytes 24576 | tf_op jit(solution)/shard_map/reduce_sum | solution.py:431
  (5 shorter events, 0.1 us)
Async XLA Ops:
  0.6 1.1 %copy-start = (f32[256,768]{1,0:T(8,128)S(1)}, f32[256,768]{1,0:T(8,128)}, u32[]{:S(2)}) copy-start(f32[256,768]{1,0:T(8,128)} %emb_ref.1) | copy-start | bytes 2359300
  0.6 1.1 %copy-start.2 = (s32[256]{0:T(256)S(1)}, s32[256]{0:T(256)}, u32[]{:S(2)}) copy-start(s32[256]{0:T(256)} %param.5) | copy-start | bytes 3076
  0.7 1.1 %copy-start.1 = (s32[256]{0:T(256)S(1)}, s32[256]{0:T(256)}, u32[]{:S(2)}) copy-start(s32[256]{0:T(256)} %param.4) | copy-start | bytes 3076
  2.8 9.5 %collective-permute-start = (s16[400,128]{1,0:T(8,128)(2,1)S(1)}, s16[400,128]{1,0:T(8,128)(2,1)S(1)}, u32[]{:S(2)}, u32[]{:S(2)}) collective-permute-start(s16[400,128]{1,0:T(8,128)(2,1)S(1)} %get-tuple-element.41), channel_id=1, source_target_pairs={{0,12},{2,14},{4,8},{6,10},{8,4},{10,6},{12,0},{14,2},{1,13},{3,15... | collective-permute-start | bytes 307208 | tf_op jit(solution)/shard_map/ppermute | solution.py:362
  7.9 9.5 %collective-permute-start.1 = (s16[400,128]{1,0:T(8,128)(2,1)S(1)}, s16[400,128]{1,0:T(8,128)(2,1)S(1)}, u32[]{:S(2)}, u32[]{:S(2)}) collective-permute-start(s16[400,128]{1,0:T(8,128)(2,1)S(1)} %get-tuple-element.42), channel_id=1, source_target_pairs={{0,2},{2,0},{4,6},{6,4},{8,10},{10,8},{12,14},{14,12},{1,3},{3,1},... | collective-permute-start | bytes 307208 | tf_op jit(solution)/shard_map/ppermute | solution.py:362
  9.4 11.8 %collective-permute-start.2 = (s16[400,128]{1,0:T(8,128)(2,1)S(1)}, s16[400,128]{1,0:T(8,128)(2,1)S(1)}, u32[]{:S(2)}, u32[]{:S(2)}) collective-permute-start(s16[400,128]{1,0:T(8,128)(2,1)S(1)} %get-tuple-element.43), channel_id=1, source_target_pairs={{0,10},{2,8},{4,14},{6,12},{8,2},{10,0},{12,6},{14,4},{1,11},{3,9}... | collective-permute-start | bytes 307208 | tf_op jit(solution)/shard_map/ppermute | solution.py:362
  9.4 11.8 %collective-permute-start.3 = (s16[400,128]{1,0:T(8,128)(2,1)S(1)}, s16[400,128]{1,0:T(8,128)(2,1)S(1)}, u32[]{:S(2)}, u32[]{:S(2)}) collective-permute-start(s16[400,128]{1,0:T(8,128)(2,1)S(1)} %get-tuple-element.44), channel_id=1, source_target_pairs={{0,4},{2,6},{4,0},{6,2},{8,12},{10,14},{12,8},{14,10},{1,5},{3,7},... | collective-permute-start | bytes 307208 | tf_op jit(solution)/shard_map/ppermute | solution.py:362
  10.0 15.5 %collective-permute-start.6 = (s16[400,128]{1,0:T(8,128)(2,1)S(1)}, s16[400,128]{1,0:T(8,128)(2,1)S(1)}, u32[]{:S(2)}, u32[]{:S(2)}) collective-permute-start(s16[400,128]{1,0:T(8,128)(2,1)S(1)} %get-tuple-element.46), channel_id=1, source_target_pairs={{0,8},{2,10},{4,12},{6,14},{8,0},{10,2},{12,4},{14,6},{1,9},{3,11}... | collective-permute-start | bytes 307208 | tf_op jit(solution)/shard_map/ppermute | solution.py:362
  12.3 13.5 %collective-permute-start.10 = (s16[400,128]{1,0:T(8,128)(2,1)S(1)}, s16[400,128]{1,0:T(8,128)(2,1)S(1)}, u32[]{:S(2)}, u32[]{:S(2)}) collective-permute-start(s16[400,128]{1,0:T(8,128)(2,1)S(1)} %get-tuple-element.65), channel_id=1, source_target_pairs={{0,6},{2,4},{4,2},{6,0},{8,14},{10,12},{12,10},{14,8},{1,7},{3,5},... | collective-permute-start | bytes 307208 | tf_op jit(solution)/shard_map/ppermute | solution.py:362
  17.4 8.7 %collective-permute-start.13 = (s16[400,128]{1,0:T(8,128)(2,1)S(1)}, s16[400,128]{1,0:T(8,128)(2,1)S(1)}, u32[]{:S(2)}, u32[]{:S(2)}) collective-permute-start(s16[400,128]{1,0:T(8,128)(2,1)S(1)} %get-tuple-element.67), channel_id=1, source_target_pairs={{0,14},{2,12},{4,10},{6,8},{8,6},{10,4},{12,2},{14,0},{1,15},{3,13... | collective-permute-start | bytes 307208 | tf_op jit(solution)/shard_map/ppermute | solution.py:362
  21.2 5.1 %collective-permute-start.12 = (s16[400,128]{1,0:T(8,128)(2,1)S(1)}, s16[400,128]{1,0:T(8,128)(2,1)S(1)}, u32[]{:S(2)}, u32[]{:S(2)}) collective-permute-start(s16[400,128]{1,0:T(8,128)(2,1)S(1)} %get-tuple-element.66.refs_2_), channel_id=1, source_target_pairs={{0,1},{1,0},{2,3},{3,2},{4,5},{5,4},{6,7},{7,6},{8,9},{9,8},{10,11... | collective-permute-start | bytes 307208 | tf_op jit(solution)/shard_map/ppermute | solution.py:28
  21.8 1.5 %collective-permute-start.7 = (s16[400,128]{1,0:T(8,128)(2,1)S(1)}, s16[400,128]{1,0:T(8,128)(2,1)S(1)}, u32[]{:S(2)}, u32[]{:S(2)}) collective-permute-start(s16[400,128]{1,0:T(8,128)(2,1)S(1)} %collective-permute-done.refs_2_), channel_id=1, source_target_pairs={{0,1},{1,0},{2,3},{3,2},{4,5},{5,4},{6,7},{7,6},{8,9},{9,8},{10,11... | collective-permute-start | bytes 307208 | tf_op jit(solution)/shard_map/ppermute | solution.py:28
  23.4 1.3 %collective-permute-start.8 = (s16[400,128]{1,0:T(8,128)(2,1)S(1)}, s16[400,128]{1,0:T(8,128)(2,1)S(1)}, u32[]{:S(2)}, u32[]{:S(2)}) collective-permute-start(s16[400,128]{1,0:T(8,128)(2,1)S(1)} %collective-permute-done.1.refs_3_), channel_id=1, source_target_pairs={{0,1},{1,0},{2,3},{3,2},{4,5},{5,4},{6,7},{7,6},{8,9},{9,8},{10,11... | collective-permute-start | bytes 307208 | tf_op jit(solution)/shard_map/ppermute | solution.py:28
  24.7 2.9 %collective-permute-start.4 = (s16[400,128]{1,0:T(8,128)(2,1)S(1)}, s16[400,128]{1,0:T(8,128)(2,1)S(1)}, u32[]{:S(2)}, u32[]{:S(2)}) collective-permute-start(s16[400,128]{1,0:T(8,128)(2,1)S(1)} %collective-permute-done.2.refs_4_), channel_id=1, source_target_pairs={{0,1},{1,0},{2,3},{3,2},{4,5},{5,4},{6,7},{7,6},{8,9},{9,8},{10,11... | collective-permute-start | bytes 307208 | tf_op jit(solution)/shard_map/ppermute | solution.py:28
  25.6 2.0 %collective-permute-start.5 = (s16[400,128]{1,0:T(8,128)(2,1)S(1)}, s16[400,128]{1,0:T(8,128)(2,1)S(1)}, u32[]{:S(2)}, u32[]{:S(2)}) collective-permute-start(s16[400,128]{1,0:T(8,128)(2,1)S(1)} %collective-permute-done.3.refs_5_), channel_id=1, source_target_pairs={{0,1},{1,0},{2,3},{3,2},{4,5},{5,4},{6,7},{7,6},{8,9},{9,8},{10,11... | collective-permute-start | bytes 307208 | tf_op jit(solution)/shard_map/ppermute | solution.py:28
  25.8 1.8 %collective-permute-start.11 = (s16[400,128]{1,0:T(8,128)(2,1)S(1)}, s16[400,128]{1,0:T(8,128)(2,1)S(1)}, u32[]{:S(2)}, u32[]{:S(2)}) collective-permute-start(s16[400,128]{1,0:T(8,128)(2,1)S(1)} %collective-permute-done.10.refs_1_), channel_id=1, source_target_pairs={{0,1},{1,0},{2,3},{3,2},{4,5},{5,4},{6,7},{7,6},{8,9},{9,8},{10,11... | collective-permute-start | bytes 307208 | tf_op jit(solution)/shard_map/ppermute | solution.py:28
  26.1 1.4 %collective-permute-start.14 = (s16[400,128]{1,0:T(8,128)(2,1)S(1)}, s16[400,128]{1,0:T(8,128)(2,1)S(1)}, u32[]{:S(2)}, u32[]{:S(2)}) collective-permute-start(s16[400,128]{1,0:T(8,128)(2,1)S(1)} %collective-permute-done.13.refs_3_), channel_id=1, source_target_pairs={{0,1},{1,0},{2,3},{3,2},{4,5},{5,4},{6,7},{7,6},{8,9},{9,8},{10,11... | collective-permute-start | bytes 307208 | tf_op jit(solution)/shard_map/ppermute | solution.py:28
  26.3 1.3 %collective-permute-start.9 = (s16[400,128]{1,0:T(8,128)(2,1)S(1)}, s16[400,128]{1,0:T(8,128)(2,1)S(1)}, u32[]{:S(2)}, u32[]{:S(2)}) collective-permute-start(s16[400,128]{1,0:T(8,128)(2,1)S(1)} %collective-permute-done.6.refs_0_), channel_id=1, source_target_pairs={{0,1},{1,0},{2,3},{3,2},{4,5},{5,4},{6,7},{7,6},{8,9},{9,8},{10,11... | collective-permute-start | bytes 307208 | tf_op jit(solution)/shard_map/ppermute | solution.py:28
  29.4 9.7 %all-to-all-start = ((f32[8,1,128]{2,1,0:T(1,128)}), f32[8,1,128]{2,1,0:T(1,128)S(1)}, u32[]{:S(2)}, u32[]{:S(2)}) async-start(f32[8,1,128]{2,1,0:T(1,128)} %bitcast.4), calls=%async_computation | async-start | bytes 8192 | tf_op jit(solution)/shard_map/all_to_all | solution.py:423
